TPU v7x, 256 devices: a whole 4x4x8 slice. The times are simulated.
256 devices in a mesh: aux: 4 (over y), mu: 4 (over z_lo, core), nu: 16 (over x, z_hi).
Axes of the slice: x: 4, y: 4, z: 8 (z_hi: 4, z_lo: 2; z = z_hi * 2 + z_lo), core: 2. Of those that a mesh axis runs over, the one named last changes fastest.
Arguments:
- integrals: bfloat16 [256, 1024, 1024], P('aux', 'nu', 'mu'), may hold values from -0.625 to 0.625
- integral_mask: int32 [4, 16, 16], P('aux', 'nu', 'mu'), may hold values 0 or 1
- density: bfloat16 [1024, 1024], P('mu', 'nu'), as said below
- density_mask: int32 [16, 16], P('mu', 'nu'), may hold values from 0 to 1, as said below
Outputs:
- exchange_matrix: float32 [1024, 1024], P(('aux', 'mu', 'nu'))
Inputs may be any that keep to these rules, and one draw needn't show every extreme that they name: `density`: symmetric. `density_mask`: symmetric, with every diagonal block present and some off-diagonal block absent.
All inputs are finite; a program needn't handle non-finite values. No bound on the sum of `integral_mask` on one device may be relied on, other than what follows from the above.
Results may differ from a plain program's by a relative error of at most 0.0029.
Values may be sent and summed in bfloat16 or wider, within the bound.
No kernel may reach another device: no remote copies, remote signals or barrier semaphores. Data moves between devices by JAX's collectives and lax.ppermute only.
A program may use at most 64 MiB of HBM per device.

v0:
```python
import jax
import jax.numpy as jnp
from jax import lax
from jax.sharding import PartitionSpec as P

BW = 64


def widen_blocks(blocks, width):
    first, second, third = blocks.shape
    tiled = jnp.broadcast_to(
        blocks[:, None, :, None, :, None], (first, width, second, width, third, width)
    )
    return tiled.reshape(first * width, second * width, third * width).astype(jnp.bfloat16)


def widen_pairs(blocks, width):
    first, second = blocks.shape
    tiled = jnp.broadcast_to(blocks[:, None, :, None], (first, width, second, width))
    return tiled.reshape(first * width, second * width).astype(jnp.bfloat16)


def body(integrals, integral_mask, density, density_mask):
    screened = integrals * widen_blocks(integral_mask, BW)
    masked_density = density * widen_pairs(density_mask, BW)
    row_density = lax.all_gather(masked_density, "nu", axis=1, tiled=True)
    summed = jnp.einsum(
        "pml,sl->spm",
        lax.all_gather(screened, "mu", axis=2, tiled=True),
        row_density,
        preferred_element_type=jnp.float32,
    )
    contracted = summed.astype(jnp.bfloat16)
    swapped, partners = (
        lax.all_to_all(contracted, "nu", split_axis=1, concat_axis=2, tiled=True),
        lax.all_to_all(screened[None], "nu", split_axis=1, concat_axis=2, tiled=True),
    )
    exchange_part = jnp.einsum(
        "spm,pns->mn", swapped, partners[0], preferred_element_type=jnp.float32
    )
    return lax.psum_scatter(exchange_part, ("aux", "mu", "nu"), scatter_dimension=0, tiled=True)


def solution(mesh):
    in_specs = (P("aux", "nu", "mu"), P("aux", "nu", "mu"), P("mu", "nu"), P("mu", "nu"))
    out_specs = P(("aux", "mu", "nu"), None)
    return jax.shard_map(body, mesh=mesh, in_specs=in_specs, out_specs=out_specs, check_vma=False)
```

profile of v0, /device:TPU:2, one launch (start us, length us, event | category | flops | bytes accessed | tf_op | source)
XLA Modules:
  0.0 498.0 jit_solution(18371565037664750374)
XLA Ops:
  6.5 0.0 all-gather.2.cloned.1.call-start
  6.5 0.7 convert_bitcast_fusion
  7.2 0.1 broadcast_in_dim.21
  7.3 0.1 convert_element_type.30
  7.4 3.1 broadcast_multiply_fusion
  10.5 0.0 copy-start
  10.5 0.0 all-gather.2.cloned.1.call-update
  10.5 1.6 copy-done
  12.0 1.5 fusion.4
  13.5 0.0 copy-start.3
  13.5 0.0 copy-start.2
  13.5 11.6 %all-to-all-start.1 = ((bf16[1,64,64,256]{3,2,0,1:T(8,128)(2,1)}), bf16[1,64,64,256]{3,2,0,1:T(8,128)(2,1)S(1)}, u32[]{:S(2)}, u32[]{:S(2)}) async-start(bf16[1,64,64,256]{3,2,0,1:T(8,128)(2,1)} %fusion.4), calls=%async_computation.1 | async-start | bytes 4194304 | tf_op jit(solution)/shard_map/all_to_all | solution.py:36
  25.1 0.0 copy-done.3
  25.1 0.1 broadcast_in_dim.19
  25.2 0.1 convert_element_type.27
  25.3 0.0 copy-done.2
  25.3 107.9 %all_gather.6 = bf16[256,1024]{0,1:T(8,128)(2,1)S(1)} all-gather(bf16[256,64]{0,1:T(8,128)(2,1)S(1)} %broadcast_multiply_fusion.1), channel_id=1, replica_groups=mesh['aux'=4,'mu'=4,'nu'=16] {'nu'}, dimensions={1}, use_global_device_ids=true | all-gather | bytes 557056 | tf_op jit(solution)/shard_map/all_gather | solution.py:26
  133.2 15.5 %all-gather.2.cloned.1.call-done = bf16[64,64,1024]{2,1,0:T(8,128)(2,1)} async-done(((bf16[64,64,256]{2,1,0:T(8,128)(2,1)}), bf16[64,64,1024]{2,1,0:T(8,128)(2,1)}) %all-gather.2.cloned.1.call-update) | async-done | bytes 8388624 | tf_op jit(solution)/shard_map/all_gather | solution.py:29
  148.8 7.1 %convolution_convert_fusion = bf16[256,64,64]{0,2,1:T(8,128)(2,1)} fusion(bf16[64,64,1024]{2,1,0:T(8,128)(2,1)} %all-gather.2.cloned.1.call-done, bf16[256,1024]{0,1:T(8,128)(2,1)S(1)} %all_gather.6), kind=kOutput, calls=%fused_computation.1 | convolution fusion | flops 2148532224 | bytes 11010048 | tf_op jit(solution)/shard_map/pml,sl->spm/dot_general | solution.py:27
  155.8 0.0 all-to-all-done.1
  155.8 9.2 %all-to-all-start = ((bf16[256,64,64]{0,2,1:T(8,128)(2,1)}), bf16[256,64,64]{0,2,1:T(8,128)(2,1)}, u32[]{:S(2)}, u32[]{:S(2)}) async-start(bf16[256,64,64]{0,2,1:T(8,128)(2,1)} %convolution_convert_fusion), calls=%async_computation | async-start | bytes 4194304 | tf_op jit(solution)/shard_map/all_to_all | solution.py:35
  165.0 0.0 all-reduce.3.cloned.1.call-start
  165.1 1.5 copy.9
  166.5 48.4 %all-to-all-done = bf16[256,64,64]{0,2,1:T(8,128)(2,1)} async-done(((bf16[256,64,64]{0,2,1:T(8,128)(2,1)}), bf16[256,64,64]{0,2,1:T(8,128)(2,1)}, u32[]{:S(2)}, u32[]{:S(2)}) %all-to-all-start) | async-done | bytes 2097184 | tf_op jit(solution)/shard_map/all_to_all | solution.py:35
  214.9 0.0 copy-start.1
  214.9 1.9 copy.7
  216.8 0.3 copy-done.1
  217.1 4.3 convolution_bitcast_fusion
  221.4 0.0 all-reduce.3.cloned.1.call-update
  221.5 268.4 %all-reduce.3.cloned.1.call-done = f32[1024,1024]{1,0:T(8,128)} async-done(((f32[1024,1024]{1,0:T(8,128)}), f32[1024,1024]{1,0:T(8,128)}) %all-reduce.3.cloned.1.call-update) | async-done | bytes 4194320
  489.8 1.4 constant_dynamic-slice_fusion
  (2 shorter events, 0.0 us)
Async XLA Ops:
  6.5 142.2 %all-gather.2.cloned.1.call-start = ((), (), s32[]{:S(2)}) async-start(), calls=%async_computation.2 | async-start | bytes 10485760 | tf_op jit(solution)/shard_map/all_gather | solution.py:29
  10.5 1.6 copy-start
  13.5 11.6 %copy-start.3 = (s32[4,1]{0,1:T(1,128)S(1)}, s32[4,1]{0,1:T(1,128)}, u32[]{:S(2)}) copy-start(s32[4,1]{0,1:T(1,128)} %param.7) | copy-start | bytes 52
  13.5 11.8 %copy-start.2 = (bf16[256,64]{0,1:T(8,128)(2,1)S(1)}, bf16[256,64]{0,1:T(8,128)(2,1)}, u32[]{:S(2)}) copy-start(bf16[256,64]{0,1:T(8,128)(2,1)} %param.6) | copy-start | bytes 98308
  13.5 142.3 %all-to-all-start.1 = ((bf16[1,64,64,256]{3,2,0,1:T(8,128)(2,1)}), bf16[1,64,64,256]{3,2,0,1:T(8,128)(2,1)S(1)}, u32[]{:S(2)}, u32[]{:S(2)}) async-start(bf16[1,64,64,256]{3,2,0,1:T(8,128)(2,1)} %fusion.4), calls=%async_computation.1 | async-start | bytes 4194304 | tf_op jit(solution)/shard_map/all_to_all | solution.py:36
  155.8 59.0 %all-to-all-start = ((bf16[256,64,64]{0,2,1:T(8,128)(2,1)}), bf16[256,64,64]{0,2,1:T(8,128)(2,1)}, u32[]{:S(2)}, u32[]{:S(2)}) async-start(bf16[256,64,64]{0,2,1:T(8,128)(2,1)} %convolution_convert_fusion), calls=%async_computation | async-start | bytes 4194304 | tf_op jit(solution)/shard_map/all_to_all | solution.py:35
  165.0 324.8 %all-reduce.3.cloned.1.call-start = ((), (), s32[]{:S(2)}) async-start(), calls=%async_computation.3 | async-start | bytes 8388608
  214.9 2.2 copy-start.1
Sparse Core Ops, SparseCore 0:
  10.6 138.1 all-gather.1
  221.6 268.2 all-reduce.2
where the time goes:
time: 498 us
  waiting for transfers between devices  332 us (67%)
  blocking collectives  108 us (22%)
  starting transfers between devices  20.8 us (4%)
  between operations  13.4 us (3%)
  matrix products  11.4 us (2%)
  local copies, waits for them, and re-layouts  6.93 us (1%)
  other arithmetic  5.23 us (1%)
    unnamed x3, waiting for transfers between devices  268 us
    all_gather x1, blocking collectives, body(): row_density = lax.all_gather(masked_density, 'nu', axis=1, tiled=True)  108 us
    all_to_all x1, waiting for transfers between devices, body(): lax.all_to_all(contracted, 'nu', split_axis=1, concat_axis=2, tiled=True)  48.4 us
    all_gather x1, waiting for transfers between devices, body(): lax.all_gather(screened, 'mu', axis=2, tiled=True)  15.5 us
    all_to_all x1, starting transfers between devices, body(): lax.all_to_all(screened[None], 'nu', split_axis=1, concat_axis=2, tiled=T...  11.6 us
  transfers between devices with their start and end apart: 4, of which 3 were waited for; matrix products, arithmetic and copies ran while one was open for 2% of the time, Pallas kernels for 0%

commit v1 on v0

v1 whole, which is shorter than its diff:
```python
import jax
import jax.numpy as jnp
from jax import lax
from jax.experimental import pallas as pl
from jax.experimental.pallas import tpu as pltpu
from jax.sharding import Mesh, PartitionSpec as P

BW = 64
NA = 1024
PLANE = ("x", "c", "zh", "zl")
SPREAD = ("x", "zh", "zl")
OWNERS = ("y", "zl", "x", "zh")
NT = (((1,), (1,)), ((), ()))


def first_kernel(where, parts, mask, *refs):
    mine, theirs = refs[0:4], refs[4:8]
    other_out, own_contracted, screened, density, contracted = refs[8:]
    y, c = where[0], where[1]
    for x in range(4):
        for zh in range(4):
            rows = slice((x * 4 + zh) * BW, (x * 4 + zh + 1) * BW)
            for zl in range(2):
                for core in range(2):
                    cols = slice((zl * 2 + core) * 256, (zl * 2 + core + 1) * 256)
                    block = ((x * 2 + core) * 4 + zh) * 2 + zl
                    screened[rows, cols] = parts[block] * mask[x * 4 + zh, :, cols]
    for step in range(4):
        from_y = lax.rem(y + 4 - step, 4)
        for source, core in ((mine[step], c), (theirs[step], 1 - c)):
            for x in range(4):
                for zh in range(4):
                    row = pl.multiple_of((x * 4 + zh) * BW + from_y * 16, 16)
                    for zl in range(2):
                        col = pl.multiple_of((zl * 2 + core) * 256, 256)
                        density[pl.ds(row, 16), pl.ds(col, 256)] = source[(x * 4 + zh) * 2 + zl]
    for chunk in range(4):
        rows = slice(chunk * 256, (chunk + 1) * 256)
        got = jnp.dot(screened[rows, :], density[...], preferred_element_type=jnp.float32)
        got = got.astype(jnp.bfloat16)
        for zl in range(2):
            for core in range(2):
                low = (zl * 2 + core) * BW
                contracted[lax.rem(core + c, 2), pl.ds((chunk * 2 + zl) * BW, BW), :] = got[low : low + BW]
    own_contracted[...] = contracted[0]
    for half in range(2):
        rows = slice(half * 256, (half + 1) * 256)
        other_out[rows, :] = lax.dot_general(
            contracted[1, rows, :], screened[...], NT, preferred_element_type=jnp.float32
        ).astype(jnp.bfloat16)


def second_kernel(contracted, screened, out):
    for half in range(2):
        rows = slice(half * 256, (half + 1) * 256)
        out[rows, :] = lax.dot_general(
            contracted[rows, :], screened[...], NT, preferred_element_type=jnp.float32
        )


def gather_density(density, density_mask):
    y = lax.axis_index("y")
    wide = jnp.repeat(density_mask[:, 0], BW).astype(jnp.bfloat16)
    block = density.T * wide[None, :]
    piece = lax.dynamic_slice(block, (16 * y, 0), (16, 256))
    plane = lax.all_to_all(
        jnp.broadcast_to(piece[None], (32, 16, 256)), SPREAD, split_axis=0, concat_axis=0, tiled=True
    )
    mine = [plane] + [lax.ppermute(plane, "y", [(i, (i + j) % 4) for i in range(4)]) for j in range(1, 4)]
    theirs = [lax.ppermute(one, "c", [(0, 1), (1, 0)]) for one in mine]
    return mine, theirs


def gather_mask(integral_mask):
    wide = jnp.repeat(integral_mask[0, 0], BW).astype(jnp.bfloat16).reshape(1, 2, 128)
    got = lax.all_to_all(
        jnp.broadcast_to(wide, (64, 2, 128)), PLANE, split_axis=0, concat_axis=0, tiled=True
    )
    got = got.reshape(4, 2, 4, 2, 256).transpose(0, 2, 3, 1, 4)
    return got.reshape(16, 1, NA)


def body(integrals, integral_mask, density, density_mask):
    parts = lax.all_to_all(integrals, PLANE, split_axis=0, concat_axis=0, tiled=True)
    mask = gather_mask(integral_mask)
    mine, theirs = gather_density(density, density_mask)
    where = jnp.stack([lax.axis_index("y"), lax.axis_index("c")]).astype(jnp.int32)
    vmem = pl.BlockSpec(memory_space=pltpu.VMEM)
    smem = pl.BlockSpec(memory_space=pltpu.SMEM)
    half = jax.ShapeDtypeStruct((NA // 2, NA), jnp.bfloat16)
    other_half, own_contracted, screened = pl.pallas_call(
        first_kernel,
        out_shape=(half, half, jax.ShapeDtypeStruct((NA, NA), jnp.bfloat16)),
        in_specs=[smem] + [vmem] * 10,
        out_specs=(vmem, vmem, vmem),
        scratch_shapes=[pltpu.VMEM((NA, NA), jnp.bfloat16), pltpu.VMEM((2, NA // 2, NA), jnp.bfloat16)],
        compiler_params=pltpu.CompilerParams(vmem_limit_bytes=40 * 2**20),
        cost_estimate=pl.CostEstimate(flops=3 * 2**30, bytes_accessed=8 * 2**20, transcendentals=0),
        name="contract",
    )(where, parts, mask, *mine, *theirs)
    arrived = lax.ppermute(other_half, "c", [(0, 1), (1, 0)])
    own_half = pl.pallas_call(
        second_kernel,
        out_shape=jax.ShapeDtypeStruct((NA // 2, NA), jnp.float32),
        in_specs=[vmem] * 2,
        out_specs=vmem,
        compiler_params=pltpu.CompilerParams(vmem_limit_bytes=40 * 2**20),
        cost_estimate=pl.CostEstimate(flops=2**30, bytes_accessed=5 * 2**20, transcendentals=0),
        name="exchange",
    )(own_contracted, screened)
    term = (own_half + arrived.astype(jnp.float32)).astype(jnp.bfloat16).reshape(128, 4, NA)
    terms = lax.all_to_all(term, OWNERS, split_axis=0, concat_axis=0, tiled=True)
    return jnp.sum(terms.astype(jnp.float32), axis=0)


def solution(mesh):
    fine = Mesh(mesh.devices.reshape(4, 2, 2, 4, 4), ("y", "zl", "c", "x", "zh"))
    m, n = ("zl", "c"), ("x", "zh")
    in_specs = (P("y", n, m), P("y", n, m), P(m, n), P(m, n))
    out_specs = P(("y", "zl", "c", "x", "zh"), None)
    return jax.shard_map(body, mesh=fine, in_specs=in_specs, out_specs=out_specs, check_vma=False)
```

time: 498 us -> 146 us (0.29)
  waiting for transfers between devices: 332 us -> 53.2 us
  blocking collectives: 108 us -> 56.4 us
  between operations: 13.4 us -> 0.12 us
  matrix products: 11.4 us -> 0 us
  Pallas kernels: 0 us -> 6.47 us
  local copies, waits for them, and re-layouts: 6.93 us -> 1.56 us
    unnamed x3 -> x0, waiting for transfers between devices: 268 us -> none
    all_gather x1 -> x0, blocking collectives: 108 us -> none  [body(): row_density = lax.all_gather(masked_density, 'nu', axis=1, tiled=True)]
    all_to_all x0 -> x2, blocking collectives: none -> 56.4 us  [the longest x1 41 us: body(): lax.all_to_all(term, OWNERS, split_axis=0, concat_axis=0, tiled=True)]
    ppermute x0 -> x8, waiting for transfers between devices: none -> 15.9 us  [the longest x3 13.1 us: gather_density(): lax.ppermute(plane, 'y', [(i, (i + j) % 4) for i in range(4)])]
    all_gather x1 -> x0, waiting for transfers between devices: 15.5 us -> none  [body(): lax.all_gather(screened, 'mu', axis=2, tiled=True)]
    dot_general x2 -> x0, matrix products: 11.4 us -> none  [the longest x1 7.08 us: body(): jnp.einsum('pml,sl->spm', lax.all_gather(screened, 'mu', axis=2, tiled=Tr...]
    all_to_all x2, waiting for transfers between devices: 48.4 us -> 37.3 us  [the longest x1 30.2 us: body(): lax.all_to_all(integrals, PLANE, split_axis=0, concat_axis=0, tiled=True)]
    pallas_call x0 -> x2, Pallas kernels: none -> 6.47 us  [the longest x1 5.19 us: body(): pl.pallas_call(first_kernel, out_shape=(half, half, jax.ShapeDtypeStruct(...]
  transfers between devices with their start and end apart: 4 -> 10, of which waited for: 3 -> 6; matrix products, arithmetic and copies ran while one was open for 2% -> 1% of each run, Pallas kernels for 0% -> 1%
where the time goes in v1:
time: 146 us; the launch traced here: 145 us
  blocking collectives  56.4 us (39%)
  waiting for transfers between devices  53.2 us (36%)
  starting transfers between devices  23.6 us (16%)
  Pallas kernels  6.47 us (4%)
  other arithmetic  3.54 us (2%)
  local copies, waits for them, and re-layouts  1.56 us (1%)
    all_to_all x1, blocking collectives, body(): lax.all_to_all(term, OWNERS, split_axis=0, concat_axis=0, tiled=True)  41 us
    all_to_all x1, waiting for transfers between devices, body(): lax.all_to_all(integrals, PLANE, split_axis=0, concat_axis=0, tiled=True)  30.2 us
    all_to_all x1, blocking collectives, gather_density(): lax.all_to_all(jnp.broadcast_to(piece[None], (32, 16, 256)), SPREAD, spli...  15.4 us
    ppermute x3, waiting for transfers between devices, gather_density(): lax.ppermute(plane, 'y', [(i, (i + j) % 4) for i in range(4)])  13.1 us
    all_to_all x1, starting transfers between devices, gather_mask(): lax.all_to_all(jnp.broadcast_to(wide, (64, 2, 128)), PLANE, split_axis=0,...  12 us
    all_to_all x1, waiting for transfers between devices, gather_mask(): lax.all_to_all(jnp.broadcast_to(wide, (64, 2, 128)), PLANE, split_axis=0,...  7.13 us
    all_to_all x1, starting transfers between devices, body(): lax.all_to_all(integrals, PLANE, split_axis=0, concat_axis=0, tiled=True)  6.05 us
    pallas_call x1, Pallas kernels, body(): pl.pallas_call(first_kernel, out_shape=(half, half, jax.ShapeDtypeStruct(...  5.19 us
  transfers between devices with their start and end apart: 10, of which 6 were waited for; matrix products, arithmetic and copies ran while one was open for 1% of the time, Pallas kernels for 1%

profile of v1, /device:TPU:2, one launch (start us, length us, event | category | flops | bytes accessed | tf_op | source)
XLA Modules:
  0.0 144.9 jit_solution(15955445603397588547)
XLA Ops:
  0.0 0.7 convert_reduce_fusion.1
  0.7 0.1 convert_element_type.38
  0.8 0.1 broadcast_in_dim.8
  0.8 0.1 convert_element_type.39
  0.9 0.6 broadcast_in_dim.9
  1.5 12.0 %all-to-all-start.1 = ((bf16[64,2,128]{2,1,0:T(2,128)(2,1)}), bf16[64,2,128]{2,1,0:T(2,128)(2,1)S(1)}, u32[]{:S(2)}, u32[]{:S(2)}) async-start(bf16[64,2,128]{2,1,0:T(2,128)(2,1)} %broadcast_in_dim.9), calls=%async_computation.1 | async-start | bytes 65536 | tf_op jit(solution)/shard_map/all_to_all | solution.py:76
  13.6 0.7 convert_bitcast_fusion
  14.2 0.1 broadcast_in_dim.20
  14.3 0.1 convert_element_type.42
  14.4 0.7 fusion
  15.1 7.1 %all-to-all-done.1 = bf16[64,2,128]{2,1,0:T(2,128)(2,1)S(1)} async-done(((bf16[64,2,128]{2,1,0:T(2,128)(2,1)}), bf16[64,2,128]{2,1,0:T(2,128)(2,1)S(1)}, u32[]{:S(2)}, u32[]{:S(2)}) %all-to-all-start.1) | async-done | bytes 32800 | tf_op jit(solution)/shard_map/all_to_all | solution.py:76
  22.3 15.4 %all_to_all.20.refs_0_ = bf16[32,16,256]{2,1,0:T(8,128)(2,1)S(1)} all-to-all(bf16[32,16,256]{2,1,0:T(8,128)(2,1)S(1)} %broadcast_in_dim.21), channel_id=1, replica_groups=mesh['y'=4,'zl'=2,'c'=2,'x'=4,'zh'=4] {'x','zh','zl'}, dimensions={0} | all-to-all | bytes 524288 | tf_op jit(solution)/shard_map/all_to_all | solution.py:66
  37.7 6.1 %all-to-all-start = ((bf16[64,64,256]{2,1,0:T(8,128)(2,1)}), bf16[64,64,256]{2,1,0:T(8,128)(2,1)S(1)}, u32[]{:S(2)}, u32[]{:S(2)}) async-start(bf16[64,64,256]{2,1,0:T(8,128)(2,1)} %param.4), calls=%async_computation | async-start | bytes 4194304 | tf_op jit(solution)/shard_map/all_to_all | solution.py:84
  43.8 3.1 %collective-permute-start.2 = (bf16[32,16,256]{2,1,0:T(8,128)(2,1)S(1)}, bf16[32,16,256]{2,1,0:T(8,128)(2,1)S(1)}, u32[]{:S(2)}, u32[]{:S(2)}) collective-permute-start(bf16[32,16,256]{2,1,0:T(8,128)(2,1)S(1)} %all_to_all.20.refs_0_), channel_id=1, source_target_pairs={{0,192},{64,0},{128,64},{192,128},{1,193},{65,1},{129,65},{193,129... | collective-permute-start | bytes 786440 | tf_op jit(solution)/shard_map/ppermute | solution.py:69
  46.8 0.6 collective-permute-start.1
  47.5 1.0 collective-permute-start
  48.4 0.0 collective-permute-start.3
  48.5 9.9 %collective-permute-done.2.refs_3_ = bf16[32,16,256]{2,1,0:T(8,128)(2,1)S(1)} collective-permute-done((bf16[32,16,256]{2,1,0:T(8,128)(2,1)S(1)}, bf16[32,16,256]{2,1,0:T(8,128)(2,1)S(1)}, u32[]{:S(2)}, u32[]{:S(2)}) %collective-permute-start.2) | collective-permute-done | bytes 262176 | tf_op jit(solution)/shard_map/ppermute | solution.py:69
  58.4 0.0 collective-permute-start.6
  58.4 0.0 collective-permute-done.1.refs_2_
  58.4 0.5 collective-permute-start.5
  58.9 3.2 %collective-permute-done.refs_1_ = bf16[32,16,256]{2,1,0:T(8,128)(2,1)S(1)} collective-permute-done((bf16[32,16,256]{2,1,0:T(8,128)(2,1)S(1)}, bf16[32,16,256]{2,1,0:T(8,128)(2,1)S(1)}, u32[]{:S(2)}, u32[]{:S(2)}) %collective-permute-start) | collective-permute-done | bytes 262176 | tf_op jit(solution)/shard_map/ppermute | solution.py:69
  62.1 0.0 collective-permute-start.4
  62.1 0.1 pad_add_fusion.where
  62.3 0.0 collective-permute-done.3.refs_4_
  62.3 0.0 collective-permute-done.6.refs_7_
  62.3 0.0 collective-permute-done.5.refs_6_
  62.3 1.4 collective-permute-done.4.refs_5_
  63.7 30.2 %all-to-all-done.parts = bf16[64,64,256]{2,1,0:T(8,128)(2,1)S(1)} async-done(((bf16[64,64,256]{2,1,0:T(8,128)(2,1)}), bf16[64,64,256]{2,1,0:T(8,128)(2,1)S(1)}, u32[]{:S(2)}, u32[]{:S(2)}) %all-to-all-start) | async-done | bytes 2097184 | tf_op jit(solution)/shard_map/all_to_all | solution.py:84
  93.9 5.2 %contract.1 = (bf16[512,1024]{1,0:T(8,128)(2,1)S(1)}, bf16[512,1024]{1,0:T(8,128)(2,1)S(1)}, bf16[1024,1024]{1,0:T(8,128)(2,1)S(1)}) custom-call(s32[2]{0:T(128)S(1)} %pad_add_fusion.where, bf16[64,64,256]{2,1,0:T(8,128)(2,1)S(1)} %all-to-all-done.parts, bf16[16,1,1024]{2,1,0:T(2,128)(2,1)S(1)} %reshape.36.mask, ...), custom_call_target="tpu_custom_call" | custom-call | flops 3221225472 | bytes 8388608 | tf_op jit(solution)/shard_map/contract/pallas_call | solution.py:91
  99.1 0.3 collective-permute-start.7
  99.4 1.3 exchange.1
  100.7 1.4 collective-permute-done.7
  102.0 0.3 add_convert_fusion
  102.4 0.4 reshape.35
  102.8 41.0 %all_to_all.21 = bf16[128,4,1024]{2,1,0:T(4,128)(2,1)S(1)} all-to-all(bf16[128,4,1024]{2,1,0:T(4,128)(2,1)S(1)} %reshape.35), channel_id=1, replica_groups=mesh['y'=4,'zl'=2,'c'=2,'x'=4,'zh'=4] {'y','zl','x','zh'}, dimensions={0} | all-to-all | bytes 2097152 | tf_op jit(solution)/shard_map/all_to_all | solution.py:112
  143.8 1.1 convert_reduce_fusion
  (4 shorter events, 0.1 us)
Async XLA Ops:
  1.5 20.7 %all-to-all-start.1 = ((bf16[64,2,128]{2,1,0:T(2,128)(2,1)}), bf16[64,2,128]{2,1,0:T(2,128)(2,1)S(1)}, u32[]{:S(2)}, u32[]{:S(2)}) async-start(bf16[64,2,128]{2,1,0:T(2,128)(2,1)} %broadcast_in_dim.9), calls=%async_computation.1 | async-start | bytes 65536 | tf_op jit(solution)/shard_map/all_to_all | solution.py:76
  37.7 56.2 %all-to-all-start = ((bf16[64,64,256]{2,1,0:T(8,128)(2,1)}), bf16[64,64,256]{2,1,0:T(8,128)(2,1)S(1)}, u32[]{:S(2)}, u32[]{:S(2)}) async-start(bf16[64,64,256]{2,1,0:T(8,128)(2,1)} %param.4), calls=%async_computation | async-start | bytes 4194304 | tf_op jit(solution)/shard_map/all_to_all | solution.py:84
  43.8 14.6 %collective-permute-start.2 = (bf16[32,16,256]{2,1,0:T(8,128)(2,1)S(1)}, bf16[32,16,256]{2,1,0:T(8,128)(2,1)S(1)}, u32[]{:S(2)}, u32[]{:S(2)}) collective-permute-start(bf16[32,16,256]{2,1,0:T(8,128)(2,1)S(1)} %all_to_all.20.refs_0_), channel_id=1, source_target_pairs={{0,192},{64,0},{128,64},{192,128},{1,193},{65,1},{129,65},{193,129... | collective-permute-start | bytes 786440 | tf_op jit(solution)/shard_map/ppermute | solution.py:69
  46.8 11.5 %collective-permute-start.1 = (bf16[32,16,256]{2,1,0:T(8,128)(2,1)S(1)}, bf16[32,16,256]{2,1,0:T(8,128)(2,1)S(1)}, u32[]{:S(2)}, u32[]{:S(2)}) collective-permute-start(bf16[32,16,256]{2,1,0:T(8,128)(2,1)S(1)} %all_to_all.20.refs_0_), channel_id=1, source_target_pairs={{0,128},{64,192},{128,0},{192,64},{1,129},{65,193},{129,1},{193,65... | collective-permute-start | bytes 786440 | tf_op jit(solution)/shard_map/ppermute | solution.py:69
  47.5 14.6 %collective-permute-start = (bf16[32,16,256]{2,1,0:T(8,128)(2,1)S(1)}, bf16[32,16,256]{2,1,0:T(8,128)(2,1)S(1)}, u32[]{:S(2)}, u32[]{:S(2)}) collective-permute-start(bf16[32,16,256]{2,1,0:T(8,128)(2,1)S(1)} %all_to_all.20.refs_0_), channel_id=1, source_target_pairs={{0,64},{64,128},{128,192},{192,0},{1,65},{65,129},{129,193},{193,1... | collective-permute-start | bytes 786440 | tf_op jit(solution)/shard_map/ppermute | solution.py:69
  48.4 13.8 %collective-permute-start.3 = (bf16[32,16,256]{2,1,0:T(8,128)(2,1)S(1)}, bf16[32,16,256]{2,1,0:T(8,128)(2,1)S(1)}, u32[]{:S(2)}, u32[]{:S(2)}) collective-permute-start(bf16[32,16,256]{2,1,0:T(8,128)(2,1)S(1)} %all_to_all.20.refs_0_), channel_id=1, source_target_pairs={{0,16},{16,0},{1,17},{17,1},{2,18},{18,2},{3,19},{19,3},{4,20},{20... | collective-permute-start | bytes 786440 | tf_op jit(solution)/shard_map/ppermute | solution.py:70
  58.4 3.9 %collective-permute-start.6 = (bf16[32,16,256]{2,1,0:T(8,128)(2,1)S(1)}, bf16[32,16,256]{2,1,0:T(8,128)(2,1)}, u32[]{:S(2)}, u32[]{:S(2)}) collective-permute-start(bf16[32,16,256]{2,1,0:T(8,128)(2,1)S(1)} %collective-permute-done.2.refs_3_), channel_id=1, source_target_pairs={{0,16},{16,0},{1,17},{17,1},{2,18},{18,2},{3,19},{19,3},{4,20},{20... | collective-permute-start | bytes 786440 | tf_op jit(solution)/shard_map/ppermute | solution.py:70
  58.4 3.9 %collective-permute-start.5 = (bf16[32,16,256]{2,1,0:T(8,128)(2,1)S(1)}, bf16[32,16,256]{2,1,0:T(8,128)(2,1)}, u32[]{:S(2)}, u32[]{:S(2)}) collective-permute-start(bf16[32,16,256]{2,1,0:T(8,128)(2,1)S(1)} %collective-permute-done.1.refs_2_), channel_id=1, source_target_pairs={{0,16},{16,0},{1,17},{17,1},{2,18},{18,2},{3,19},{19,3},{4,20},{20... | collective-permute-start | bytes 786440 | tf_op jit(solution)/shard_map/ppermute | solution.py:70
  62.1 1.7 %collective-permute-start.4 = (bf16[32,16,256]{2,1,0:T(8,128)(2,1)S(1)}, bf16[32,16,256]{2,1,0:T(8,128)(2,1)}, u32[]{:S(2)}, u32[]{:S(2)}) collective-permute-start(bf16[32,16,256]{2,1,0:T(8,128)(2,1)S(1)} %collective-permute-done.refs_1_), channel_id=1, source_target_pairs={{0,16},{16,0},{1,17},{17,1},{2,18},{18,2},{3,19},{19,3},{4,20},{20... | collective-permute-start | bytes 786440 | tf_op jit(solution)/shard_map/ppermute | solution.py:70
  99.1 2.9 %collective-permute-start.7 = (bf16[512,1024]{1,0:T(8,128)(2,1)S(1)}, bf16[512,1024]{1,0:T(8,128)(2,1)S(1)}, u32[]{:S(2)}, u32[]{:S(2)}) collective-permute-start(bf16[512,1024]{1,0:T(8,128)(2,1)S(1)} %get-tuple-element.10), channel_id=1, source_target_pairs={{0,16},{16,0},{1,17},{17,1},{2,18},{18,2},{3,19},{19,3},{4,20},{20... | collective-permute-start | bytes 3145736 | tf_op jit(solution)/shard_map/ppermute | solution.py:101

commit v2 on v0

v2 whole, which is shorter than its diff:
```python
import jax
import jax.numpy as jnp
from jax import lax
from jax.experimental import pallas as pl
from jax.experimental.pallas import tpu as pltpu
from jax.sharding import Mesh, PartitionSpec as P

BW = 64
NA = 1024
PLANE = ("x", "c", "zh", "zl")
NT = (((1,), (1,)), ((), ()))
SWAP = [(0, 1), (1, 0)]
VMEM = pl.BlockSpec(memory_space=pltpu.VMEM)
HBM = pl.BlockSpec(memory_space=pltpu.HBM)
SMEM = pl.BlockSpec(memory_space=pltpu.SMEM)
PARAMS = pltpu.CompilerParams(vmem_limit_bytes=40 * 2**20)
WIDE = pltpu.CompilerParams(vmem_limit_bytes=46 * 2**20)
ALONE = pltpu.CompilerParams(vmem_limit_bytes=59 * 2**20)


def shape(*sizes, dtype=jnp.bfloat16):
    return jax.ShapeDtypeStruct(sizes, dtype)


def from_four(one, axis):
    return [one] + [lax.ppermute(one, axis, [(i, i ^ j) for i in range(4)]) for j in range(1, 4)]


def place_kernel(where, pieces0, pieces1, pieces2, pieces3, half):
    y, x, zh, zl = where[0], where[1], where[2], where[3]
    for y_step, pieces in enumerate((pieces0, pieces1, pieces2, pieces3)):
        from_y = lax.bitwise_xor(y, y_step)
        from_zl = lax.bitwise_xor(zl, from_y // 2)
        col = pl.multiple_of(from_zl * 256, 256)
        for x_step in range(4):
            from_x = lax.bitwise_xor(x, x_step)
            row_block = lax.rem(from_x, 2) * 2 + from_x // 2
            for z_step in range(2):
                from_zh = lax.bitwise_xor(zh, lax.rem(from_y, 2) * 2 + z_step)
                row = pl.multiple_of(row_block * 256 + from_zh * BW, BW)
                half[pl.ds(row, BW), pl.ds(col, 256)] = pieces[x_step, z_step]


def join_kernel(where, mine, theirs, whole, sems):
    core = where[4]
    copies = [
        pltpu.make_async_copy(
            source, whole.at[pl.ds(0, NA), pl.ds(pl.multiple_of(place * 512, 512), 512)], sems.at[index]
        )
        for index, (source, place) in enumerate(((mine, core), (theirs, 1 - core)))
    ]
    for copy in copies:
        copy.start()
    for copy in copies:
        copy.wait()


def scale_row(blocks):
    place = lax.broadcasted_iota(jnp.int32, (1, 256), 1) // BW
    row = jnp.zeros((1, 256), jnp.float32)
    for index, entry in enumerate(blocks):
        row = jnp.where(place == index, entry.astype(jnp.float32), row)
    return row


def block_kernel(mask, block, out, scalars, held, sems):
    copies = [
        pltpu.make_async_copy(mask, scalars, sems.at[0]),
        pltpu.make_async_copy(block, held, sems.at[1]),
    ]
    for copy in copies:
        copy.start()
    for copy in copies:
        copy.wait()
    row = scale_row([scalars[0, index] for index in range(4)])
    out[...] = (held[...].astype(jnp.float32) * row).astype(jnp.bfloat16)


def screen_kernel(mask, integrals, out, scalars, held, sems, out_sems):
    inward, outward = [], []
    for index in range(8):
        part = pl.ds(index * 8, 8)
        inward.append(pltpu.make_async_copy(integrals.at[part], held.at[part], sems.at[index]))
        outward.append(pltpu.make_async_copy(held.at[part], out.at[part], out_sems.at[index]))
    first = pltpu.make_async_copy(mask, scalars, sems.at[8])
    first.start()
    for copy in inward:
        copy.start()
    first.wait()
    row = scale_row([scalars[0, 0, index] for index in range(4)]).astype(jnp.bfloat16)
    for index in range(8):
        part = pl.ds(index * 8, 8)
        inward[index].wait()
        held[part] = held[part] * row[None]
        outward[index].start()
    for copy in outward:
        copy.wait()


def pick_rows(core, screened, rows):
    for x in range(4):
        for y in range(4):
            for zl in range(2):
                low = pl.multiple_of((y * 4 + zl * 2 + core) * BW + x * 16, 16)
                to = ((x * 4 + y) * 2 + zl) * 16
                rows[to : to + 16, :] = screened[pl.ds(low, 16), :]


def contract_rows(rows, density, contracted, half):
    contracted[:, half] = jnp.dot(rows[...], density[:, half], preferred_element_type=jnp.float32).astype(
        jnp.bfloat16
    )


def exchange_rows(contracted, screened, half):
    return lax.dot_general(contracted[...], screened[half, :], NT, preferred_element_type=jnp.float32)


HALVES = (slice(0, 512), slice(512, 1024))


def first_kernel(where, parts, density_in, out, screened, density, rows, contracted, sems):
    fetch = [
        pltpu.make_async_copy(
            density_in.at[pl.ds(0, NA), pl.ds(half * 512, 512)],
            density.at[:, pl.ds(half * 512, 512)],
            sems.at[half],
        )
        for half in range(2)
    ]
    for copy in fetch:
        copy.start()
    for x in range(4):
        for zh in range(4):
            low = (x * 4 + zh) * BW
            for zl in range(2):
                for core in range(2):
                    left = (core * 2 + zl) * 256
                    screened[low : low + BW, left : left + 256] = parts[((x * 2 + core) * 4 + zh) * 2 + zl]
    pick_rows(1 - where[4], screened, rows)
    for copy, half in zip(fetch, HALVES):
        copy.wait()
        contract_rows(rows, density, contracted, half)
    for half in HALVES:
        out[:, half] = exchange_rows(contracted, screened, half).astype(jnp.bfloat16)


def second_kernel(where, screened, density, out, rows, contracted):
    pick_rows(where[4], screened, rows)
    for half in HALVES:
        contract_rows(rows, density, contracted, half)
    for half in HALVES:
        out[:, half] = exchange_rows(contracted, screened, half)


def gather_z(block):
    return [
        lax.ppermute(
            block,
            ("y", "zl", "zh"),
            [(y * 8 + z, y * 8 + (z ^ (y * 2 + step))) for y in range(4) for z in range(8)],
        )
        for step in range(2)
    ]


def gather(where, two):
    plane = jnp.stack(from_four(jnp.stack(two), "x"))
    half = pl.pallas_call(
        place_kernel,
        out_shape=shape(NA, 512),
        in_specs=[SMEM] + [VMEM] * 4,
        out_specs=VMEM,
        compiler_params=PARAMS,
        cost_estimate=pl.CostEstimate(flops=0, bytes_accessed=2 * 2**20, transcendentals=0),
        name="place",
    )(where, *from_four(plane, "y"))
    return pl.pallas_call(
        join_kernel,
        out_shape=shape(8 * NA, NA),
        in_specs=[SMEM] + [VMEM] * 2,
        out_specs=HBM,
        scratch_shapes=[pltpu.SemaphoreType.DMA((2,))],
        compiler_params=PARAMS,
        cost_estimate=pl.CostEstimate(flops=0, bytes_accessed=4 * 2**20, transcendentals=0),
        name="join",
    )(where, half, lax.ppermute(half, "c", SWAP))


def body(integrals, integral_mask, density, density_mask):
    where = jnp.stack([lax.axis_index(name) for name in ("y", "x", "zh", "zl", "c")]).astype(jnp.int32)
    block = pl.pallas_call(
        block_kernel,
        out_shape=shape(BW, 256),
        in_specs=[HBM] * 2,
        out_specs=VMEM,
        scratch_shapes=[
            pltpu.SMEM((1, 4), jnp.int32),
            pltpu.VMEM((BW, 256), jnp.bfloat16),
            pltpu.SemaphoreType.DMA((2,)),
        ],
        compiler_params=ALONE,
        name="block",
    )(density_mask.T, density.T)
    screened = pl.pallas_call(
        screen_kernel,
        out_shape=shape(64, 64, 256),
        in_specs=[HBM] * 2,
        out_specs=HBM,
        scratch_shapes=[
            pltpu.SMEM((1, 1, 4), jnp.int32),
            pltpu.VMEM((64, 64, 256), jnp.bfloat16),
            pltpu.SemaphoreType.DMA((9,)),
            pltpu.SemaphoreType.DMA((8,)),
        ],
        compiler_params=ALONE,
        cost_estimate=pl.CostEstimate(flops=0, bytes_accessed=4 * 2**20, transcendentals=0),
        name="screen",
    )(integral_mask, integrals)
    two = gather_z(block)
    screened, two = lax.optimization_barrier((screened, two))
    parts = lax.all_to_all(screened, PLANE, split_axis=0, concat_axis=0, tiled=True)
    whole = gather(where, two)
    other_half, screened, whole = pl.pallas_call(
        first_kernel,
        out_shape=(shape(NA // 2, NA), shape(NA, NA), shape(NA, NA)),
        in_specs=[SMEM, VMEM, HBM],
        out_specs=(VMEM, VMEM, VMEM),
        scratch_shapes=[pltpu.VMEM((NA // 2, NA), jnp.bfloat16)] * 2 + [pltpu.SemaphoreType.DMA((2,))],
        compiler_params=WIDE,
        cost_estimate=pl.CostEstimate(flops=2**31, bytes_accessed=8 * 2**20, transcendentals=0),
        name="other",
    )(where, parts, whole)
    arrived = lax.ppermute(other_half, "c", SWAP)
    own_half = pl.pallas_call(
        second_kernel,
        out_shape=shape(NA // 2, NA, dtype=jnp.float32),
        in_specs=[SMEM] + [VMEM] * 2,
        out_specs=VMEM,
        scratch_shapes=[pltpu.VMEM((NA // 2, NA), jnp.bfloat16)] * 2,
        compiler_params=PARAMS,
        cost_estimate=pl.CostEstimate(flops=2**31, bytes_accessed=6 * 2**20, transcendentals=0),
        name="own",
    )(where, screened, whole)
    term = (own_half + arrived.astype(jnp.float32)).astype(jnp.bfloat16).reshape(16, 32, NA)
    layers = lax.all_to_all(term, ("x", "y"), split_axis=0, concat_axis=0, tiled=True)
    column = jnp.sum(layers.astype(jnp.float32), axis=0).reshape(8, 4, NA)
    terms = lax.all_to_all(column, ("zl", "zh"), split_axis=0, concat_axis=0, tiled=True)
    return jnp.sum(terms, axis=0)


def solution(mesh):
    fine = Mesh(mesh.devices.reshape(4, 2, 2, 4, 4), ("y", "zl", "c", "x", "zh"))
    m, n = ("zl", "c"), ("x", "zh")
    in_specs = (P("y", n, m), P("y", n, m), P(m, n), P(m, n))
    out_specs = P(("y", "zl", "c", "x", "zh"), None)
    return jax.shard_map(body, mesh=fine, in_specs=in_specs, out_specs=out_specs, check_vma=False)
```

time: 498 us -> 118 us (0.24)
  waiting for transfers between devices: 332 us -> 33.5 us
  blocking collectives: 108 us -> 38.8 us
  Pallas kernels: 0 us -> 13.7 us
  between operations: 13.4 us -> 0.13 us
  matrix products: 11.4 us -> 0 us
  starting transfers between devices: 20.8 us -> 29 us
  local copies, waits for them, and re-layouts: 6.93 us -> 0.12 us
    unnamed x3 -> x0, waiting for transfers between devices: 268 us -> none
    all_gather x1 -> x0, blocking collectives: 108 us -> none  [body(): row_density = lax.all_gather(masked_density, 'nu', axis=1, tiled=True)]
    all_to_all x0 -> x2, blocking collectives: none -> 38.8 us  [the longest x1 27.1 us: body(): lax.all_to_all(term, ('x', 'y'), split_axis=0, concat_axis=0, tiled=True)]
    all_to_all x2 -> x1, waiting for transfers between devices: 48.4 us -> 11.8 us  [body(): lax.all_to_all(screened, PLANE, split_axis=0, concat_axis=0, tiled=True)]
    ppermute x0 -> x10, waiting for transfers between devices: none -> 21.7 us  [the longest x6 19 us: from_four(): lax.ppermute(one, axis, [(i, i ^ j) for i in range(4)])]
    ppermute x0 -> x10, starting transfers between devices: none -> 18.7 us  [the longest x6 13.8 us: from_four(): lax.ppermute(one, axis, [(i, i ^ j) for i in range(4)])]
    all_gather x1 -> x0, waiting for transfers between devices: 15.5 us -> none  [body(): lax.all_gather(screened, 'mu', axis=2, tiled=True)]
    pallas_call x0 -> x6, Pallas kernels: none -> 13.7 us  [the longest x1 4.29 us: body(): pl.pallas_call(first_kernel, out_shape=(shape(NA // 2, NA), shape(NA, NA)...]
  transfers between devices with their start and end apart: 4 -> 11, of which waited for: 3 -> 6; matrix products, arithmetic and copies ran while one was open for 2% -> 0% of each run, Pallas kernels for 0% -> 7%
where the time goes in v2:
time: 118 us; the launch traced here: 116 us
  blocking collectives  38.8 us (33%)
  waiting for transfers between devices  33.5 us (28%)
  starting transfers between devices  29 us (25%)
  Pallas kernels  13.7 us (12%)
  other arithmetic  1.22 us (1%)
    all_to_all x1, blocking collectives, body(): lax.all_to_all(term, ('x', 'y'), split_axis=0, concat_axis=0, tiled=True)  27.1 us
    ppermute x6, waiting for transfers between devices, from_four(): lax.ppermute(one, axis, [(i, i ^ j) for i in range(4)])  19 us
    ppermute x6, starting transfers between devices, from_four(): lax.ppermute(one, axis, [(i, i ^ j) for i in range(4)])  13.8 us
    all_to_all x1, waiting for transfers between devices, body(): lax.all_to_all(screened, PLANE, split_axis=0, concat_axis=0, tiled=True)  11.8 us
    all_to_all x1, blocking collectives, body(): lax.all_to_all(column, ('zl', 'zh'), split_axis=0, concat_axis=0, tiled=T...  11.7 us
    all_to_all x1, starting transfers between devices, body(): lax.all_to_all(screened, PLANE, split_axis=0, concat_axis=0, tiled=True)  10.2 us
    ppermute x2, starting transfers between devices, gather_z(): lax.ppermute(block, ('y', 'zl', 'zh'), [(y * 8 + z, y * 8 + (z ^ y * 2 +...  4.76 us
    pallas_call x1, Pallas kernels, body(): pl.pallas_call(first_kernel, out_shape=(shape(NA // 2, NA), shape(NA, NA)...  4.29 us
  transfers between devices with their start and end apart: 11, of which 6 were waited for; matrix products, arithmetic and copies ran while one was open for 0% of the time, Pallas kernels for 7%

profile of v2, /device:TPU:2, one launch (start us, length us, event | category | flops | bytes accessed | tf_op | source)
XLA Modules:
  0.0 116.4 jit_solution(13403820595543237138)
XLA Ops:
  0.0 1.4 %block.1 = bf16[64,256]{1,0:T(8,128)(2,1)} custom-call(s32[1,4]{1,0:T(1,128)} %bitcast.22, bf16[64,256]{1,0:T(8,128)(2,1)} %bitcast.19), custom_call_target="tpu_custom_call" | custom-call | tf_op jit(solution)/shard_map/block/pallas_call | solution.py:192
  1.4 3.4 %collective-permute-start.1 = (bf16[64,256]{1,0:T(8,128)(2,1)}, bf16[64,256]{1,0:T(8,128)(2,1)S(1)}, u32[]{:S(2)}, u32[]{:S(2)}) collective-permute-start(bf16[64,256]{1,0:T(8,128)(2,1)} %block.1), channel_id=1, source_target_pairs={{0,1},{1,0},{2,3},{3,2},{32,33},{33,32},{34,35},{35,34},{64,67},{6... | collective-permute-start | bytes 98312 | tf_op jit(solution)/shard_map/ppermute | solution.py:158
  4.8 1.4 %collective-permute-start = (bf16[64,256]{1,0:T(8,128)(2,1)}, bf16[64,256]{1,0:T(8,128)(2,1)S(1)}, u32[]{:S(2)}, u32[]{:S(2)}) collective-permute-start(bf16[64,256]{1,0:T(8,128)(2,1)} %block.1), channel_id=1, source_target_pairs={{0,0},{1,1},{2,2},{3,3},{32,32},{33,33},{34,34},{35,35},{64,66},{6... | collective-permute-start | bytes 98312 | tf_op jit(solution)/shard_map/ppermute | solution.py:158
  6.2 2.5 %screen.1 = bf16[64,64,256]{2,1,0:T(8,128)(2,1)} custom-call(s32[1,1,4]{2,1,0:T(1,128)} %mask.1, bf16[64,64,256]{2,1,0:T(8,128)(2,1)} %integrals.1), custom_call_target="tpu_custom_call" | custom-call | bytes 4194304 | tf_op jit(solution)/shard_map/screen/pallas_call | solution.py:205
  8.6 0.0 collective-permute-done.1
  8.6 0.0 collective-permute-done
  8.7 10.2 %all-to-all-start = ((bf16[64,64,256]{2,1,0:T(8,128)(2,1)}), bf16[64,64,256]{2,1,0:T(8,128)(2,1)S(1)}, u32[]{:S(2)}, u32[]{:S(2)}) async-start(bf16[64,64,256]{2,1,0:T(8,128)(2,1)} %screen.1), calls=%async_computation | async-start | bytes 4194304 | tf_op jit(solution)/shard_map/all_to_all | solution.py:222
  18.9 2.4 %collective-permute-start.3 = (bf16[2,64,256]{2,1,0:T(8,128)(2,1)S(1)}, bf16[2,64,256]{2,1,0:T(8,128)(2,1)S(1)}, u32[]{:S(2)}, u32[]{:S(2)}) collective-permute-start(bf16[2,64,256]{2,1,0:T(8,128)(2,1)S(1)} %get-tuple-element.18), channel_id=1, source_target_pairs={{0,8},{4,12},{8,0},{12,4},{1,9},{5,13},{9,1},{13,5},{2,10},{6,14},... | collective-permute-start | bytes 196616 | tf_op jit(solution)/shard_map/ppermute | solution.py:26
  21.3 1.4 %collective-permute-start.2 = (bf16[2,64,256]{2,1,0:T(8,128)(2,1)S(1)}, bf16[2,64,256]{2,1,0:T(8,128)(2,1)S(1)}, u32[]{:S(2)}, u32[]{:S(2)}) collective-permute-start(bf16[2,64,256]{2,1,0:T(8,128)(2,1)S(1)} %get-tuple-element.18), channel_id=1, source_target_pairs={{0,4},{4,0},{8,12},{12,8},{1,5},{5,1},{9,13},{13,9},{2,6},{6,2},{1... | collective-permute-start | bytes 196616 | tf_op jit(solution)/shard_map/ppermute | solution.py:26
  22.6 0.5 collective-permute-start.4
  23.1 6.8 %collective-permute-done.3 = bf16[2,64,256]{2,1,0:T(8,128)(2,1)S(1)} collective-permute-done((bf16[2,64,256]{2,1,0:T(8,128)(2,1)S(1)}, bf16[2,64,256]{2,1,0:T(8,128)(2,1)S(1)}, u32[]{:S(2)}, u32[]{:S(2)}) %collective-permute-start.3) | collective-permute-done | bytes 65568 | tf_op jit(solution)/shard_map/ppermute | solution.py:26
  29.9 0.0 collective-permute-done.2
  29.9 1.5 %collective-permute-done.4 = bf16[2,64,256]{2,1,0:T(8,128)(2,1)S(1)} collective-permute-done((bf16[2,64,256]{2,1,0:T(8,128)(2,1)S(1)}, bf16[2,64,256]{2,1,0:T(8,128)(2,1)S(1)}, u32[]{:S(2)}, u32[]{:S(2)}) %collective-permute-start.4) | collective-permute-done | bytes 65568 | tf_op jit(solution)/shard_map/ppermute | solution.py:26
  31.5 7.9 %collective-permute-start.7 = (bf16[4,2,64,256]{3,2,1,0:T(8,128)(2,1)S(1)}, bf16[4,2,64,256]{3,2,1,0:T(8,128)(2,1)S(1)}, u32[]{:S(2)}, u32[]{:S(2)}) collective-permute-start(bf16[4,2,64,256]{3,2,1,0:T(8,128)(2,1)S(1)} %pad_maximum_fusion.pieces0), channel_id=1, source_target_pairs={{0,192},{64,128},{128,64},{192,0},{1,193},{65,129},{129,65},{193,1... | collective-permute-start | bytes 786440 | tf_op jit(solution)/shard_map/ppermute | solution.py:26
  39.4 1.8 %collective-permute-start.6 = (bf16[4,2,64,256]{3,2,1,0:T(8,128)(2,1)S(1)}, bf16[4,2,64,256]{3,2,1,0:T(8,128)(2,1)S(1)}, u32[]{:S(2)}, u32[]{:S(2)}) collective-permute-start(bf16[4,2,64,256]{3,2,1,0:T(8,128)(2,1)S(1)} %pad_maximum_fusion.pieces0), channel_id=1, source_target_pairs={{0,128},{64,192},{128,0},{192,64},{1,129},{65,193},{129,1},{193,65... | collective-permute-start | bytes 786440 | tf_op jit(solution)/shard_map/ppermute | solution.py:26
  41.1 0.0 collective-permute-start.5
  41.1 0.1 stack.47.where
  41.2 9.9 %collective-permute-done.7.pieces3 = bf16[4,2,64,256]{3,2,1,0:T(8,128)(2,1)S(1)} collective-permute-done((bf16[4,2,64,256]{3,2,1,0:T(8,128)(2,1)S(1)}, bf16[4,2,64,256]{3,2,1,0:T(8,128)(2,1)S(1)}, u32[]{:S(2)}, u32[]{:S(2)}) %collective-permute-start.7) | collective-permute-done | bytes 262176 | tf_op jit(solution)/shard_map/ppermute | solution.py:26
  51.1 0.0 collective-permute-done.6.pieces2
  51.1 0.8 collective-permute-done.5.pieces1
  51.9 0.7 place.1.mine
  52.6 0.1 collective-permute-start.8
  52.7 2.6 %collective-permute-done.8.theirs = bf16[1024,512]{1,0:T(8,128)(2,1)S(1)} collective-permute-done((bf16[1024,512]{1,0:T(8,128)(2,1)S(1)}, bf16[1024,512]{1,0:T(8,128)(2,1)S(1)}, u32[]{:S(2)}, u32[]{:S(2)}) %collective-permute-start.8) | collective-permute-done | bytes 1048608 | tf_op jit(solution)/shard_map/ppermute | solution.py:187
  55.4 1.9 %join.1.density_in = bf16[8192,1024]{1,0:T(8,128)(2,1)} custom-call(s32[5]{0:T(128)S(1)} %stack.47.where, bf16[1024,512]{1,0:T(8,128)(2,1)S(1)} %place.1.mine, bf16[1024,512]{1,0:T(8,128)(2,1)S(1)} %collective-permute-done.8.theirs), custom_call_target="tpu_custom_call" | custom-call | bytes 4194304 | tf_op jit(solution)/shard_map/join/pallas_call | solution.py:178
  57.3 11.8 %all-to-all-done.parts = bf16[64,64,256]{2,1,0:T(8,128)(2,1)S(1)} async-done(((bf16[64,64,256]{2,1,0:T(8,128)(2,1)}), bf16[64,64,256]{2,1,0:T(8,128)(2,1)S(1)}, u32[]{:S(2)}, u32[]{:S(2)}) %all-to-all-start) | async-done | bytes 2097184 | tf_op jit(solution)/shard_map/all_to_all | solution.py:222
  69.1 4.3 %other.1 = (bf16[512,1024]{1,0:T(8,128)(2,1)S(1)}, bf16[1024,1024]{1,0:T(8,128)(2,1)S(1)}, bf16[1024,1024]{1,0:T(8,128)(2,1)S(1)}) custom-call(s32[5]{0:T(128)S(1)} %stack.47.where, bf16[64,64,256]{2,1,0:T(8,128)(2,1)S(1)} %all-to-all-done.parts, bf16[8192,1024]{1,0:T(8,128)(2,1)} %join.1.density_in), custom_call_target="tpu_custom_call" | custom-call | flops 2147483648 | bytes 8388608 | tf_op jit(solution)/shard_map/other/pallas_call | solution.py:224
  73.4 0.1 collective-permute-start.9
  73.5 2.9 %own.1 = f32[512,1024]{1,0:T(8,128)S(1)} custom-call(s32[5]{0:T(128)S(1)} %stack.47.where, bf16[1024,1024]{1,0:T(8,128)(2,1)S(1)} %get-tuple-element.14.screened, bf16[1024,1024]{1,0:T(8,128)(2,1)S(1)} %get-tuple-element.15.density), custom_call_target="tpu_custom_call" | custom-call | flops 2147483648 | bytes 6291456 | tf_op jit(solution)/shard_map/own/pallas_call | solution.py:235
  76.4 0.0 collective-permute-done.9
  76.4 0.3 add_convert_fusion
  76.7 27.1 %all_to_all.15 = bf16[16,32,1024]{2,1,0:T(8,128)(2,1)S(1)} all-to-all(bf16[16,32,1024]{2,1,0:T(8,128)(2,1)S(1)} %bitcast.15), channel_id=1, replica_groups=mesh['y'=4,'zl'=2,'c'=2,'x'=4,'zh'=4] {'x','y'}, dimensions={0} | all-to-all | bytes 2097152 | tf_op jit(solution)/shard_map/all_to_all | solution.py:246
  103.9 0.2 convert_reduce_fusion
  104.1 11.7 %all_to_all.16 = f32[8,4,1024]{2,1,0:T(4,128)S(1)} all-to-all(f32[8,4,1024]{2,1,0:T(4,128)S(1)} %reshape.7), channel_id=1, replica_groups=mesh['y'=4,'zl'=2,'c'=2,'x'=4,'zh'=4] {'zl','zh'}, dimensions={0} | all-to-all | bytes 262144 | tf_op jit(solution)/shard_map/all_to_all | solution.py:248
  115.8 0.6 reduce_sum.19
  (3 shorter events, 0.1 us)
Async XLA Ops:
  1.4 7.2 %collective-permute-start.1 = (bf16[64,256]{1,0:T(8,128)(2,1)}, bf16[64,256]{1,0:T(8,128)(2,1)S(1)}, u32[]{:S(2)}, u32[]{:S(2)}) collective-permute-start(bf16[64,256]{1,0:T(8,128)(2,1)} %block.1), channel_id=1, source_target_pairs={{0,1},{1,0},{2,3},{3,2},{32,33},{33,32},{34,35},{35,34},{64,67},{6... | collective-permute-start | bytes 98312 | tf_op jit(solution)/shard_map/ppermute | solution.py:158
  4.8 3.9 %collective-permute-start = (bf16[64,256]{1,0:T(8,128)(2,1)}, bf16[64,256]{1,0:T(8,128)(2,1)S(1)}, u32[]{:S(2)}, u32[]{:S(2)}) collective-permute-start(bf16[64,256]{1,0:T(8,128)(2,1)} %block.1), channel_id=1, source_target_pairs={{0,0},{1,1},{2,2},{3,3},{32,32},{33,33},{34,34},{35,35},{64,66},{6... | collective-permute-start | bytes 98312 | tf_op jit(solution)/shard_map/ppermute | solution.py:158
  8.7 60.4 %all-to-all-start = ((bf16[64,64,256]{2,1,0:T(8,128)(2,1)}), bf16[64,64,256]{2,1,0:T(8,128)(2,1)S(1)}, u32[]{:S(2)}, u32[]{:S(2)}) async-start(bf16[64,64,256]{2,1,0:T(8,128)(2,1)} %screen.1), calls=%async_computation | async-start | bytes 4194304 | tf_op jit(solution)/shard_map/all_to_all | solution.py:222
  18.9 11.0 %collective-permute-start.3 = (bf16[2,64,256]{2,1,0:T(8,128)(2,1)S(1)}, bf16[2,64,256]{2,1,0:T(8,128)(2,1)S(1)}, u32[]{:S(2)}, u32[]{:S(2)}) collective-permute-start(bf16[2,64,256]{2,1,0:T(8,128)(2,1)S(1)} %get-tuple-element.18), channel_id=1, source_target_pairs={{0,8},{4,12},{8,0},{12,4},{1,9},{5,13},{9,1},{13,5},{2,10},{6,14},... | collective-permute-start | bytes 196616 | tf_op jit(solution)/shard_map/ppermute | solution.py:26
  21.3 8.6 %collective-permute-start.2 = (bf16[2,64,256]{2,1,0:T(8,128)(2,1)S(1)}, bf16[2,64,256]{2,1,0:T(8,128)(2,1)S(1)}, u32[]{:S(2)}, u32[]{:S(2)}) collective-permute-start(bf16[2,64,256]{2,1,0:T(8,128)(2,1)S(1)} %get-tuple-element.18), channel_id=1, source_target_pairs={{0,4},{4,0},{8,12},{12,8},{1,5},{5,1},{9,13},{13,9},{2,6},{6,2},{1... | collective-permute-start | bytes 196616 | tf_op jit(solution)/shard_map/ppermute | solution.py:26
  22.6 8.8 %collective-permute-start.4 = (bf16[2,64,256]{2,1,0:T(8,128)(2,1)S(1)}, bf16[2,64,256]{2,1,0:T(8,128)(2,1)S(1)}, u32[]{:S(2)}, u32[]{:S(2)}) collective-permute-start(bf16[2,64,256]{2,1,0:T(8,128)(2,1)S(1)} %get-tuple-element.18), channel_id=1, source_target_pairs={{0,12},{4,8},{8,4},{12,0},{1,13},{5,9},{9,5},{13,1},{2,14},{6,10},... | collective-permute-start | bytes 196616 | tf_op jit(solution)/shard_map/ppermute | solution.py:26
  31.5 19.6 %collective-permute-start.7 = (bf16[4,2,64,256]{3,2,1,0:T(8,128)(2,1)S(1)}, bf16[4,2,64,256]{3,2,1,0:T(8,128)(2,1)S(1)}, u32[]{:S(2)}, u32[]{:S(2)}) collective-permute-start(bf16[4,2,64,256]{3,2,1,0:T(8,128)(2,1)S(1)} %pad_maximum_fusion.pieces0), channel_id=1, source_target_pairs={{0,192},{64,128},{128,64},{192,0},{1,193},{65,129},{129,65},{193,1... | collective-permute-start | bytes 786440 | tf_op jit(solution)/shard_map/ppermute | solution.py:26
  39.4 11.8 %collective-permute-start.6 = (bf16[4,2,64,256]{3,2,1,0:T(8,128)(2,1)S(1)}, bf16[4,2,64,256]{3,2,1,0:T(8,128)(2,1)S(1)}, u32[]{:S(2)}, u32[]{:S(2)}) collective-permute-start(bf16[4,2,64,256]{3,2,1,0:T(8,128)(2,1)S(1)} %pad_maximum_fusion.pieces0), channel_id=1, source_target_pairs={{0,128},{64,192},{128,0},{192,64},{1,129},{65,193},{129,1},{193,65... | collective-permute-start | bytes 786440 | tf_op jit(solution)/shard_map/ppermute | solution.py:26
  41.1 10.8 %collective-permute-start.5 = (bf16[4,2,64,256]{3,2,1,0:T(8,128)(2,1)S(1)}, bf16[4,2,64,256]{3,2,1,0:T(8,128)(2,1)S(1)}, u32[]{:S(2)}, u32[]{:S(2)}) collective-permute-start(bf16[4,2,64,256]{3,2,1,0:T(8,128)(2,1)S(1)} %pad_maximum_fusion.pieces0), channel_id=1, source_target_pairs={{0,64},{64,0},{128,192},{192,128},{1,65},{65,1},{129,193},{193,129... | collective-permute-start | bytes 786440 | tf_op jit(solution)/shard_map/ppermute | solution.py:26
  52.6 2.7 %collective-permute-start.8 = (bf16[1024,512]{1,0:T(8,128)(2,1)S(1)}, bf16[1024,512]{1,0:T(8,128)(2,1)S(1)}, u32[]{:S(2)}, u32[]{:S(2)}) collective-permute-start(bf16[1024,512]{1,0:T(8,128)(2,1)S(1)} %place.1.mine), channel_id=1, source_target_pairs={{0,16},{16,0},{1,17},{17,1},{2,18},{18,2},{3,19},{19,3},{4,20},{20... | collective-permute-start | bytes 3145736 | tf_op jit(solution)/shard_map/ppermute | solution.py:187
  73.4 3.0 %collective-permute-start.9 = (bf16[512,1024]{1,0:T(8,128)(2,1)S(1)}, bf16[512,1024]{1,0:T(8,128)(2,1)S(1)}, u32[]{:S(2)}, u32[]{:S(2)}) collective-permute-start(bf16[512,1024]{1,0:T(8,128)(2,1)S(1)} %get-tuple-element.16), channel_id=1, source_target_pairs={{0,16},{16,0},{1,17},{17,1},{2,18},{18,2},{3,19},{19,3},{4,20},{20... | collective-permute-start | bytes 3145736 | tf_op jit(solution)/shard_map/ppermute | solution.py:234

commit v3 on v2

--- a/solution.py
+++ b/solution.py
@@ -41,6 +41,11 @@
                 half[pl.ds(row, BW), pl.ds(col, 256)] = pieces[x_step, z_step]
 
 
+def pair_kernel(first, second, out):
+    out[0] = first[...]
+    out[1] = second[...]
+
+
 def join_kernel(where, mine, theirs, whole, sems):
     core = where[4]
     copies = [
@@ -63,30 +68,24 @@
     return row
 
 
-def block_kernel(mask, block, out, scalars, held, sems):
-    copies = [
-        pltpu.make_async_copy(mask, scalars, sems.at[0]),
-        pltpu.make_async_copy(block, held, sems.at[1]),
+def prepare_kernel(block_mask, block, mask, integrals, block_out, out, block_scalars, scalars, block_in, held, sems, out_sems):
+    small = [
+        pltpu.make_async_copy(block_mask, block_scalars, sems.at[0]),
+        pltpu.make_async_copy(block, block_in, sems.at[1]),
+        pltpu.make_async_copy(mask, scalars, sems.at[2]),
     ]
-    for copy in copies:
+    for copy in small:
         copy.start()
-    for copy in copies:
-        copy.wait()
-    row = scale_row([scalars[0, index] for index in range(4)])
-    out[...] = (held[...].astype(jnp.float32) * row).astype(jnp.bfloat16)
-
-
-def screen_kernel(mask, integrals, out, scalars, held, sems, out_sems):
     inward, outward = [], []
     for index in range(8):
         part = pl.ds(index * 8, 8)
-        inward.append(pltpu.make_async_copy(integrals.at[part], held.at[part], sems.at[index]))
+        inward.append(pltpu.make_async_copy(integrals.at[part], held.at[part], sems.at[3 + index]))
         outward.append(pltpu.make_async_copy(held.at[part], out.at[part], out_sems.at[index]))
-    first = pltpu.make_async_copy(mask, scalars, sems.at[8])
-    first.start()
-    for copy in inward:
-        copy.start()
-    first.wait()
+        inward[-1].start()
+    for copy in small:
+        copy.wait()
+    row = scale_row([block_scalars[0, index] for index in range(4)])
+    block_out[...] = (block_in[...].astype(jnp.float32) * row).astype(jnp.bfloat16)
     row = scale_row([scalars[0, 0, index] for index in range(4)]).astype(jnp.bfloat16)
     for index in range(8):
         part = pl.ds(index * 8, 8)
@@ -101,56 +100,50 @@
     for x in range(4):
         for y in range(4):
             for zl in range(2):
-                low = pl.multiple_of((y * 4 + zl * 2 + core) * BW + x * 16, 16)
                 to = ((x * 4 + y) * 2 + zl) * 16
-                rows[to : to + 16, :] = screened[pl.ds(low, 16), :]
+                rows[to : to + 16, :] = screened[y, zl * 2 + core, x * 16 : (x + 1) * 16, :]
 
 
 def contract_rows(rows, density, contracted, half):
-    contracted[:, half] = jnp.dot(rows[...], density[:, half], preferred_element_type=jnp.float32).astype(
-        jnp.bfloat16
-    )
+    columns = slice(half * 512, (half + 1) * 512)
+    contracted[:, columns] = jnp.dot(
+        rows[...], density[:, columns], preferred_element_type=jnp.float32
+    ).astype(jnp.bfloat16)
 
 
 def exchange_rows(contracted, screened, half):
-    return lax.dot_general(contracted[...], screened[half, :], NT, preferred_element_type=jnp.float32)
-
-
-HALVES = (slice(0, 512), slice(512, 1024))
+    several = screened[half * 2 : half * 2 + 2].reshape(512, NA)
+    return lax.dot_general(contracted[...], several, NT, preferred_element_type=jnp.float32)
 
 
 def first_kernel(where, parts, density_in, out, screened, density, rows, contracted, sems):
-    fetch = [
-        pltpu.make_async_copy(
-            density_in.at[pl.ds(0, NA), pl.ds(half * 512, 512)],
-            density.at[:, pl.ds(half * 512, 512)],
-            sems.at[half],
+    me = where[4]
+    fetch = []
+    for half in range(2):
+        columns = pl.ds(half * 512, 512)
+        fetch.append(
+            pltpu.make_async_copy(density_in.at[pl.ds(0, NA), columns], density.at[:, columns], sems.at[half])
         )
-        for half in range(2)
-    ]
-    for copy in fetch:
-        copy.start()
-    for x in range(4):
-        for zh in range(4):
-            low = (x * 4 + zh) * BW
-            for zl in range(2):
-                for core in range(2):
-                    left = (core * 2 + zl) * 256
-                    screened[low : low + BW, left : left + 256] = parts[((x * 2 + core) * 4 + zh) * 2 + zl]
-    pick_rows(1 - where[4], screened, rows)
-    for copy, half in zip(fetch, HALVES):
-        copy.wait()
+        fetch[half].start()
+    for source in range(2):
+        for z in range(2):
+            left = (source * 2 + z) * 256
+            for zh in range(4):
+                screened[:, zh, :, left : left + 256] = parts[:, source, zh, z]
+    pick_rows(1 - me, screened, rows)
+    for half in range(2):
+        fetch[half].wait()
         contract_rows(rows, density, contracted, half)
-    for half in HALVES:
-        out[:, half] = exchange_rows(contracted, screened, half).astype(jnp.bfloat16)
+    for half in range(2):
+        out[:, half * 512 : (half + 1) * 512] = exchange_rows(contracted, screened, half).astype(jnp.bfloat16)
 
 
 def second_kernel(where, screened, density, out, rows, contracted):
     pick_rows(where[4], screened, rows)
-    for half in HALVES:
+    for half in range(2):
         contract_rows(rows, density, contracted, half)
-    for half in HALVES:
-        out[:, half] = exchange_rows(contracted, screened, half)
+    for half in range(2):
+        out[:, half * 512 : (half + 1) * 512] = exchange_rows(contracted, screened, half)
 
 
 def gather_z(block):
@@ -165,7 +158,16 @@
 
 
 def gather(where, two):
-    plane = jnp.stack(from_four(jnp.stack(two), "x"))
+    pair = pl.pallas_call(
+        pair_kernel,
+        out_shape=shape(2, BW, 256),
+        in_specs=[VMEM] * 2,
+        out_specs=VMEM,
+        compiler_params=PARAMS,
+        cost_estimate=pl.CostEstimate(flops=2**35, bytes_accessed=2**17, transcendentals=0),
+        name="pair",
+    )(*two)
+    plane = jnp.stack(from_four(pair, "x"))
     half = pl.pallas_call(
         place_kernel,
         out_shape=shape(NA, 512),
@@ -189,48 +191,36 @@
 
 def body(integrals, integral_mask, density, density_mask):
     where = jnp.stack([lax.axis_index(name) for name in ("y", "x", "zh", "zl", "c")]).astype(jnp.int32)
-    block = pl.pallas_call(
-        block_kernel,
-        out_shape=shape(BW, 256),
-        in_specs=[HBM] * 2,
-        out_specs=VMEM,
+    block, screened = pl.pallas_call(
+        prepare_kernel,
+        out_shape=(shape(BW, 256), shape(64, 64, 256)),
+        in_specs=[HBM] * 4,
+        out_specs=(VMEM, HBM),
         scratch_shapes=[
             pltpu.SMEM((1, 4), jnp.int32),
+            pltpu.SMEM((1, 1, 4), jnp.int32),
             pltpu.VMEM((BW, 256), jnp.bfloat16),
-            pltpu.SemaphoreType.DMA((2,)),
-        ],
-        compiler_params=ALONE,
-        name="block",
-    )(density_mask.T, density.T)
-    screened = pl.pallas_call(
-        screen_kernel,
-        out_shape=shape(64, 64, 256),
-        in_specs=[HBM] * 2,
-        out_specs=HBM,
-        scratch_shapes=[
-            pltpu.SMEM((1, 1, 4), jnp.int32),
             pltpu.VMEM((64, 64, 256), jnp.bfloat16),
-            pltpu.SemaphoreType.DMA((9,)),
+            pltpu.SemaphoreType.DMA((11,)),
             pltpu.SemaphoreType.DMA((8,)),
         ],
         compiler_params=ALONE,
         cost_estimate=pl.CostEstimate(flops=0, bytes_accessed=4 * 2**20, transcendentals=0),
-        name="screen",
-    )(integral_mask, integrals)
+        name="prepare",
+    )(density_mask.T, density.T, integral_mask, integrals)
     two = gather_z(block)
-    screened, two = lax.optimization_barrier((screened, two))
     parts = lax.all_to_all(screened, PLANE, split_axis=0, concat_axis=0, tiled=True)
     whole = gather(where, two)
     other_half, screened, whole = pl.pallas_call(
         first_kernel,
-        out_shape=(shape(NA // 2, NA), shape(NA, NA), shape(NA, NA)),
+        out_shape=(shape(NA // 2, NA), shape(4, 4, BW, NA), shape(NA, NA)),
         in_specs=[SMEM, VMEM, HBM],
         out_specs=(VMEM, VMEM, VMEM),
         scratch_shapes=[pltpu.VMEM((NA // 2, NA), jnp.bfloat16)] * 2 + [pltpu.SemaphoreType.DMA((2,))],
         compiler_params=WIDE,
         cost_estimate=pl.CostEstimate(flops=2**31, bytes_accessed=8 * 2**20, transcendentals=0),
         name="other",
-    )(where, parts, whole)
+    )(where, parts.reshape(4, 2, 4, 2, BW, 256), whole)
     arrived = lax.ppermute(other_half, "c", SWAP)
     own_half = pl.pallas_call(
         second_kernel,

time: 118 us -> 117 us (level)
  starting transfers between devices: 29 us -> 27.5 us
  waiting for transfers between devices: 33.5 us -> 34.9 us
    all_to_all x1, waiting for transfers between devices: 11.8 us -> 13.5 us  [body(): lax.all_to_all(screened, PLANE, split_axis=0, concat_axis=0, tiled=True)]
    ppermute x6, starting transfers between devices: 13.8 us -> 12.3 us  [from_four(): lax.ppermute(one, axis, [(i, i ^ j) for i in range(4)])]
  transfers between devices with their start and end apart: 11 -> 11, of which waited for: 6 -> 5; matrix products, arithmetic and copies ran while one was open for 0% -> 0% of each run, Pallas kernels for 7% -> 5%
where the time goes in v3:
time: 117 us; the launch traced here: 115 us
  blocking collectives  38.1 us (33%)
  waiting for transfers between devices  34.9 us (30%)
  starting transfers between devices  27.5 us (24%)
  Pallas kernels  12.9 us (11%)
  other arithmetic  1.21 us (1%)
    all_to_all x1, blocking collectives, body(): lax.all_to_all(term, ('x', 'y'), split_axis=0, concat_axis=0, tiled=True)  26.5 us
    ppermute x6, waiting for transfers between devices, from_four(): lax.ppermute(one, axis, [(i, i ^ j) for i in range(4)])  18.8 us
    all_to_all x1, waiting for transfers between devices, body(): lax.all_to_all(screened, PLANE, split_axis=0, concat_axis=0, tiled=True)  13.5 us
    ppermute x6, starting transfers between devices, from_four(): lax.ppermute(one, axis, [(i, i ^ j) for i in range(4)])  12.3 us
    all_to_all x1, blocking collectives, body(): lax.all_to_all(column, ('zl', 'zh'), split_axis=0, concat_axis=0, tiled=T...  11.7 us
    all_to_all x1, starting transfers between devices, body(): lax.all_to_all(screened, PLANE, split_axis=0, concat_axis=0, tiled=True)  10.2 us
    ppermute x2, starting transfers between devices, gather_z(): lax.ppermute(block, ('y', 'zl', 'zh'), [(y * 8 + z, y * 8 + (z ^ y * 2 +...  4.76 us
    pallas_call x1, Pallas kernels, body(): pl.pallas_call(first_kernel, out_shape=(shape(NA // 2, NA), shape(4, 4, B...  4.29 us
  transfers between devices with their start and end apart: 11, of which 5 were waited for; matrix products, arithmetic and copies ran while one was open for 0% of the time, Pallas kernels for 5%

profile of v3, /device:TPU:2, one launch (start us, length us, event | category | flops | bytes accessed | tf_op | source)
XLA Modules:
  0.0 115.0 jit_solution(5437762679996821730)
XLA Ops:
  0.0 3.1 %prepare.1 = (bf16[64,256]{1,0:T(8,128)(2,1)}, bf16[64,64,256]{2,1,0:T(8,128)(2,1)}) custom-call(s32[1,4]{1,0:T(1,128)} %bitcast.20, bf16[64,256]{1,0:T(8,128)(2,1)} %bitcast.19, s32[1,1,4]{2,1,0:T(1,128)} %mask.1, bf16[64,64,256]{2,1,0:T(8,128)(2,1)} %integrals.1), custom_call_target="tpu_custom_call" | custom-call | bytes 4194304 | tf_op jit(solution)/shard_map/prepare/pallas_call | solution.py:194
  3.1 3.4 %collective-permute-start.1 = (bf16[64,256]{1,0:T(8,128)(2,1)}, bf16[64,256]{1,0:T(8,128)(2,1)S(1)}, u32[]{:S(2)}, u32[]{:S(2)}) collective-permute-start(bf16[64,256]{1,0:T(8,128)(2,1)} %get-tuple-element.11), channel_id=1, source_target_pairs={{0,1},{1,0},{2,3},{3,2},{32,33},{33,32},{34,35},{35,34},{64,67},{6... | collective-permute-start | bytes 98312 | tf_op jit(solution)/shard_map/ppermute | solution.py:151
  6.5 1.4 %collective-permute-start = (bf16[64,256]{1,0:T(8,128)(2,1)}, bf16[64,256]{1,0:T(8,128)(2,1)S(1)}, u32[]{:S(2)}, u32[]{:S(2)}) collective-permute-start(bf16[64,256]{1,0:T(8,128)(2,1)} %get-tuple-element.11), channel_id=1, source_target_pairs={{0,0},{1,1},{2,2},{3,3},{32,32},{33,33},{34,34},{35,35},{64,66},{6... | collective-permute-start | bytes 98312 | tf_op jit(solution)/shard_map/ppermute | solution.py:151
  7.9 10.2 %all-to-all-start = ((bf16[64,64,256]{2,1,0:T(8,128)(2,1)}), bf16[64,64,256]{2,1,0:T(8,128)(2,1)S(1)}, u32[]{:S(2)}, u32[]{:S(2)}) async-start(bf16[64,64,256]{2,1,0:T(8,128)(2,1)} %get-tuple-element.10), calls=%async_computation | async-start | bytes 4194304 | tf_op jit(solution)/shard_map/all_to_all | solution.py:212
  18.1 0.0 collective-permute-done.1.second
  18.1 0.0 collective-permute-done.first
  18.1 1.6 %collective-permute-start.4 = (bf16[2,64,256]{2,1,0:T(8,128)(2,1)S(1)}, bf16[2,64,256]{2,1,0:T(8,128)(2,1)S(1)}, u32[]{:S(2)}, u32[]{:S(2)}) collective-permute-start(bf16[2,64,256]{2,1,0:T(8,128)(2,1)S(1)} %pair.1), channel_id=1, source_target_pairs={{0,12},{4,8},{8,4},{12,0},{1,13},{5,9},{9,5},{13,1},{2,14},{6,10},... | collective-permute-start | bytes 196616 | tf_op jit(solution)/shard_map/ppermute | solution.py:26
  19.8 1.0 collective-permute-start.3
  20.8 1.6 %collective-permute-start.2 = (bf16[2,64,256]{2,1,0:T(8,128)(2,1)S(1)}, bf16[2,64,256]{2,1,0:T(8,128)(2,1)S(1)}, u32[]{:S(2)}, u32[]{:S(2)}) collective-permute-start(bf16[2,64,256]{2,1,0:T(8,128)(2,1)S(1)} %pair.1), channel_id=1, source_target_pairs={{0,4},{4,0},{8,12},{12,8},{1,5},{5,1},{9,13},{13,9},{2,6},{6,2},{1... | collective-permute-start | bytes 196616 | tf_op jit(solution)/shard_map/ppermute | solution.py:26
  22.3 7.4 %collective-permute-done.4 = bf16[2,64,256]{2,1,0:T(8,128)(2,1)S(1)} collective-permute-done((bf16[2,64,256]{2,1,0:T(8,128)(2,1)S(1)}, bf16[2,64,256]{2,1,0:T(8,128)(2,1)S(1)}, u32[]{:S(2)}, u32[]{:S(2)}) %collective-permute-start.4) | collective-permute-done | bytes 65568 | tf_op jit(solution)/shard_map/ppermute | solution.py:26
  29.7 0.0 collective-permute-done.3
  29.7 0.0 collective-permute-done.2
  29.8 7.2 %collective-permute-start.7 = (bf16[4,2,64,256]{3,2,1,0:T(8,128)(2,1)S(1)}, bf16[4,2,64,256]{3,2,1,0:T(8,128)(2,1)S(1)}, u32[]{:S(2)}, u32[]{:S(2)}) collective-permute-start(bf16[4,2,64,256]{3,2,1,0:T(8,128)(2,1)S(1)} %pad_maximum_fusion.pieces0), channel_id=1, source_target_pairs={{0,192},{64,128},{128,64},{192,0},{1,193},{65,129},{129,65},{193,1... | collective-permute-start | bytes 786440 | tf_op jit(solution)/shard_map/ppermute | solution.py:26
  37.0 0.6 collective-permute-start.6
  37.6 0.3 collective-permute-start.5
  37.9 0.1 stack.38.where
  38.0 10.6 %collective-permute-done.7.pieces3 = bf16[4,2,64,256]{3,2,1,0:T(8,128)(2,1)S(1)} collective-permute-done((bf16[4,2,64,256]{3,2,1,0:T(8,128)(2,1)S(1)}, bf16[4,2,64,256]{3,2,1,0:T(8,128)(2,1)S(1)}, u32[]{:S(2)}, u32[]{:S(2)}) %collective-permute-start.7) | collective-permute-done | bytes 262176 | tf_op jit(solution)/shard_map/ppermute | solution.py:26
  48.6 0.0 collective-permute-done.6.pieces2
  48.6 0.7 collective-permute-done.5.pieces1
  49.4 0.7 place.1.mine
  50.1 0.1 collective-permute-start.8
  50.2 2.6 %collective-permute-done.8.theirs = bf16[1024,512]{1,0:T(8,128)(2,1)S(1)} collective-permute-done((bf16[1024,512]{1,0:T(8,128)(2,1)S(1)}, bf16[1024,512]{1,0:T(8,128)(2,1)S(1)}, u32[]{:S(2)}, u32[]{:S(2)}) %collective-permute-start.8) | collective-permute-done | bytes 1048608 | tf_op jit(solution)/shard_map/ppermute | solution.py:189
  52.8 1.9 %join.1.density_in = bf16[8192,1024]{1,0:T(8,128)(2,1)} custom-call(s32[5]{0:T(128)S(1)} %stack.38.where, bf16[1024,512]{1,0:T(8,128)(2,1)S(1)} %place.1.mine, bf16[1024,512]{1,0:T(8,128)(2,1)S(1)} %collective-permute-done.8.theirs), custom_call_target="tpu_custom_call" | custom-call | bytes 4194304 | tf_op jit(solution)/shard_map/join/pallas_call | solution.py:180
  54.8 13.5 %all-to-all-done = bf16[64,64,256]{2,1,0:T(8,128)(2,1)S(1)} async-done(((bf16[64,64,256]{2,1,0:T(8,128)(2,1)}), bf16[64,64,256]{2,1,0:T(8,128)(2,1)S(1)}, u32[]{:S(2)}, u32[]{:S(2)}) %all-to-all-start) | async-done | bytes 2097184 | tf_op jit(solution)/shard_map/all_to_all | solution.py:212
  68.3 4.3 %other.1 = (bf16[512,1024]{1,0:T(8,128)(2,1)S(1)}, bf16[4,4,64,1024]{3,2,1,0:T(8,128)(2,1)S(1)}, bf16[1024,1024]{1,0:T(8,128)(2,1)S(1)}) custom-call(s32[5]{0:T(128)S(1)} %stack.38.where, bf16[4,2,4,2,64,256]{5,4,3,2,1,0:T(8,128)(2,1)S(1)} %bitcast.13, bf16[8192,1024]{1,0:T(8,128)(2,1)} %join.1.density_in), custom_call_target="tpu_custom_call" | custom-call | flops 2147483648 | bytes 8388608 | tf_op jit(solution)/shard_map/other/pallas_call | solution.py:214
  72.6 0.1 collective-permute-start.9
  72.7 2.9 %own.1 = f32[512,1024]{1,0:T(8,128)S(1)} custom-call(s32[5]{0:T(128)S(1)} %stack.38.where, bf16[4,4,64,1024]{3,2,1,0:T(8,128)(2,1)S(1)} %get-tuple-element.12.screened, bf16[1024,1024]{1,0:T(8,128)(2,1)S(1)} %get-tuple-element.13.density), custom_call_target="tpu_custom_call" | custom-call | flops 2147483648 | bytes 6291456 | tf_op jit(solution)/shard_map/own/pallas_call | solution.py:225
  75.6 0.0 collective-permute-done.9
  75.6 0.3 add_convert_fusion
  75.9 26.5 %all_to_all.15 = bf16[16,32,1024]{2,1,0:T(8,128)(2,1)S(1)} all-to-all(bf16[16,32,1024]{2,1,0:T(8,128)(2,1)S(1)} %bitcast.15), channel_id=1, replica_groups=mesh['y'=4,'zl'=2,'c'=2,'x'=4,'zh'=4] {'x','y'}, dimensions={0} | all-to-all | bytes 2097152 | tf_op jit(solution)/shard_map/all_to_all | solution.py:236
  102.4 0.2 convert_reduce_fusion
  102.6 11.7 %all_to_all.16 = f32[8,4,1024]{2,1,0:T(4,128)S(1)} all-to-all(f32[8,4,1024]{2,1,0:T(4,128)S(1)} %reshape.11), channel_id=1, replica_groups=mesh['y'=4,'zl'=2,'c'=2,'x'=4,'zh'=4] {'zl','zh'}, dimensions={0} | all-to-all | bytes 262144 | tf_op jit(solution)/shard_map/all_to_all | solution.py:238
  114.3 0.6 reduce_sum.19
  (3 shorter events, 0.1 us)
Async XLA Ops:
  3.1 15.0 %collective-permute-start.1 = (bf16[64,256]{1,0:T(8,128)(2,1)}, bf16[64,256]{1,0:T(8,128)(2,1)S(1)}, u32[]{:S(2)}, u32[]{:S(2)}) collective-permute-start(bf16[64,256]{1,0:T(8,128)(2,1)} %get-tuple-element.11), channel_id=1, source_target_pairs={{0,1},{1,0},{2,3},{3,2},{32,33},{33,32},{34,35},{35,34},{64,67},{6... | collective-permute-start | bytes 98312 | tf_op jit(solution)/shard_map/ppermute | solution.py:151
  6.5 11.7 %collective-permute-start = (bf16[64,256]{1,0:T(8,128)(2,1)}, bf16[64,256]{1,0:T(8,128)(2,1)S(1)}, u32[]{:S(2)}, u32[]{:S(2)}) collective-permute-start(bf16[64,256]{1,0:T(8,128)(2,1)} %get-tuple-element.11), channel_id=1, source_target_pairs={{0,0},{1,1},{2,2},{3,3},{32,32},{33,33},{34,34},{35,35},{64,66},{6... | collective-permute-start | bytes 98312 | tf_op jit(solution)/shard_map/ppermute | solution.py:151
  7.9 60.4 %all-to-all-start = ((bf16[64,64,256]{2,1,0:T(8,128)(2,1)}), bf16[64,64,256]{2,1,0:T(8,128)(2,1)S(1)}, u32[]{:S(2)}, u32[]{:S(2)}) async-start(bf16[64,64,256]{2,1,0:T(8,128)(2,1)} %get-tuple-element.10), calls=%async_computation | async-start | bytes 4194304 | tf_op jit(solution)/shard_map/all_to_all | solution.py:212
  18.1 11.6 %collective-permute-start.4 = (bf16[2,64,256]{2,1,0:T(8,128)(2,1)S(1)}, bf16[2,64,256]{2,1,0:T(8,128)(2,1)S(1)}, u32[]{:S(2)}, u32[]{:S(2)}) collective-permute-start(bf16[2,64,256]{2,1,0:T(8,128)(2,1)S(1)} %pair.1), channel_id=1, source_target_pairs={{0,12},{4,8},{8,4},{12,0},{1,13},{5,9},{9,5},{13,1},{2,14},{6,10},... | collective-permute-start | bytes 196616 | tf_op jit(solution)/shard_map/ppermute | solution.py:26
  19.8 10.0 %collective-permute-start.3 = (bf16[2,64,256]{2,1,0:T(8,128)(2,1)S(1)}, bf16[2,64,256]{2,1,0:T(8,128)(2,1)S(1)}, u32[]{:S(2)}, u32[]{:S(2)}) collective-permute-start(bf16[2,64,256]{2,1,0:T(8,128)(2,1)S(1)} %pair.1), channel_id=1, source_target_pairs={{0,8},{4,12},{8,0},{12,4},{1,9},{5,13},{9,1},{13,5},{2,10},{6,14},... | collective-permute-start | bytes 196616 | tf_op jit(solution)/shard_map/ppermute | solution.py:26
  20.8 9.0 %collective-permute-start.2 = (bf16[2,64,256]{2,1,0:T(8,128)(2,1)S(1)}, bf16[2,64,256]{2,1,0:T(8,128)(2,1)S(1)}, u32[]{:S(2)}, u32[]{:S(2)}) collective-permute-start(bf16[2,64,256]{2,1,0:T(8,128)(2,1)S(1)} %pair.1), channel_id=1, source_target_pairs={{0,4},{4,0},{8,12},{12,8},{1,5},{5,1},{9,13},{13,9},{2,6},{6,2},{1... | collective-permute-start | bytes 196616 | tf_op jit(solution)/shard_map/ppermute | solution.py:26
  29.8 18.9 %collective-permute-start.7 = (bf16[4,2,64,256]{3,2,1,0:T(8,128)(2,1)S(1)}, bf16[4,2,64,256]{3,2,1,0:T(8,128)(2,1)S(1)}, u32[]{:S(2)}, u32[]{:S(2)}) collective-permute-start(bf16[4,2,64,256]{3,2,1,0:T(8,128)(2,1)S(1)} %pad_maximum_fusion.pieces0), channel_id=1, source_target_pairs={{0,192},{64,128},{128,64},{192,0},{1,193},{65,129},{129,65},{193,1... | collective-permute-start | bytes 786440 | tf_op jit(solution)/shard_map/ppermute | solution.py:26
  37.0 11.7 %collective-permute-start.6 = (bf16[4,2,64,256]{3,2,1,0:T(8,128)(2,1)S(1)}, bf16[4,2,64,256]{3,2,1,0:T(8,128)(2,1)S(1)}, u32[]{:S(2)}, u32[]{:S(2)}) collective-permute-start(bf16[4,2,64,256]{3,2,1,0:T(8,128)(2,1)S(1)} %pad_maximum_fusion.pieces0), channel_id=1, source_target_pairs={{0,128},{64,192},{128,0},{192,64},{1,129},{65,193},{129,1},{193,65... | collective-permute-start | bytes 786440 | tf_op jit(solution)/shard_map/ppermute | solution.py:26
  37.6 11.8 %collective-permute-start.5 = (bf16[4,2,64,256]{3,2,1,0:T(8,128)(2,1)S(1)}, bf16[4,2,64,256]{3,2,1,0:T(8,128)(2,1)S(1)}, u32[]{:S(2)}, u32[]{:S(2)}) collective-permute-start(bf16[4,2,64,256]{3,2,1,0:T(8,128)(2,1)S(1)} %pad_maximum_fusion.pieces0), channel_id=1, source_target_pairs={{0,64},{64,0},{128,192},{192,128},{1,65},{65,1},{129,193},{193,129... | collective-permute-start | bytes 786440 | tf_op jit(solution)/shard_map/ppermute | solution.py:26
  50.1 2.7 %collective-permute-start.8 = (bf16[1024,512]{1,0:T(8,128)(2,1)S(1)}, bf16[1024,512]{1,0:T(8,128)(2,1)S(1)}, u32[]{:S(2)}, u32[]{:S(2)}) collective-permute-start(bf16[1024,512]{1,0:T(8,128)(2,1)S(1)} %place.1.mine), channel_id=1, source_target_pairs={{0,16},{16,0},{1,17},{17,1},{2,18},{18,2},{3,19},{19,3},{4,20},{20... | collective-permute-start | bytes 3145736 | tf_op jit(solution)/shard_map/ppermute | solution.py:189
  72.6 3.0 %collective-permute-start.9 = (bf16[512,1024]{1,0:T(8,128)(2,1)S(1)}, bf16[512,1024]{1,0:T(8,128)(2,1)S(1)}, u32[]{:S(2)}, u32[]{:S(2)}) collective-permute-start(bf16[512,1024]{1,0:T(8,128)(2,1)S(1)} %get-tuple-element.14), channel_id=1, source_target_pairs={{0,16},{16,0},{1,17},{17,1},{2,18},{18,2},{3,19},{19,3},{4,20},{20... | collective-permute-start | bytes 3145736 | tf_op jit(solution)/shard_map/ppermute | solution.py:224

commit v4 on v3

--- a/solution.py
+++ b/solution.py
@@ -10,11 +10,12 @@
 PLANE = ("x", "c", "zh", "zl")
 NT = (((1,), (1,)), ((), ()))
 SWAP = [(0, 1), (1, 0)]
+STEPS = (2, 1, 3, 0)
 VMEM = pl.BlockSpec(memory_space=pltpu.VMEM)
 HBM = pl.BlockSpec(memory_space=pltpu.HBM)
 SMEM = pl.BlockSpec(memory_space=pltpu.SMEM)
 PARAMS = pltpu.CompilerParams(vmem_limit_bytes=40 * 2**20)
-WIDE = pltpu.CompilerParams(vmem_limit_bytes=46 * 2**20)
+WIDE = pltpu.CompilerParams(vmem_limit_bytes=42 * 2**20)
 ALONE = pltpu.CompilerParams(vmem_limit_bytes=59 * 2**20)
 
 
@@ -96,12 +97,11 @@
         copy.wait()
 
 
-def pick_rows(core, screened, rows):
-    for x in range(4):
-        for y in range(4):
-            for zl in range(2):
-                to = ((x * 4 + y) * 2 + zl) * 16
-                rows[to : to + 16, :] = screened[y, zl * 2 + core, x * 16 : (x + 1) * 16, :]
+def pick_rows(where, core, screened, rows):
+    for index, step in enumerate(STEPS):
+        for zl in range(2):
+            to = (index * 2 + zl) * BW
+            rows[to : to + BW, :] = screened[lax.bitwise_xor(where[0], step), zl * 2 + core]
 
 
 def contract_rows(rows, density, contracted, half):
@@ -116,34 +116,53 @@
     return lax.dot_general(contracted[...], several, NT, preferred_element_type=jnp.float32)
 
 
-def first_kernel(where, parts, density_in, out, screened, density, rows, contracted, sems):
-    me = where[4]
+def first_kernel(where, parts, density_in, out, screened, density, contracted, rows, sems):
     fetch = []
     for half in range(2):
         columns = pl.ds(half * 512, 512)
-        fetch.append(
-            pltpu.make_async_copy(density_in.at[pl.ds(0, NA), columns], density.at[:, columns], sems.at[half])
-        )
-        fetch[half].start()
+        for part in range(4):
+            low = pl.ds(part * 256, 256)
+            fetch.append(
+                pltpu.make_async_copy(
+                    density_in.at[low, columns], density.at[low, columns], sems.at[half * 4 + part]
+                )
+            )
+            fetch[-1].start()
     for source in range(2):
         for z in range(2):
             left = (source * 2 + z) * 256
             for zh in range(4):
                 screened[:, zh, :, left : left + 256] = parts[:, source, zh, z]
-    pick_rows(1 - me, screened, rows)
-    for half in range(2):
-        fetch[half].wait()
+    pick_rows(where, 1 - where[4], screened, rows)
+    for half in range(2):
+        for copy in fetch[half * 4 : half * 4 + 4]:
+            copy.wait()
         contract_rows(rows, density, contracted, half)
     for half in range(2):
-        out[:, half * 512 : (half + 1) * 512] = exchange_rows(contracted, screened, half).astype(jnp.bfloat16)
-
-
-def second_kernel(where, screened, density, out, rows, contracted):
-    pick_rows(where[4], screened, rows)
+        out[:, half * 512 : (half + 1) * 512] = exchange_rows(contracted.at[:256], screened, half)
+
+
+def second_kernel(where, screened, density, contracted, rows):
+    pick_rows(where, where[4], screened, rows)
     for half in range(2):
         contract_rows(rows, density, contracted, half)
+
+
+def rest_kernel(contracted, screened, out):
     for half in range(2):
         out[:, half * 512 : (half + 1) * 512] = exchange_rows(contracted, screened, half)
+
+
+def add_kernel(first, second, third, out):
+    out[...] = first[...] + second[...].astype(jnp.float32) + third[...].astype(jnp.float32)
+
+
+def third_kernel(contracted, screened, arrived, out_a, out_b):
+    for half in range(2):
+        columns = slice(half * 512, (half + 1) * 512)
+        got = exchange_rows(contracted, screened, half) + arrived[:, columns]
+        out_a[:, columns] = got[:128].astype(out_a.dtype)
+        out_b[:, columns] = got[128:].astype(out_b.dtype)
 
 
 def gather_z(block):
@@ -211,32 +230,80 @@
     two = gather_z(block)
     parts = lax.all_to_all(screened, PLANE, split_axis=0, concat_axis=0, tiled=True)
     whole = gather(where, two)
-    other_half, screened, whole = pl.pallas_call(
+    near_out, screened, whole, far_rows = pl.pallas_call(
         first_kernel,
-        out_shape=(shape(NA // 2, NA), shape(4, 4, BW, NA), shape(NA, NA)),
+        out_shape=(shape(256, NA, dtype=jnp.float32), shape(4, 4, BW, NA), shape(NA, NA), shape(512, NA)),
         in_specs=[SMEM, VMEM, HBM],
-        out_specs=(VMEM, VMEM, VMEM),
-        scratch_shapes=[pltpu.VMEM((NA // 2, NA), jnp.bfloat16)] * 2 + [pltpu.SemaphoreType.DMA((2,))],
+        out_specs=(VMEM,) * 4,
+        scratch_shapes=[pltpu.VMEM((512, NA), jnp.bfloat16), pltpu.SemaphoreType.DMA((8,))],
         compiler_params=WIDE,
-        cost_estimate=pl.CostEstimate(flops=2**31, bytes_accessed=8 * 2**20, transcendentals=0),
-        name="other",
+        cost_estimate=pl.CostEstimate(flops=3 * 2**29, bytes_accessed=8 * 2**20, transcendentals=0),
+        name="first",
     )(where, parts.reshape(4, 2, 4, 2, BW, 256), whole)
-    arrived = lax.ppermute(other_half, "c", SWAP)
-    own_half = pl.pallas_call(
+    arrived = lax.ppermute(near_out, "c", SWAP)
+    contracted = pl.pallas_call(
         second_kernel,
-        out_shape=shape(NA // 2, NA, dtype=jnp.float32),
+        out_shape=shape(512, NA),
         in_specs=[SMEM] + [VMEM] * 2,
         out_specs=VMEM,
-        scratch_shapes=[pltpu.VMEM((NA // 2, NA), jnp.bfloat16)] * 2,
-        compiler_params=PARAMS,
-        cost_estimate=pl.CostEstimate(flops=2**31, bytes_accessed=6 * 2**20, transcendentals=0),
+        scratch_shapes=[pltpu.VMEM((512, NA), jnp.bfloat16)],
+        compiler_params=PARAMS,
+        cost_estimate=pl.CostEstimate(flops=2**30, bytes_accessed=5 * 2**20, transcendentals=0),
         name="own",
     )(where, screened, whole)
-    term = (own_half + arrived.astype(jnp.float32)).astype(jnp.bfloat16).reshape(16, 32, NA)
-    layers = lax.all_to_all(term, ("x", "y"), split_axis=0, concat_axis=0, tiled=True)
-    column = jnp.sum(layers.astype(jnp.float32), axis=0).reshape(8, 4, NA)
-    terms = lax.all_to_all(column, ("zl", "zh"), split_axis=0, concat_axis=0, tiled=True)
-    return jnp.sum(terms, axis=0)
+    half_rows = [pl.BlockSpec((256, NA), lambda i, half=half: (half, 0)) for half in range(2)]
+    everything = pl.BlockSpec((4, 4, BW, NA), lambda i: (0, 0, 0, 0))
+    near = pl.pallas_call(
+        third_kernel,
+        out_shape=(shape(128, NA),) * 2,
+        grid=(1,),
+        in_specs=[half_rows[0], everything, half_rows[0]],
+        out_specs=(VMEM,) * 2,
+        compiler_params=PARAMS,
+        cost_estimate=pl.CostEstimate(flops=2**29, bytes_accessed=4 * 2**20, transcendentals=0),
+        name="near",
+    )(contracted, screened, arrived)
+    far_rows, near = lax.optimization_barrier((far_rows, near))
+    arrived = lax.ppermute(
+        pl.pallas_call(
+            rest_kernel,
+            out_shape=shape(256, NA, dtype=jnp.float32),
+            grid=(1,),
+            in_specs=[half_rows[1], everything],
+            out_specs=half_rows[0],
+            compiler_params=PARAMS,
+            cost_estimate=pl.CostEstimate(flops=2**29, bytes_accessed=4 * 2**20, transcendentals=0),
+            name="rest",
+        )(far_rows, screened),
+        "c",
+        SWAP,
+    )
+    far, own = pl.pallas_call(
+        third_kernel,
+        out_shape=(shape(128, NA), shape(128, NA, dtype=jnp.float32)),
+        grid=(1,),
+        in_specs=[half_rows[1], everything, half_rows[0]],
+        out_specs=(VMEM,) * 2,
+        compiler_params=PARAMS,
+        cost_estimate=pl.CostEstimate(flops=2**29, bytes_accessed=4 * 2**20, transcendentals=0),
+        name="far",
+    )(contracted, screened, arrived)
+    sent = [
+        lax.ppermute(quarter, "y", [(i, i ^ step) for i in range(4)])
+        for step, quarter in zip(STEPS, (near[0], near[1], far))
+    ]
+    total = pl.pallas_call(
+        add_kernel,
+        out_shape=shape(128, NA, dtype=jnp.float32),
+        in_specs=[VMEM] * 3,
+        out_specs=VMEM,
+        compiler_params=PARAMS,
+        cost_estimate=pl.CostEstimate(flops=2**35, bytes_accessed=2**21, transcendentals=0),
+        name="add",
+    )(own, sent[0], sent[1])
+    term = (total + sent[2].astype(jnp.float32)).astype(jnp.bfloat16).reshape(32, 4, NA)
+    terms = lax.all_to_all(term, ("zl", "x", "zh"), split_axis=0, concat_axis=0, tiled=True)
+    return jnp.sum(terms.astype(jnp.float32), axis=0)
 
 
 def solution(mesh):

time: 117 us -> 117 us (level)
  blocking collectives: 38.1 us -> 17.7 us
  waiting for transfers between devices: 34.9 us -> 45.5 us
  starting transfers between devices: 27.5 us -> 37.4 us
    all_to_all x2 -> x1, blocking collectives: 38.1 us -> 17.7 us  [body(): lax.all_to_all(term, ('zl', 'x', 'zh'), split_axis=0, concat_axis=0, tile...]
    ppermute x1 -> x5, waiting for transfers between devices: 0.01 us -> 10.6 us  [the longest x3 9.72 us: body(): lax.ppermute(quarter, 'y', [(i, i ^ step) for i in range(4)])]
    ppermute x1 -> x5, starting transfers between devices: 0.09 us -> 10 us  [the longest x3 9.71 us: body(): lax.ppermute(quarter, 'y', [(i, i ^ step) for i in range(4)])]
    pallas_call x2 -> x6, Pallas kernels: 7.17 us -> 7.85 us  [the longest x1 3.77 us: body(): pl.pallas_call(first_kernel, out_shape=(shape(256, NA, dtype=jnp.float32)...]
  transfers between devices with their start and end apart: 11 -> 15, of which waited for: 5 -> 8; matrix products, arithmetic and copies ran while one was open for 0% -> 0% of each run, Pallas kernels for 5% -> 5%
where the time goes in v4:
time: 117 us; the launch traced here: 115 us
  waiting for transfers between devices  45.5 us (39%)
  starting transfers between devices  37.4 us (32%)
  blocking collectives  17.7 us (15%)
  Pallas kernels  13.6 us (12%)
    ppermute x6, waiting for transfers between devices, from_four(): lax.ppermute(one, axis, [(i, i ^ j) for i in range(4)])  18.8 us
    all_to_all x1, blocking collectives, body(): lax.all_to_all(term, ('zl', 'x', 'zh'), split_axis=0, concat_axis=0, tile...  17.7 us
    all_to_all x1, waiting for transfers between devices, body(): lax.all_to_all(screened, PLANE, split_axis=0, concat_axis=0, tiled=True)  13.5 us
    ppermute x6, starting transfers between devices, from_four(): lax.ppermute(one, axis, [(i, i ^ j) for i in range(4)])  12.3 us
    all_to_all x1, starting transfers between devices, body(): lax.all_to_all(screened, PLANE, split_axis=0, concat_axis=0, tiled=True)  10.2 us
    ppermute x3, waiting for transfers between devices, body(): lax.ppermute(quarter, 'y', [(i, i ^ step) for i in range(4)])  9.72 us
    ppermute x3, starting transfers between devices, body(): lax.ppermute(quarter, 'y', [(i, i ^ step) for i in range(4)])  9.71 us
    ppermute x2, starting transfers between devices, gather_z(): lax.ppermute(block, ('y', 'zl', 'zh'), [(y * 8 + z, y * 8 + (z ^ y * 2 +...  4.76 us
  transfers between devices with their start and end apart: 15, of which 8 were waited for; matrix products, arithmetic and copies ran while one was open for 0% of the time, Pallas kernels for 5%

profile of v4, /device:TPU:2, one launch (start us, length us, event | category | flops | bytes accessed | tf_op | source)
XLA Modules:
  0.0 115.4 jit_solution(3141832009948571341)
XLA Ops:
  0.0 3.1 %prepare.1 = (bf16[64,256]{1,0:T(8,128)(2,1)}, bf16[64,64,256]{2,1,0:T(8,128)(2,1)}) custom-call(s32[1,4]{1,0:T(1,128)} %bitcast.18, bf16[64,256]{1,0:T(8,128)(2,1)} %bitcast.17, s32[1,1,4]{2,1,0:T(1,128)} %mask.1, bf16[64,64,256]{2,1,0:T(8,128)(2,1)} %integrals.1), custom_call_target="tpu_custom_call" | custom-call | bytes 4194304 | tf_op jit(solution)/shard_map/prepare/pallas_call | solution.py:213
  3.1 3.4 %collective-permute-start.1 = (bf16[64,256]{1,0:T(8,128)(2,1)}, bf16[64,256]{1,0:T(8,128)(2,1)S(1)}, u32[]{:S(2)}, u32[]{:S(2)}) collective-permute-start(bf16[64,256]{1,0:T(8,128)(2,1)} %get-tuple-element.19), channel_id=1, source_target_pairs={{0,1},{1,0},{2,3},{3,2},{32,33},{33,32},{34,35},{35,34},{64,67},{6... | collective-permute-start | bytes 98312 | tf_op jit(solution)/shard_map/ppermute | solution.py:170
  6.5 1.4 %collective-permute-start = (bf16[64,256]{1,0:T(8,128)(2,1)}, bf16[64,256]{1,0:T(8,128)(2,1)S(1)}, u32[]{:S(2)}, u32[]{:S(2)}) collective-permute-start(bf16[64,256]{1,0:T(8,128)(2,1)} %get-tuple-element.19), channel_id=1, source_target_pairs={{0,0},{1,1},{2,2},{3,3},{32,32},{33,33},{34,34},{35,35},{64,66},{6... | collective-permute-start | bytes 98312 | tf_op jit(solution)/shard_map/ppermute | solution.py:170
  7.9 10.2 %all-to-all-start = ((bf16[64,64,256]{2,1,0:T(8,128)(2,1)}), bf16[64,64,256]{2,1,0:T(8,128)(2,1)S(1)}, u32[]{:S(2)}, u32[]{:S(2)}) async-start(bf16[64,64,256]{2,1,0:T(8,128)(2,1)} %get-tuple-element.18), calls=%async_computation | async-start | bytes 4194304 | tf_op jit(solution)/shard_map/all_to_all | solution.py:231
  18.1 0.0 collective-permute-done.1.second
  18.1 0.0 collective-permute-done.first
  18.1 1.6 %collective-permute-start.4 = (bf16[2,64,256]{2,1,0:T(8,128)(2,1)S(1)}, bf16[2,64,256]{2,1,0:T(8,128)(2,1)S(1)}, u32[]{:S(2)}, u32[]{:S(2)}) collective-permute-start(bf16[2,64,256]{2,1,0:T(8,128)(2,1)S(1)} %pair.1), channel_id=1, source_target_pairs={{0,12},{4,8},{8,4},{12,0},{1,13},{5,9},{9,5},{13,1},{2,14},{6,10},... | collective-permute-start | bytes 196616 | tf_op jit(solution)/shard_map/ppermute | solution.py:27
  19.8 1.0 collective-permute-start.3
  20.7 1.6 %collective-permute-start.2 = (bf16[2,64,256]{2,1,0:T(8,128)(2,1)S(1)}, bf16[2,64,256]{2,1,0:T(8,128)(2,1)S(1)}, u32[]{:S(2)}, u32[]{:S(2)}) collective-permute-start(bf16[2,64,256]{2,1,0:T(8,128)(2,1)S(1)} %pair.1), channel_id=1, source_target_pairs={{0,4},{4,0},{8,12},{12,8},{1,5},{5,1},{9,13},{13,9},{2,6},{6,2},{1... | collective-permute-start | bytes 196616 | tf_op jit(solution)/shard_map/ppermute | solution.py:27
  22.3 7.4 %collective-permute-done.4 = bf16[2,64,256]{2,1,0:T(8,128)(2,1)S(1)} collective-permute-done((bf16[2,64,256]{2,1,0:T(8,128)(2,1)S(1)}, bf16[2,64,256]{2,1,0:T(8,128)(2,1)S(1)}, u32[]{:S(2)}, u32[]{:S(2)}) %collective-permute-start.4) | collective-permute-done | bytes 65568 | tf_op jit(solution)/shard_map/ppermute | solution.py:27
  29.7 0.0 collective-permute-done.3
  29.7 0.0 collective-permute-done.2
  29.8 7.2 %collective-permute-start.7 = (bf16[4,2,64,256]{3,2,1,0:T(8,128)(2,1)S(1)}, bf16[4,2,64,256]{3,2,1,0:T(8,128)(2,1)S(1)}, u32[]{:S(2)}, u32[]{:S(2)}) collective-permute-start(bf16[4,2,64,256]{3,2,1,0:T(8,128)(2,1)S(1)} %pad_maximum_fusion.pieces0), channel_id=1, source_target_pairs={{0,192},{64,128},{128,64},{192,0},{1,193},{65,129},{129,65},{193,1... | collective-permute-start | bytes 786440 | tf_op jit(solution)/shard_map/ppermute | solution.py:27
  37.0 0.6 collective-permute-start.6
  37.6 0.3 collective-permute-start.5
  37.9 0.1 stack.38.where
  38.0 10.6 %collective-permute-done.7.pieces3 = bf16[4,2,64,256]{3,2,1,0:T(8,128)(2,1)S(1)} collective-permute-done((bf16[4,2,64,256]{3,2,1,0:T(8,128)(2,1)S(1)}, bf16[4,2,64,256]{3,2,1,0:T(8,128)(2,1)S(1)}, u32[]{:S(2)}, u32[]{:S(2)}) %collective-permute-start.7) | collective-permute-done | bytes 262176 | tf_op jit(solution)/shard_map/ppermute | solution.py:27
  48.6 0.0 collective-permute-done.6.pieces2
  48.6 0.7 collective-permute-done.5.pieces1
  49.4 0.7 place.1.mine
  50.1 0.1 collective-permute-start.8
  50.2 2.6 %collective-permute-done.8.theirs = bf16[1024,512]{1,0:T(8,128)(2,1)S(1)} collective-permute-done((bf16[1024,512]{1,0:T(8,128)(2,1)S(1)}, bf16[1024,512]{1,0:T(8,128)(2,1)S(1)}, u32[]{:S(2)}, u32[]{:S(2)}) %collective-permute-start.8) | collective-permute-done | bytes 1048608 | tf_op jit(solution)/shard_map/ppermute | solution.py:208
  52.8 1.9 %join.1.density_in = bf16[8192,1024]{1,0:T(8,128)(2,1)} custom-call(s32[5]{0:T(128)S(1)} %stack.38.where, bf16[1024,512]{1,0:T(8,128)(2,1)S(1)} %place.1.mine, bf16[1024,512]{1,0:T(8,128)(2,1)S(1)} %collective-permute-done.8.theirs), custom_call_target="tpu_custom_call" | custom-call | bytes 4194304 | tf_op jit(solution)/shard_map/join/pallas_call | solution.py:199
  54.8 13.5 %all-to-all-done = bf16[64,64,256]{2,1,0:T(8,128)(2,1)S(1)} async-done(((bf16[64,64,256]{2,1,0:T(8,128)(2,1)}), bf16[64,64,256]{2,1,0:T(8,128)(2,1)S(1)}, u32[]{:S(2)}, u32[]{:S(2)}) %all-to-all-start) | async-done | bytes 2097184 | tf_op jit(solution)/shard_map/all_to_all | solution.py:231
  68.3 3.8 %first.1 = (f32[256,1024]{1,0:T(8,128)S(1)}, bf16[4,4,64,1024]{3,2,1,0:T(8,128)(2,1)S(1)}, bf16[1024,1024]{1,0:T(8,128)(2,1)S(1)}, bf16[512,1024]{1,0:T(8,128)(2,1)S(1)}) custom-call(s32[5]{0:T(128)S(1)} %stack.38.where, bf16[4,2,4,2,64,256]{5,4,3,2,1,0:T(8,128)(2,1)S(1)} %bitcast.12, bf16[8192,1024]{1,0:T(8,128)(2,1)} %join.1.density_in), custom_call_target="tpu_custom_call" | custom-call | flops 1610612736 | bytes 8388608 | tf_op jit(solution)/shard_map/first/pallas_call | solution.py:233
  72.1 0.1 collective-permute-start.9
  72.2 1.8 %own.1.contracted = bf16[512,1024]{1,0:T(8,128)(2,1)S(1)} custom-call(s32[5]{0:T(128)S(1)} %stack.38.where, bf16[4,4,64,1024]{3,2,1,0:T(8,128)(2,1)S(1)} %get-tuple-element.20.screened, bf16[1024,1024]{1,0:T(8,128)(2,1)S(1)} %get-tuple-element.21.density), custom_call_target="tpu_custom_call" | custom-call | flops 1073741824 | bytes 5242880 | tf_op jit(solution)/shard_map/own/pallas_call | solution.py:244
  73.9 0.9 collective-permute-done.9.arrived
  74.8 0.7 near.1
  75.5 0.7 rest.1
  76.3 0.2 collective-permute-start.10
  76.5 4.7 %collective-permute-start.11 = (bf16[128,1024]{1,0:T(8,128)(2,1)S(1)}, bf16[128,1024]{1,0:T(8,128)(2,1)S(1)}, u32[]{:S(2)}, u32[]{:S(2)}) collective-permute-start(bf16[128,1024]{1,0:T(8,128)(2,1)S(1)} %get-tuple-element.28), channel_id=1, source_target_pairs={{0,128},{64,192},{128,0},{192,64},{1,129},{65,193},{129,1},{193,65... | collective-permute-start | bytes 786440 | tf_op jit(solution)/shard_map/ppermute | solution.py:292
  81.3 3.2 %collective-permute-start.12 = (bf16[128,1024]{1,0:T(8,128)(2,1)S(1)}, bf16[128,1024]{1,0:T(8,128)(2,1)S(1)}, u32[]{:S(2)}, u32[]{:S(2)}) collective-permute-start(bf16[128,1024]{1,0:T(8,128)(2,1)S(1)} %get-tuple-element.29), channel_id=1, source_target_pairs={{0,64},{64,0},{128,192},{192,128},{1,65},{65,1},{129,193},{193,129... | collective-permute-start | bytes 786440 | tf_op jit(solution)/shard_map/ppermute | solution.py:292
  84.5 0.0 collective-permute-done.10.arrived
  84.5 0.7 far.1
  85.2 1.7 %collective-permute-start.13 = (bf16[128,1024]{1,0:T(8,128)(2,1)S(1)}, bf16[128,1024]{1,0:T(8,128)(2,1)S(1)}, u32[]{:S(2)}, u32[]{:S(2)}) collective-permute-start(bf16[128,1024]{1,0:T(8,128)(2,1)S(1)} %get-tuple-element.30), channel_id=1, source_target_pairs={{0,192},{64,128},{128,64},{192,0},{1,193},{65,129},{129,65},{193,1... | collective-permute-start | bytes 786440 | tf_op jit(solution)/shard_map/ppermute | solution.py:292
  87.0 1.4 %collective-permute-done.11.second = bf16[128,1024]{1,0:T(8,128)(2,1)S(1)} collective-permute-done((bf16[128,1024]{1,0:T(8,128)(2,1)S(1)}, bf16[128,1024]{1,0:T(8,128)(2,1)S(1)}, u32[]{:S(2)}, u32[]{:S(2)}) %collective-permute-start.11) | collective-permute-done | bytes 262176 | tf_op jit(solution)/shard_map/ppermute | solution.py:292
  88.4 8.3 %collective-permute-done.12.third = bf16[128,1024]{1,0:T(8,128)(2,1)S(1)} collective-permute-done((bf16[128,1024]{1,0:T(8,128)(2,1)S(1)}, bf16[128,1024]{1,0:T(8,128)(2,1)S(1)}, u32[]{:S(2)}, u32[]{:S(2)}) %collective-permute-start.12) | collective-permute-done | bytes 262176 | tf_op jit(solution)/shard_map/ppermute | solution.py:292
  96.7 0.1 add.6
  96.8 0.0 collective-permute-done.13
  96.8 0.1 add_convert_fusion
  96.8 0.1 reshape.7
  97.0 17.7 %all_to_all.10 = bf16[32,4,1024]{2,1,0:T(4,128)(2,1)S(1)} all-to-all(bf16[32,4,1024]{2,1,0:T(4,128)(2,1)S(1)} %reshape.7), channel_id=1, replica_groups=mesh['y'=4,'zl'=2,'c'=2,'x'=4,'zh'=4] {'zl','x','zh'}, dimensions={0} | all-to-all | bytes 524288 | tf_op jit(solution)/shard_map/all_to_all | solution.py:305
  114.7 0.7 convert_reduce_fusion
  (2 shorter events, 0.0 us)
Async XLA Ops:
  3.1 15.0 %collective-permute-start.1 = (bf16[64,256]{1,0:T(8,128)(2,1)}, bf16[64,256]{1,0:T(8,128)(2,1)S(1)}, u32[]{:S(2)}, u32[]{:S(2)}) collective-permute-start(bf16[64,256]{1,0:T(8,128)(2,1)} %get-tuple-element.19), channel_id=1, source_target_pairs={{0,1},{1,0},{2,3},{3,2},{32,33},{33,32},{34,35},{35,34},{64,67},{6... | collective-permute-start | bytes 98312 | tf_op jit(solution)/shard_map/ppermute | solution.py:170
  6.5 11.7 %collective-permute-start = (bf16[64,256]{1,0:T(8,128)(2,1)}, bf16[64,256]{1,0:T(8,128)(2,1)S(1)}, u32[]{:S(2)}, u32[]{:S(2)}) collective-permute-start(bf16[64,256]{1,0:T(8,128)(2,1)} %get-tuple-element.19), channel_id=1, source_target_pairs={{0,0},{1,1},{2,2},{3,3},{32,32},{33,33},{34,34},{35,35},{64,66},{6... | collective-permute-start | bytes 98312 | tf_op jit(solution)/shard_map/ppermute | solution.py:170
  7.9 60.4 %all-to-all-start = ((bf16[64,64,256]{2,1,0:T(8,128)(2,1)}), bf16[64,64,256]{2,1,0:T(8,128)(2,1)S(1)}, u32[]{:S(2)}, u32[]{:S(2)}) async-start(bf16[64,64,256]{2,1,0:T(8,128)(2,1)} %get-tuple-element.18), calls=%async_computation | async-start | bytes 4194304 | tf_op jit(solution)/shard_map/all_to_all | solution.py:231
  18.1 11.6 %collective-permute-start.4 = (bf16[2,64,256]{2,1,0:T(8,128)(2,1)S(1)}, bf16[2,64,256]{2,1,0:T(8,128)(2,1)S(1)}, u32[]{:S(2)}, u32[]{:S(2)}) collective-permute-start(bf16[2,64,256]{2,1,0:T(8,128)(2,1)S(1)} %pair.1), channel_id=1, source_target_pairs={{0,12},{4,8},{8,4},{12,0},{1,13},{5,9},{9,5},{13,1},{2,14},{6,10},... | collective-permute-start | bytes 196616 | tf_op jit(solution)/shard_map/ppermute | solution.py:27
  19.8 10.0 %collective-permute-start.3 = (bf16[2,64,256]{2,1,0:T(8,128)(2,1)S(1)}, bf16[2,64,256]{2,1,0:T(8,128)(2,1)S(1)}, u32[]{:S(2)}, u32[]{:S(2)}) collective-permute-start(bf16[2,64,256]{2,1,0:T(8,128)(2,1)S(1)} %pair.1), channel_id=1, source_target_pairs={{0,8},{4,12},{8,0},{12,4},{1,9},{5,13},{9,1},{13,5},{2,10},{6,14},... | collective-permute-start | bytes 196616 | tf_op jit(solution)/shard_map/ppermute | solution.py:27
  20.7 9.0 %collective-permute-start.2 = (bf16[2,64,256]{2,1,0:T(8,128)(2,1)S(1)}, bf16[2,64,256]{2,1,0:T(8,128)(2,1)S(1)}, u32[]{:S(2)}, u32[]{:S(2)}) collective-permute-start(bf16[2,64,256]{2,1,0:T(8,128)(2,1)S(1)} %pair.1), channel_id=1, source_target_pairs={{0,4},{4,0},{8,12},{12,8},{1,5},{5,1},{9,13},{13,9},{2,6},{6,2},{1... | collective-permute-start | bytes 196616 | tf_op jit(solution)/shard_map/ppermute | solution.py:27
  29.8 18.9 %collective-permute-start.7 = (bf16[4,2,64,256]{3,2,1,0:T(8,128)(2,1)S(1)}, bf16[4,2,64,256]{3,2,1,0:T(8,128)(2,1)S(1)}, u32[]{:S(2)}, u32[]{:S(2)}) collective-permute-start(bf16[4,2,64,256]{3,2,1,0:T(8,128)(2,1)S(1)} %pad_maximum_fusion.pieces0), channel_id=1, source_target_pairs={{0,192},{64,128},{128,64},{192,0},{1,193},{65,129},{129,65},{193,1... | collective-permute-start | bytes 786440 | tf_op jit(solution)/shard_map/ppermute | solution.py:27
  37.0 11.7 %collective-permute-start.6 = (bf16[4,2,64,256]{3,2,1,0:T(8,128)(2,1)S(1)}, bf16[4,2,64,256]{3,2,1,0:T(8,128)(2,1)S(1)}, u32[]{:S(2)}, u32[]{:S(2)}) collective-permute-start(bf16[4,2,64,256]{3,2,1,0:T(8,128)(2,1)S(1)} %pad_maximum_fusion.pieces0), channel_id=1, source_target_pairs={{0,128},{64,192},{128,0},{192,64},{1,129},{65,193},{129,1},{193,65... | collective-permute-start | bytes 786440 | tf_op jit(solution)/shard_map/ppermute | solution.py:27
  37.6 11.8 %collective-permute-start.5 = (bf16[4,2,64,256]{3,2,1,0:T(8,128)(2,1)S(1)}, bf16[4,2,64,256]{3,2,1,0:T(8,128)(2,1)S(1)}, u32[]{:S(2)}, u32[]{:S(2)}) collective-permute-start(bf16[4,2,64,256]{3,2,1,0:T(8,128)(2,1)S(1)} %pad_maximum_fusion.pieces0), channel_id=1, source_target_pairs={{0,64},{64,0},{128,192},{192,128},{1,65},{65,1},{129,193},{193,129... | collective-permute-start | bytes 786440 | tf_op jit(solution)/shard_map/ppermute | solution.py:27
  50.1 2.7 %collective-permute-start.8 = (bf16[1024,512]{1,0:T(8,128)(2,1)S(1)}, bf16[1024,512]{1,0:T(8,128)(2,1)S(1)}, u32[]{:S(2)}, u32[]{:S(2)}) collective-permute-start(bf16[1024,512]{1,0:T(8,128)(2,1)S(1)} %place.1.mine), channel_id=1, source_target_pairs={{0,16},{16,0},{1,17},{17,1},{2,18},{18,2},{3,19},{19,3},{4,20},{20... | collective-permute-start | bytes 3145736 | tf_op jit(solution)/shard_map/ppermute | solution.py:208
  72.1 2.7 %collective-permute-start.9 = (f32[256,1024]{1,0:T(8,128)S(1)}, f32[256,1024]{1,0:T(8,128)S(1)}, u32[]{:S(2)}, u32[]{:S(2)}) collective-permute-start(f32[256,1024]{1,0:T(8,128)S(1)} %get-tuple-element.23), channel_id=1, source_target_pairs={{0,16},{16,0},{1,17},{17,1},{2,18},{18,2},{3,19},{19,3},{4,20},{20... | collective-permute-start | bytes 3145736 | tf_op jit(solution)/shard_map/ppermute | solution.py:243
  76.3 8.2 %collective-permute-start.10 = (f32[256,1024]{1,0:T(8,128)S(1)}, f32[256,1024]{1,0:T(8,128)S(1)}, u32[]{:S(2)}, u32[]{:S(2)}) collective-permute-start(f32[256,1024]{1,0:T(8,128)S(1)} %rest.1), channel_id=1, source_target_pairs={{0,16},{16,0},{1,17},{17,1},{2,18},{18,2},{3,19},{19,3},{4,20},{20... | collective-permute-start | bytes 3145736 | tf_op jit(solution)/shard_map/ppermute | solution.py:267
  76.5 11.9 %collective-permute-start.11 = (bf16[128,1024]{1,0:T(8,128)(2,1)S(1)}, bf16[128,1024]{1,0:T(8,128)(2,1)S(1)}, u32[]{:S(2)}, u32[]{:S(2)}) collective-permute-start(bf16[128,1024]{1,0:T(8,128)(2,1)S(1)} %get-tuple-element.28), channel_id=1, source_target_pairs={{0,128},{64,192},{128,0},{192,64},{1,129},{65,193},{129,1},{193,65... | collective-permute-start | bytes 786440 | tf_op jit(solution)/shard_map/ppermute | solution.py:292
  81.3 15.4 %collective-permute-start.12 = (bf16[128,1024]{1,0:T(8,128)(2,1)S(1)}, bf16[128,1024]{1,0:T(8,128)(2,1)S(1)}, u32[]{:S(2)}, u32[]{:S(2)}) collective-permute-start(bf16[128,1024]{1,0:T(8,128)(2,1)S(1)} %get-tuple-element.29), channel_id=1, source_target_pairs={{0,64},{64,0},{128,192},{192,128},{1,65},{65,1},{129,193},{193,129... | collective-permute-start | bytes 786440 | tf_op jit(solution)/shard_map/ppermute | solution.py:292
  85.2 11.5 %collective-permute-start.13 = (bf16[128,1024]{1,0:T(8,128)(2,1)S(1)}, bf16[128,1024]{1,0:T(8,128)(2,1)S(1)}, u32[]{:S(2)}, u32[]{:S(2)}) collective-permute-start(bf16[128,1024]{1,0:T(8,128)(2,1)S(1)} %get-tuple-element.30), channel_id=1, source_target_pairs={{0,192},{64,128},{128,64},{192,0},{1,193},{65,129},{129,65},{193,1... | collective-permute-start | bytes 786440 | tf_op jit(solution)/shard_map/ppermute | solution.py:292

commit v5 on v4

--- a/solution.py
+++ b/solution.py
@@ -10,7 +10,7 @@
 PLANE = ("x", "c", "zh", "zl")
 NT = (((1,), (1,)), ((), ()))
 SWAP = [(0, 1), (1, 0)]
-STEPS = (2, 1, 3, 0)
+STEPS = (1, 3, 2, 0)
 VMEM = pl.BlockSpec(memory_space=pltpu.VMEM)
 HBM = pl.BlockSpec(memory_space=pltpu.HBM)
 SMEM = pl.BlockSpec(memory_space=pltpu.SMEM)
@@ -116,7 +116,7 @@
     return lax.dot_general(contracted[...], several, NT, preferred_element_type=jnp.float32)
 
 
-def first_kernel(where, parts, density_in, out, screened, density, contracted, rows, sems):
+def first_kernel(where, parts, density_in, near, far, screened, density, rows, contracted, sems):
     fetch = []
     for half in range(2):
         columns = pl.ds(half * 512, 512)
@@ -139,18 +139,16 @@
             copy.wait()
         contract_rows(rows, density, contracted, half)
     for half in range(2):
-        out[:, half * 512 : (half + 1) * 512] = exchange_rows(contracted.at[:256], screened, half)
+        columns = slice(half * 512, (half + 1) * 512)
+        got = exchange_rows(contracted, screened, half)
+        near[:, columns] = got[:256]
+        far[:, columns] = got[256:]
 
 
 def second_kernel(where, screened, density, contracted, rows):
     pick_rows(where, where[4], screened, rows)
     for half in range(2):
         contract_rows(rows, density, contracted, half)
-
-
-def rest_kernel(contracted, screened, out):
-    for half in range(2):
-        out[:, half * 512 : (half + 1) * 512] = exchange_rows(contracted, screened, half)
 
 
 def add_kernel(first, second, third, out):
@@ -230,17 +228,18 @@
     two = gather_z(block)
     parts = lax.all_to_all(screened, PLANE, split_axis=0, concat_axis=0, tiled=True)
     whole = gather(where, two)
-    near_out, screened, whole, far_rows = pl.pallas_call(
+    f32 = jnp.float32
+    near, far, screened, whole = pl.pallas_call(
         first_kernel,
-        out_shape=(shape(256, NA, dtype=jnp.float32), shape(4, 4, BW, NA), shape(NA, NA), shape(512, NA)),
+        out_shape=(shape(256, NA, dtype=f32), shape(256, NA, dtype=f32), shape(4, 4, BW, NA), shape(NA, NA)),
         in_specs=[SMEM, VMEM, HBM],
         out_specs=(VMEM,) * 4,
-        scratch_shapes=[pltpu.VMEM((512, NA), jnp.bfloat16), pltpu.SemaphoreType.DMA((8,))],
+        scratch_shapes=[pltpu.VMEM((512, NA), jnp.bfloat16)] * 2 + [pltpu.SemaphoreType.DMA((8,))],
         compiler_params=WIDE,
-        cost_estimate=pl.CostEstimate(flops=3 * 2**29, bytes_accessed=8 * 2**20, transcendentals=0),
+        cost_estimate=pl.CostEstimate(flops=2**31, bytes_accessed=8 * 2**20, transcendentals=0),
         name="first",
     )(where, parts.reshape(4, 2, 4, 2, BW, 256), whole)
-    arrived = lax.ppermute(near_out, "c", SWAP)
+    arrived = [lax.ppermute(one, "c", SWAP) for one in (near, far)]
     contracted = pl.pallas_call(
         second_kernel,
         out_shape=shape(512, NA),
@@ -262,22 +261,8 @@
         compiler_params=PARAMS,
         cost_estimate=pl.CostEstimate(flops=2**29, bytes_accessed=4 * 2**20, transcendentals=0),
         name="near",
-    )(contracted, screened, arrived)
-    far_rows, near = lax.optimization_barrier((far_rows, near))
-    arrived = lax.ppermute(
-        pl.pallas_call(
-            rest_kernel,
-            out_shape=shape(256, NA, dtype=jnp.float32),
-            grid=(1,),
-            in_specs=[half_rows[1], everything],
-            out_specs=half_rows[0],
-            compiler_params=PARAMS,
-            cost_estimate=pl.CostEstimate(flops=2**29, bytes_accessed=4 * 2**20, transcendentals=0),
-            name="rest",
-        )(far_rows, screened),
-        "c",
-        SWAP,
-    )
+    )(contracted, screened, arrived[0])
+    contracted, near = lax.optimization_barrier((contracted, near))
     far, own = pl.pallas_call(
         third_kernel,
         out_shape=(shape(128, NA), shape(128, NA, dtype=jnp.float32)),
@@ -287,7 +272,7 @@
         compiler_params=PARAMS,
         cost_estimate=pl.CostEstimate(flops=2**29, bytes_accessed=4 * 2**20, transcendentals=0),
         name="far",
-    )(contracted, screened, arrived)
+    )(contracted, screened, arrived[1])
     sent = [
         lax.ppermute(quarter, "y", [(i, i ^ step) for i in range(4)])
         for step, quarter in zip(STEPS, (near[0], near[1], far))

time: 117 us -> 115 us (0.983); the launches traced: 115 us -> 115 us
    ppermute x3, waiting for transfers between devices: 9.72 us -> 11.1 us  [body(): lax.ppermute(quarter, 'y', [(i, i ^ step) for i in range(4)])]
    pallas_call x2 -> x1, Pallas kernels: 4.51 us -> 4.31 us  [body(): pl.pallas_call(first_kernel, out_shape=(shape(256, NA, dtype=f32), shape(...]
  transfers between devices with their start and end apart: 15 -> 15, of which waited for: 8 -> 9; matrix products, arithmetic and copies ran while one was open for 0% -> 0% of each run, Pallas kernels for 5% -> 5%
where the time goes in v5:
time: 115 us
  waiting for transfers between devices  46.3 us (40%)
  starting transfers between devices  36.7 us (32%)
  blocking collectives  17.3 us (15%)
  Pallas kernels  13.4 us (12%)
    ppermute x6, waiting for transfers between devices, from_four(): lax.ppermute(one, axis, [(i, i ^ j) for i in range(4)])  18.8 us
    all_to_all x1, blocking collectives, body(): lax.all_to_all(term, ('zl', 'x', 'zh'), split_axis=0, concat_axis=0, tile...  17.3 us
    all_to_all x1, waiting for transfers between devices, body(): lax.all_to_all(screened, PLANE, split_axis=0, concat_axis=0, tiled=True)  13.5 us
    ppermute x6, starting transfers between devices, from_four(): lax.ppermute(one, axis, [(i, i ^ j) for i in range(4)])  12.3 us
    ppermute x3, waiting for transfers between devices, body(): lax.ppermute(quarter, 'y', [(i, i ^ step) for i in range(4)])  11.1 us
    all_to_all x1, starting transfers between devices, body(): lax.all_to_all(screened, PLANE, split_axis=0, concat_axis=0, tiled=True)  10.2 us
    ppermute x3, starting transfers between devices, body(): lax.ppermute(quarter, 'y', [(i, i ^ step) for i in range(4)])  8.74 us
    ppermute x2, starting transfers between devices, gather_z(): lax.ppermute(block, ('y', 'zl', 'zh'), [(y * 8 + z, y * 8 + (z ^ y * 2 +...  4.76 us
  transfers between devices with their start and end apart: 15, of which 9 were waited for; matrix products, arithmetic and copies ran while one was open for 0% of the time, Pallas kernels for 5%

profile of v5, /device:TPU:2, one launch (start us, length us, event | category | flops | bytes accessed | tf_op | source)
XLA Modules:
  0.0 114.9 jit_solution(13080596625135862521)
XLA Ops:
  0.0 3.1 %prepare.1 = (bf16[64,256]{1,0:T(8,128)(2,1)}, bf16[64,64,256]{2,1,0:T(8,128)(2,1)}) custom-call(s32[1,4]{1,0:T(1,128)} %bitcast.18, bf16[64,256]{1,0:T(8,128)(2,1)} %bitcast.17, s32[1,1,4]{2,1,0:T(1,128)} %mask.1, bf16[64,64,256]{2,1,0:T(8,128)(2,1)} %integrals.1), custom_call_target="tpu_custom_call" | custom-call | bytes 4194304 | tf_op jit(solution)/shard_map/prepare/pallas_call | solution.py:211
  3.1 3.4 %collective-permute-start.1 = (bf16[64,256]{1,0:T(8,128)(2,1)}, bf16[64,256]{1,0:T(8,128)(2,1)S(1)}, u32[]{:S(2)}, u32[]{:S(2)}) collective-permute-start(bf16[64,256]{1,0:T(8,128)(2,1)} %get-tuple-element.19), channel_id=1, source_target_pairs={{0,1},{1,0},{2,3},{3,2},{32,33},{33,32},{34,35},{35,34},{64,67},{6... | collective-permute-start | bytes 98312 | tf_op jit(solution)/shard_map/ppermute | solution.py:168
  6.5 1.4 %collective-permute-start = (bf16[64,256]{1,0:T(8,128)(2,1)}, bf16[64,256]{1,0:T(8,128)(2,1)S(1)}, u32[]{:S(2)}, u32[]{:S(2)}) collective-permute-start(bf16[64,256]{1,0:T(8,128)(2,1)} %get-tuple-element.19), channel_id=1, source_target_pairs={{0,0},{1,1},{2,2},{3,3},{32,32},{33,33},{34,34},{35,35},{64,66},{6... | collective-permute-start | bytes 98312 | tf_op jit(solution)/shard_map/ppermute | solution.py:168
  7.9 10.2 %all-to-all-start = ((bf16[64,64,256]{2,1,0:T(8,128)(2,1)}), bf16[64,64,256]{2,1,0:T(8,128)(2,1)S(1)}, u32[]{:S(2)}, u32[]{:S(2)}) async-start(bf16[64,64,256]{2,1,0:T(8,128)(2,1)} %get-tuple-element.18), calls=%async_computation | async-start | bytes 4194304 | tf_op jit(solution)/shard_map/all_to_all | solution.py:229
  18.1 0.0 collective-permute-done.1.second
  18.1 0.0 collective-permute-done.first
  18.1 1.6 %collective-permute-start.4 = (bf16[2,64,256]{2,1,0:T(8,128)(2,1)S(1)}, bf16[2,64,256]{2,1,0:T(8,128)(2,1)S(1)}, u32[]{:S(2)}, u32[]{:S(2)}) collective-permute-start(bf16[2,64,256]{2,1,0:T(8,128)(2,1)S(1)} %pair.1), channel_id=1, source_target_pairs={{0,12},{4,8},{8,4},{12,0},{1,13},{5,9},{9,5},{13,1},{2,14},{6,10},... | collective-permute-start | bytes 196616 | tf_op jit(solution)/shard_map/ppermute | solution.py:27
  19.8 1.0 collective-permute-start.3
  20.7 1.6 %collective-permute-start.2 = (bf16[2,64,256]{2,1,0:T(8,128)(2,1)S(1)}, bf16[2,64,256]{2,1,0:T(8,128)(2,1)S(1)}, u32[]{:S(2)}, u32[]{:S(2)}) collective-permute-start(bf16[2,64,256]{2,1,0:T(8,128)(2,1)S(1)} %pair.1), channel_id=1, source_target_pairs={{0,4},{4,0},{8,12},{12,8},{1,5},{5,1},{9,13},{13,9},{2,6},{6,2},{1... | collective-permute-start | bytes 196616 | tf_op jit(solution)/shard_map/ppermute | solution.py:27
  22.3 7.4 %collective-permute-done.4 = bf16[2,64,256]{2,1,0:T(8,128)(2,1)S(1)} collective-permute-done((bf16[2,64,256]{2,1,0:T(8,128)(2,1)S(1)}, bf16[2,64,256]{2,1,0:T(8,128)(2,1)S(1)}, u32[]{:S(2)}, u32[]{:S(2)}) %collective-permute-start.4) | collective-permute-done | bytes 65568 | tf_op jit(solution)/shard_map/ppermute | solution.py:27
  29.7 0.0 collective-permute-done.3
  29.7 0.0 collective-permute-done.2
  29.8 7.2 %collective-permute-start.7 = (bf16[4,2,64,256]{3,2,1,0:T(8,128)(2,1)S(1)}, bf16[4,2,64,256]{3,2,1,0:T(8,128)(2,1)S(1)}, u32[]{:S(2)}, u32[]{:S(2)}) collective-permute-start(bf16[4,2,64,256]{3,2,1,0:T(8,128)(2,1)S(1)} %pad_maximum_fusion.pieces0), channel_id=1, source_target_pairs={{0,192},{64,128},{128,64},{192,0},{1,193},{65,129},{129,65},{193,1... | collective-permute-start | bytes 786440 | tf_op jit(solution)/shard_map/ppermute | solution.py:27
  37.0 0.6 collective-permute-start.6
  37.6 0.3 collective-permute-start.5
  37.9 0.1 stack.38.where
  38.0 10.6 %collective-permute-done.7.pieces3 = bf16[4,2,64,256]{3,2,1,0:T(8,128)(2,1)S(1)} collective-permute-done((bf16[4,2,64,256]{3,2,1,0:T(8,128)(2,1)S(1)}, bf16[4,2,64,256]{3,2,1,0:T(8,128)(2,1)S(1)}, u32[]{:S(2)}, u32[]{:S(2)}) %collective-permute-start.7) | collective-permute-done | bytes 262176 | tf_op jit(solution)/shard_map/ppermute | solution.py:27
  48.6 0.0 collective-permute-done.6.pieces2
  48.6 0.7 collective-permute-done.5.pieces1
  49.4 0.7 place.1.mine
  50.1 0.1 collective-permute-start.8
  50.2 2.6 %collective-permute-done.8.theirs = bf16[1024,512]{1,0:T(8,128)(2,1)S(1)} collective-permute-done((bf16[1024,512]{1,0:T(8,128)(2,1)S(1)}, bf16[1024,512]{1,0:T(8,128)(2,1)S(1)}, u32[]{:S(2)}, u32[]{:S(2)}) %collective-permute-start.8) | collective-permute-done | bytes 1048608 | tf_op jit(solution)/shard_map/ppermute | solution.py:206
  52.8 1.9 %join.1.density_in = bf16[8192,1024]{1,0:T(8,128)(2,1)} custom-call(s32[5]{0:T(128)S(1)} %stack.38.where, bf16[1024,512]{1,0:T(8,128)(2,1)S(1)} %place.1.mine, bf16[1024,512]{1,0:T(8,128)(2,1)S(1)} %collective-permute-done.8.theirs), custom_call_target="tpu_custom_call" | custom-call | bytes 4194304 | tf_op jit(solution)/shard_map/join/pallas_call | solution.py:197
  54.8 13.5 %all-to-all-done = bf16[64,64,256]{2,1,0:T(8,128)(2,1)S(1)} async-done(((bf16[64,64,256]{2,1,0:T(8,128)(2,1)}), bf16[64,64,256]{2,1,0:T(8,128)(2,1)S(1)}, u32[]{:S(2)}, u32[]{:S(2)}) %all-to-all-start) | async-done | bytes 2097184 | tf_op jit(solution)/shard_map/all_to_all | solution.py:229
  68.3 4.3 %first.1 = (f32[256,1024]{1,0:T(8,128)S(1)}, f32[256,1024]{1,0:T(8,128)S(1)}, bf16[4,4,64,1024]{3,2,1,0:T(8,128)(2,1)S(1)}, bf16[1024,1024]{1,0:T(8,128)(2,1)S(1)}) custom-call(s32[5]{0:T(128)S(1)} %stack.38.where, bf16[4,2,4,2,64,256]{5,4,3,2,1,0:T(8,128)(2,1)S(1)} %bitcast.12, bf16[8192,1024]{1,0:T(8,128)(2,1)} %join.1.density_in), custom_call_target="tpu_custom_call" | custom-call | flops 2147483648 | bytes 8388608 | tf_op jit(solution)/shard_map/first/pallas_call | solution.py:232
  72.6 0.1 collective-permute-start.9
  72.7 0.5 collective-permute-start.10
  73.2 1.8 %own.1.contracted = bf16[512,1024]{1,0:T(8,128)(2,1)S(1)} custom-call(s32[5]{0:T(128)S(1)} %stack.38.where, bf16[4,4,64,1024]{3,2,1,0:T(8,128)(2,1)S(1)} %get-tuple-element.20.screened, bf16[1024,1024]{1,0:T(8,128)(2,1)S(1)} %get-tuple-element.21.density), custom_call_target="tpu_custom_call" | custom-call | flops 1073741824 | bytes 5242880 | tf_op jit(solution)/shard_map/own/pallas_call | solution.py:243
  75.0 0.4 collective-permute-done.9.arrived
  75.3 0.7 near.1
  76.1 5.7 %collective-permute-start.11 = (bf16[128,1024]{1,0:T(8,128)(2,1)S(1)}, bf16[128,1024]{1,0:T(8,128)(2,1)S(1)}, u32[]{:S(2)}, u32[]{:S(2)}) collective-permute-start(bf16[128,1024]{1,0:T(8,128)(2,1)S(1)} %get-tuple-element.28), channel_id=1, source_target_pairs={{0,64},{64,0},{128,192},{192,128},{1,65},{65,1},{129,193},{193,129... | collective-permute-start | bytes 786440 | tf_op jit(solution)/shard_map/ppermute | solution.py:277
  81.8 1.5 %collective-permute-start.12 = (bf16[128,1024]{1,0:T(8,128)(2,1)S(1)}, bf16[128,1024]{1,0:T(8,128)(2,1)S(1)}, u32[]{:S(2)}, u32[]{:S(2)}) collective-permute-start(bf16[128,1024]{1,0:T(8,128)(2,1)S(1)} %get-tuple-element.29), channel_id=1, source_target_pairs={{0,192},{64,128},{128,64},{192,0},{1,193},{65,129},{129,65},{193,1... | collective-permute-start | bytes 786440 | tf_op jit(solution)/shard_map/ppermute | solution.py:277
  83.4 0.0 collective-permute-done.10.arrived
  83.4 0.7 far.1
  84.1 1.5 %collective-permute-start.13 = (bf16[128,1024]{1,0:T(8,128)(2,1)S(1)}, bf16[128,1024]{1,0:T(8,128)(2,1)S(1)}, u32[]{:S(2)}, u32[]{:S(2)}) collective-permute-start(bf16[128,1024]{1,0:T(8,128)(2,1)S(1)} %get-tuple-element.30), channel_id=1, source_target_pairs={{0,128},{64,192},{128,0},{192,64},{1,129},{65,193},{129,1},{193,65... | collective-permute-start | bytes 786440 | tf_op jit(solution)/shard_map/ppermute | solution.py:277
  85.6 3.3 %collective-permute-done.11.second = bf16[128,1024]{1,0:T(8,128)(2,1)S(1)} collective-permute-done((bf16[128,1024]{1,0:T(8,128)(2,1)S(1)}, bf16[128,1024]{1,0:T(8,128)(2,1)S(1)}, u32[]{:S(2)}, u32[]{:S(2)}) %collective-permute-start.11) | collective-permute-done | bytes 262176 | tf_op jit(solution)/shard_map/ppermute | solution.py:277
  88.9 5.9 %collective-permute-done.12.third = bf16[128,1024]{1,0:T(8,128)(2,1)S(1)} collective-permute-done((bf16[128,1024]{1,0:T(8,128)(2,1)S(1)}, bf16[128,1024]{1,0:T(8,128)(2,1)S(1)}, u32[]{:S(2)}, u32[]{:S(2)}) %collective-permute-start.12) | collective-permute-done | bytes 262176 | tf_op jit(solution)/shard_map/ppermute | solution.py:277
  94.9 0.1 add.6
  94.9 1.8 %collective-permute-done.13 = bf16[128,1024]{1,0:T(8,128)(2,1)S(1)} collective-permute-done((bf16[128,1024]{1,0:T(8,128)(2,1)S(1)}, bf16[128,1024]{1,0:T(8,128)(2,1)S(1)}, u32[]{:S(2)}, u32[]{:S(2)}) %collective-permute-start.13) | collective-permute-done | bytes 262176 | tf_op jit(solution)/shard_map/ppermute | solution.py:277
  96.7 0.1 add_convert_fusion
  96.8 0.1 reshape.7
  96.9 17.3 %all_to_all.10 = bf16[32,4,1024]{2,1,0:T(4,128)(2,1)S(1)} all-to-all(bf16[32,4,1024]{2,1,0:T(4,128)(2,1)S(1)} %reshape.7), channel_id=1, replica_groups=mesh['y'=4,'zl'=2,'c'=2,'x'=4,'zh'=4] {'zl','x','zh'}, dimensions={0} | all-to-all | bytes 524288 | tf_op jit(solution)/shard_map/all_to_all | solution.py:290
  114.2 0.7 convert_reduce_fusion
  (2 shorter events, 0.0 us)
Async XLA Ops:
  3.1 15.0 %collective-permute-start.1 = (bf16[64,256]{1,0:T(8,128)(2,1)}, bf16[64,256]{1,0:T(8,128)(2,1)S(1)}, u32[]{:S(2)}, u32[]{:S(2)}) collective-permute-start(bf16[64,256]{1,0:T(8,128)(2,1)} %get-tuple-element.19), channel_id=1, source_target_pairs={{0,1},{1,0},{2,3},{3,2},{32,33},{33,32},{34,35},{35,34},{64,67},{6... | collective-permute-start | bytes 98312 | tf_op jit(solution)/shard_map/ppermute | solution.py:168
  6.5 11.7 %collective-permute-start = (bf16[64,256]{1,0:T(8,128)(2,1)}, bf16[64,256]{1,0:T(8,128)(2,1)S(1)}, u32[]{:S(2)}, u32[]{:S(2)}) collective-permute-start(bf16[64,256]{1,0:T(8,128)(2,1)} %get-tuple-element.19), channel_id=1, source_target_pairs={{0,0},{1,1},{2,2},{3,3},{32,32},{33,33},{34,34},{35,35},{64,66},{6... | collective-permute-start | bytes 98312 | tf_op jit(solution)/shard_map/ppermute | solution.py:168
  7.9 60.4 %all-to-all-start = ((bf16[64,64,256]{2,1,0:T(8,128)(2,1)}), bf16[64,64,256]{2,1,0:T(8,128)(2,1)S(1)}, u32[]{:S(2)}, u32[]{:S(2)}) async-start(bf16[64,64,256]{2,1,0:T(8,128)(2,1)} %get-tuple-element.18), calls=%async_computation | async-start | bytes 4194304 | tf_op jit(solution)/shard_map/all_to_all | solution.py:229
  18.1 11.6 %collective-permute-start.4 = (bf16[2,64,256]{2,1,0:T(8,128)(2,1)S(1)}, bf16[2,64,256]{2,1,0:T(8,128)(2,1)S(1)}, u32[]{:S(2)}, u32[]{:S(2)}) collective-permute-start(bf16[2,64,256]{2,1,0:T(8,128)(2,1)S(1)} %pair.1), channel_id=1, source_target_pairs={{0,12},{4,8},{8,4},{12,0},{1,13},{5,9},{9,5},{13,1},{2,14},{6,10},... | collective-permute-start | bytes 196616 | tf_op jit(solution)/shard_map/ppermute | solution.py:27
  19.8 10.0 %collective-permute-start.3 = (bf16[2,64,256]{2,1,0:T(8,128)(2,1)S(1)}, bf16[2,64,256]{2,1,0:T(8,128)(2,1)S(1)}, u32[]{:S(2)}, u32[]{:S(2)}) collective-permute-start(bf16[2,64,256]{2,1,0:T(8,128)(2,1)S(1)} %pair.1), channel_id=1, source_target_pairs={{0,8},{4,12},{8,0},{12,4},{1,9},{5,13},{9,1},{13,5},{2,10},{6,14},... | collective-permute-start | bytes 196616 | tf_op jit(solution)/shard_map/ppermute | solution.py:27
  20.7 9.0 %collective-permute-start.2 = (bf16[2,64,256]{2,1,0:T(8,128)(2,1)S(1)}, bf16[2,64,256]{2,1,0:T(8,128)(2,1)S(1)}, u32[]{:S(2)}, u32[]{:S(2)}) collective-permute-start(bf16[2,64,256]{2,1,0:T(8,128)(2,1)S(1)} %pair.1), channel_id=1, source_target_pairs={{0,4},{4,0},{8,12},{12,8},{1,5},{5,1},{9,13},{13,9},{2,6},{6,2},{1... | collective-permute-start | bytes 196616 | tf_op jit(solution)/shard_map/ppermute | solution.py:27
  29.8 18.9 %collective-permute-start.7 = (bf16[4,2,64,256]{3,2,1,0:T(8,128)(2,1)S(1)}, bf16[4,2,64,256]{3,2,1,0:T(8,128)(2,1)S(1)}, u32[]{:S(2)}, u32[]{:S(2)}) collective-permute-start(bf16[4,2,64,256]{3,2,1,0:T(8,128)(2,1)S(1)} %pad_maximum_fusion.pieces0), channel_id=1, source_target_pairs={{0,192},{64,128},{128,64},{192,0},{1,193},{65,129},{129,65},{193,1... | collective-permute-start | bytes 786440 | tf_op jit(solution)/shard_map/ppermute | solution.py:27
  37.0 11.7 %collective-permute-start.6 = (bf16[4,2,64,256]{3,2,1,0:T(8,128)(2,1)S(1)}, bf16[4,2,64,256]{3,2,1,0:T(8,128)(2,1)S(1)}, u32[]{:S(2)}, u32[]{:S(2)}) collective-permute-start(bf16[4,2,64,256]{3,2,1,0:T(8,128)(2,1)S(1)} %pad_maximum_fusion.pieces0), channel_id=1, source_target_pairs={{0,128},{64,192},{128,0},{192,64},{1,129},{65,193},{129,1},{193,65... | collective-permute-start | bytes 786440 | tf_op jit(solution)/shard_map/ppermute | solution.py:27
  37.6 11.8 %collective-permute-start.5 = (bf16[4,2,64,256]{3,2,1,0:T(8,128)(2,1)S(1)}, bf16[4,2,64,256]{3,2,1,0:T(8,128)(2,1)S(1)}, u32[]{:S(2)}, u32[]{:S(2)}) collective-permute-start(bf16[4,2,64,256]{3,2,1,0:T(8,128)(2,1)S(1)} %pad_maximum_fusion.pieces0), channel_id=1, source_target_pairs={{0,64},{64,0},{128,192},{192,128},{1,65},{65,1},{129,193},{193,129... | collective-permute-start | bytes 786440 | tf_op jit(solution)/shard_map/ppermute | solution.py:27
  50.1 2.7 %collective-permute-start.8 = (bf16[1024,512]{1,0:T(8,128)(2,1)S(1)}, bf16[1024,512]{1,0:T(8,128)(2,1)S(1)}, u32[]{:S(2)}, u32[]{:S(2)}) collective-permute-start(bf16[1024,512]{1,0:T(8,128)(2,1)S(1)} %place.1.mine), channel_id=1, source_target_pairs={{0,16},{16,0},{1,17},{17,1},{2,18},{18,2},{3,19},{19,3},{4,20},{20... | collective-permute-start | bytes 3145736 | tf_op jit(solution)/shard_map/ppermute | solution.py:206
  72.6 2.7 %collective-permute-start.9 = (f32[256,1024]{1,0:T(8,128)S(1)}, f32[256,1024]{1,0:T(8,128)S(1)}, u32[]{:S(2)}, u32[]{:S(2)}) collective-permute-start(f32[256,1024]{1,0:T(8,128)S(1)} %get-tuple-element.22), channel_id=1, source_target_pairs={{0,16},{16,0},{1,17},{17,1},{2,18},{18,2},{3,19},{19,3},{4,20},{20... | collective-permute-start | bytes 3145736 | tf_op jit(solution)/shard_map/ppermute | solution.py:242
  72.7 10.7 %collective-permute-start.10 = (f32[256,1024]{1,0:T(8,128)S(1)}, f32[256,1024]{1,0:T(8,128)S(1)}, u32[]{:S(2)}, u32[]{:S(2)}) collective-permute-start(f32[256,1024]{1,0:T(8,128)S(1)} %get-tuple-element.26), channel_id=1, source_target_pairs={{0,16},{16,0},{1,17},{17,1},{2,18},{18,2},{3,19},{19,3},{4,20},{20... | collective-permute-start | bytes 3145736 | tf_op jit(solution)/shard_map/ppermute | solution.py:242
  76.1 12.8 %collective-permute-start.11 = (bf16[128,1024]{1,0:T(8,128)(2,1)S(1)}, bf16[128,1024]{1,0:T(8,128)(2,1)S(1)}, u32[]{:S(2)}, u32[]{:S(2)}) collective-permute-start(bf16[128,1024]{1,0:T(8,128)(2,1)S(1)} %get-tuple-element.28), channel_id=1, source_target_pairs={{0,64},{64,0},{128,192},{192,128},{1,65},{65,1},{129,193},{193,129... | collective-permute-start | bytes 786440 | tf_op jit(solution)/shard_map/ppermute | solution.py:277
  81.8 13.0 %collective-permute-start.12 = (bf16[128,1024]{1,0:T(8,128)(2,1)S(1)}, bf16[128,1024]{1,0:T(8,128)(2,1)S(1)}, u32[]{:S(2)}, u32[]{:S(2)}) collective-permute-start(bf16[128,1024]{1,0:T(8,128)(2,1)S(1)} %get-tuple-element.29), channel_id=1, source_target_pairs={{0,192},{64,128},{128,64},{192,0},{1,193},{65,129},{129,65},{193,1... | collective-permute-start | bytes 786440 | tf_op jit(solution)/shard_map/ppermute | solution.py:277
  84.1 12.6 %collective-permute-start.13 = (bf16[128,1024]{1,0:T(8,128)(2,1)S(1)}, bf16[128,1024]{1,0:T(8,128)(2,1)S(1)}, u32[]{:S(2)}, u32[]{:S(2)}) collective-permute-start(bf16[128,1024]{1,0:T(8,128)(2,1)S(1)} %get-tuple-element.30), channel_id=1, source_target_pairs={{0,128},{64,192},{128,0},{192,64},{1,129},{65,193},{129,1},{193,65... | collective-permute-start | bytes 786440 | tf_op jit(solution)/shard_map/ppermute | solution.py:277

commit v6 on v5

--- a/solution.py
+++ b/solution.py
@@ -116,7 +116,7 @@
     return lax.dot_general(contracted[...], several, NT, preferred_element_type=jnp.float32)
 
 
-def first_kernel(where, parts, density_in, near, far, screened, density, rows, contracted, sems):
+def first_kernel(where, parts, density_in, near, far, screened, density, own_rows, rows, contracted, sems):
     fetch = []
     for half in range(2):
         columns = pl.ds(half * 512, 512)
@@ -134,6 +134,7 @@
             for zh in range(4):
                 screened[:, zh, :, left : left + 256] = parts[:, source, zh, z]
     pick_rows(where, 1 - where[4], screened, rows)
+    pick_rows(where, where[4], screened, own_rows)
     for half in range(2):
         for copy in fetch[half * 4 : half * 4 + 4]:
             copy.wait()
@@ -141,12 +142,11 @@
     for half in range(2):
         columns = slice(half * 512, (half + 1) * 512)
         got = exchange_rows(contracted, screened, half)
-        near[:, columns] = got[:256]
+        near[:, columns] = got[:256].astype(near.dtype)
         far[:, columns] = got[256:]
 
 
-def second_kernel(where, screened, density, contracted, rows):
-    pick_rows(where, where[4], screened, rows)
+def second_kernel(rows, density, contracted):
     for half in range(2):
         contract_rows(rows, density, contracted, half)
 
@@ -158,7 +158,7 @@
 def third_kernel(contracted, screened, arrived, out_a, out_b):
     for half in range(2):
         columns = slice(half * 512, (half + 1) * 512)
-        got = exchange_rows(contracted, screened, half) + arrived[:, columns]
+        got = exchange_rows(contracted, screened, half) + arrived[:, columns].astype(jnp.float32)
         out_a[:, columns] = got[:128].astype(out_a.dtype)
         out_b[:, columns] = got[128:].astype(out_b.dtype)
 
@@ -229,27 +229,26 @@
     parts = lax.all_to_all(screened, PLANE, split_axis=0, concat_axis=0, tiled=True)
     whole = gather(where, two)
     f32 = jnp.float32
-    near, far, screened, whole = pl.pallas_call(
+    near, far, screened, whole, rows = pl.pallas_call(
         first_kernel,
-        out_shape=(shape(256, NA, dtype=f32), shape(256, NA, dtype=f32), shape(4, 4, BW, NA), shape(NA, NA)),
+        out_shape=(shape(256, NA), shape(256, NA, dtype=f32), shape(4, 4, BW, NA), shape(NA, NA), shape(512, NA)),
         in_specs=[SMEM, VMEM, HBM],
-        out_specs=(VMEM,) * 4,
+        out_specs=(VMEM,) * 5,
         scratch_shapes=[pltpu.VMEM((512, NA), jnp.bfloat16)] * 2 + [pltpu.SemaphoreType.DMA((8,))],
         compiler_params=WIDE,
         cost_estimate=pl.CostEstimate(flops=2**31, bytes_accessed=8 * 2**20, transcendentals=0),
         name="first",
     )(where, parts.reshape(4, 2, 4, 2, BW, 256), whole)
-    arrived = [lax.ppermute(one, "c", SWAP) for one in (near, far)]
+    arrived = lax.ppermute(near, "c", SWAP)
     contracted = pl.pallas_call(
         second_kernel,
         out_shape=shape(512, NA),
-        in_specs=[SMEM] + [VMEM] * 2,
-        out_specs=VMEM,
-        scratch_shapes=[pltpu.VMEM((512, NA), jnp.bfloat16)],
+        in_specs=[VMEM] * 2,
+        out_specs=VMEM,
         compiler_params=PARAMS,
         cost_estimate=pl.CostEstimate(flops=2**30, bytes_accessed=5 * 2**20, transcendentals=0),
         name="own",
-    )(where, screened, whole)
+    )(rows, whole)
     half_rows = [pl.BlockSpec((256, NA), lambda i, half=half: (half, 0)) for half in range(2)]
     everything = pl.BlockSpec((4, 4, BW, NA), lambda i: (0, 0, 0, 0))
     near = pl.pallas_call(
@@ -261,8 +260,8 @@
         compiler_params=PARAMS,
         cost_estimate=pl.CostEstimate(flops=2**29, bytes_accessed=4 * 2**20, transcendentals=0),
         name="near",
-    )(contracted, screened, arrived[0])
-    contracted, near = lax.optimization_barrier((contracted, near))
+    )(contracted, screened, arrived)
+    contracted, far, near = lax.optimization_barrier((contracted, far, near))
     far, own = pl.pallas_call(
         third_kernel,
         out_shape=(shape(128, NA), shape(128, NA, dtype=jnp.float32)),
@@ -272,7 +271,7 @@
         compiler_params=PARAMS,
         cost_estimate=pl.CostEstimate(flops=2**29, bytes_accessed=4 * 2**20, transcendentals=0),
         name="far",
-    )(contracted, screened, arrived[1])
+    )(contracted, screened, lax.ppermute(far, "c", SWAP))
     sent = [
         lax.ppermute(quarter, "y", [(i, i ^ step) for i in range(4)])
         for step, quarter in zip(STEPS, (near[0], near[1], far))

time: 115 us -> 115 us (level)
  transfers between devices with their start and end apart: 15 -> 15, of which waited for: 9 -> 9; matrix products, arithmetic and copies ran while one was open for 0% -> 0% of each run, Pallas kernels for 5% -> 4%
where the time goes in v6:
time: 115 us
  waiting for transfers between devices  46.9 us (41%)
  starting transfers between devices  36.4 us (32%)
  blocking collectives  17.7 us (15%)
  Pallas kernels  12.9 us (11%)
    ppermute x6, waiting for transfers between devices, from_four(): lax.ppermute(one, axis, [(i, i ^ j) for i in range(4)])  18.8 us
    all_to_all x1, blocking collectives, body(): lax.all_to_all(term, ('zl', 'x', 'zh'), split_axis=0, concat_axis=0, tile...  17.7 us
    all_to_all x1, waiting for transfers between devices, body(): lax.all_to_all(screened, PLANE, split_axis=0, concat_axis=0, tiled=True)  13.5 us
    ppermute x6, starting transfers between devices, from_four(): lax.ppermute(one, axis, [(i, i ^ j) for i in range(4)])  12.3 us
    ppermute x3, waiting for transfers between devices, body(): lax.ppermute(quarter, 'y', [(i, i ^ step) for i in range(4)])  11.3 us
    all_to_all x1, starting transfers between devices, body(): lax.all_to_all(screened, PLANE, split_axis=0, concat_axis=0, tiled=True)  10.2 us
    ppermute x3, starting transfers between devices, body(): lax.ppermute(quarter, 'y', [(i, i ^ step) for i in range(4)])  8.67 us
    ppermute x2, starting transfers between devices, gather_z(): lax.ppermute(block, ('y', 'zl', 'zh'), [(y * 8 + z, y * 8 + (z ^ y * 2 +...  4.76 us
  transfers between devices with their start and end apart: 15, of which 9 were waited for; matrix products, arithmetic and copies ran while one was open for 0% of the time, Pallas kernels for 4%

profile of v6, /device:TPU:2, one launch (start us, length us, event | category | flops | bytes accessed | tf_op | source)
XLA Modules:
  0.0 114.9 jit_solution(11394461648000102315)
XLA Ops:
  0.0 3.1 %prepare.1 = (bf16[64,256]{1,0:T(8,128)(2,1)}, bf16[64,64,256]{2,1,0:T(8,128)(2,1)}) custom-call(s32[1,4]{1,0:T(1,128)} %bitcast.18, bf16[64,256]{1,0:T(8,128)(2,1)} %bitcast.17, s32[1,1,4]{2,1,0:T(1,128)} %mask.1, bf16[64,64,256]{2,1,0:T(8,128)(2,1)} %integrals.1), custom_call_target="tpu_custom_call" | custom-call | bytes 4194304 | tf_op jit(solution)/shard_map/prepare/pallas_call | solution.py:211
  3.1 3.4 %collective-permute-start.1 = (bf16[64,256]{1,0:T(8,128)(2,1)}, bf16[64,256]{1,0:T(8,128)(2,1)S(1)}, u32[]{:S(2)}, u32[]{:S(2)}) collective-permute-start(bf16[64,256]{1,0:T(8,128)(2,1)} %get-tuple-element.21), channel_id=1, source_target_pairs={{0,1},{1,0},{2,3},{3,2},{32,33},{33,32},{34,35},{35,34},{64,67},{6... | collective-permute-start | bytes 98312 | tf_op jit(solution)/shard_map/ppermute | solution.py:168
  6.5 1.4 %collective-permute-start = (bf16[64,256]{1,0:T(8,128)(2,1)}, bf16[64,256]{1,0:T(8,128)(2,1)S(1)}, u32[]{:S(2)}, u32[]{:S(2)}) collective-permute-start(bf16[64,256]{1,0:T(8,128)(2,1)} %get-tuple-element.21), channel_id=1, source_target_pairs={{0,0},{1,1},{2,2},{3,3},{32,32},{33,33},{34,34},{35,35},{64,66},{6... | collective-permute-start | bytes 98312 | tf_op jit(solution)/shard_map/ppermute | solution.py:168
  7.9 10.2 %all-to-all-start = ((bf16[64,64,256]{2,1,0:T(8,128)(2,1)}), bf16[64,64,256]{2,1,0:T(8,128)(2,1)S(1)}, u32[]{:S(2)}, u32[]{:S(2)}) async-start(bf16[64,64,256]{2,1,0:T(8,128)(2,1)} %get-tuple-element.20), calls=%async_computation | async-start | bytes 4194304 | tf_op jit(solution)/shard_map/all_to_all | solution.py:229
  18.1 0.0 collective-permute-done.1.second
  18.1 0.0 collective-permute-done.first
  18.1 1.6 %collective-permute-start.4 = (bf16[2,64,256]{2,1,0:T(8,128)(2,1)S(1)}, bf16[2,64,256]{2,1,0:T(8,128)(2,1)S(1)}, u32[]{:S(2)}, u32[]{:S(2)}) collective-permute-start(bf16[2,64,256]{2,1,0:T(8,128)(2,1)S(1)} %pair.1), channel_id=1, source_target_pairs={{0,12},{4,8},{8,4},{12,0},{1,13},{5,9},{9,5},{13,1},{2,14},{6,10},... | collective-permute-start | bytes 196616 | tf_op jit(solution)/shard_map/ppermute | solution.py:27
  19.8 1.0 collective-permute-start.3
  20.7 1.6 %collective-permute-start.2 = (bf16[2,64,256]{2,1,0:T(8,128)(2,1)S(1)}, bf16[2,64,256]{2,1,0:T(8,128)(2,1)S(1)}, u32[]{:S(2)}, u32[]{:S(2)}) collective-permute-start(bf16[2,64,256]{2,1,0:T(8,128)(2,1)S(1)} %pair.1), channel_id=1, source_target_pairs={{0,4},{4,0},{8,12},{12,8},{1,5},{5,1},{9,13},{13,9},{2,6},{6,2},{1... | collective-permute-start | bytes 196616 | tf_op jit(solution)/shard_map/ppermute | solution.py:27
  22.3 7.4 %collective-permute-done.4 = bf16[2,64,256]{2,1,0:T(8,128)(2,1)S(1)} collective-permute-done((bf16[2,64,256]{2,1,0:T(8,128)(2,1)S(1)}, bf16[2,64,256]{2,1,0:T(8,128)(2,1)S(1)}, u32[]{:S(2)}, u32[]{:S(2)}) %collective-permute-start.4) | collective-permute-done | bytes 65568 | tf_op jit(solution)/shard_map/ppermute | solution.py:27
  29.7 0.0 collective-permute-done.3
  29.7 0.0 collective-permute-done.2
  29.8 7.2 %collective-permute-start.7 = (bf16[4,2,64,256]{3,2,1,0:T(8,128)(2,1)S(1)}, bf16[4,2,64,256]{3,2,1,0:T(8,128)(2,1)S(1)}, u32[]{:S(2)}, u32[]{:S(2)}) collective-permute-start(bf16[4,2,64,256]{3,2,1,0:T(8,128)(2,1)S(1)} %pad_maximum_fusion.pieces0), channel_id=1, source_target_pairs={{0,192},{64,128},{128,64},{192,0},{1,193},{65,129},{129,65},{193,1... | collective-permute-start | bytes 786440 | tf_op jit(solution)/shard_map/ppermute | solution.py:27
  37.0 0.6 collective-permute-start.6
  37.6 0.3 collective-permute-start.5
  37.9 0.1 stack.38.where
  38.0 10.6 %collective-permute-done.7.pieces3 = bf16[4,2,64,256]{3,2,1,0:T(8,128)(2,1)S(1)} collective-permute-done((bf16[4,2,64,256]{3,2,1,0:T(8,128)(2,1)S(1)}, bf16[4,2,64,256]{3,2,1,0:T(8,128)(2,1)S(1)}, u32[]{:S(2)}, u32[]{:S(2)}) %collective-permute-start.7) | collective-permute-done | bytes 262176 | tf_op jit(solution)/shard_map/ppermute | solution.py:27
  48.6 0.0 collective-permute-done.6.pieces2
  48.6 0.7 collective-permute-done.5.pieces1
  49.4 0.7 place.1.mine
  50.1 0.1 collective-permute-start.8
  50.2 2.6 %collective-permute-done.8.theirs = bf16[1024,512]{1,0:T(8,128)(2,1)S(1)} collective-permute-done((bf16[1024,512]{1,0:T(8,128)(2,1)S(1)}, bf16[1024,512]{1,0:T(8,128)(2,1)S(1)}, u32[]{:S(2)}, u32[]{:S(2)}) %collective-permute-start.8) | collective-permute-done | bytes 1048608 | tf_op jit(solution)/shard_map/ppermute | solution.py:206
  52.8 1.9 %join.1.density_in = bf16[8192,1024]{1,0:T(8,128)(2,1)} custom-call(s32[5]{0:T(128)S(1)} %stack.38.where, bf16[1024,512]{1,0:T(8,128)(2,1)S(1)} %place.1.mine, bf16[1024,512]{1,0:T(8,128)(2,1)S(1)} %collective-permute-done.8.theirs), custom_call_target="tpu_custom_call" | custom-call | bytes 4194304 | tf_op jit(solution)/shard_map/join/pallas_call | solution.py:197
  54.8 13.5 %all-to-all-done = bf16[64,64,256]{2,1,0:T(8,128)(2,1)S(1)} async-done(((bf16[64,64,256]{2,1,0:T(8,128)(2,1)}), bf16[64,64,256]{2,1,0:T(8,128)(2,1)S(1)}, u32[]{:S(2)}, u32[]{:S(2)}) %all-to-all-start) | async-done | bytes 2097184 | tf_op jit(solution)/shard_map/all_to_all | solution.py:229
  68.3 4.3 %first.1 = (bf16[256,1024]{1,0:T(8,128)(2,1)S(1)}, f32[256,1024]{1,0:T(8,128)S(1)}, bf16[4,4,64,1024]{3,2,1,0:T(8,128)(2,1)S(1)}, bf16[1024,1024]{1,0:T(8,128)(2,1)S(1)}, bf16[512,1024]{1,0:T(8,128)(2,1)S(1)}) custom-call(s32[5]{0:T(128)S(1)} %stack.38.where, bf16[4,2,4,2,64,256]{5,4,3,2,1,0:T(8,128)(2,1)S(1)} %bitcast.12, bf16[8192,1024]{1,0:T(8,128)(2,1)} %join.1.density_in), custom_call_target="tpu_custom_call" | custom-call | flops 2147483648 | bytes 8388608 | tf_op jit(solution)/shard_map/first/pallas_call | solution.py:232
  72.6 0.1 collective-permute-start.9
  72.7 1.2 %own.1.contracted = bf16[512,1024]{1,0:T(8,128)(2,1)S(1)} custom-call(bf16[512,1024]{1,0:T(8,128)(2,1)S(1)} %get-tuple-element.22.rows, bf16[1024,1024]{1,0:T(8,128)(2,1)S(1)} %get-tuple-element.23.density), custom_call_target="tpu_custom_call" | custom-call | flops 1073741824 | bytes 5242880 | tf_op jit(solution)/shard_map/own/pallas_call | solution.py:243
  73.9 0.6 collective-permute-done.9.arrived
  74.6 0.7 near.1
  75.3 0.2 collective-permute-start.10
  75.6 5.7 %collective-permute-start.11 = (bf16[128,1024]{1,0:T(8,128)(2,1)S(1)}, bf16[128,1024]{1,0:T(8,128)(2,1)S(1)}, u32[]{:S(2)}, u32[]{:S(2)}) collective-permute-start(bf16[128,1024]{1,0:T(8,128)(2,1)S(1)} %get-tuple-element.32), channel_id=1, source_target_pairs={{0,64},{64,0},{128,192},{192,128},{1,65},{65,1},{129,193},{193,129... | collective-permute-start | bytes 786440 | tf_op jit(solution)/shard_map/ppermute | solution.py:276
  81.2 1.5 %collective-permute-start.12 = (bf16[128,1024]{1,0:T(8,128)(2,1)S(1)}, bf16[128,1024]{1,0:T(8,128)(2,1)S(1)}, u32[]{:S(2)}, u32[]{:S(2)}) collective-permute-start(bf16[128,1024]{1,0:T(8,128)(2,1)S(1)} %get-tuple-element.33), channel_id=1, source_target_pairs={{0,192},{64,128},{128,64},{192,0},{1,193},{65,129},{129,65},{193,1... | collective-permute-start | bytes 786440 | tf_op jit(solution)/shard_map/ppermute | solution.py:276
  82.7 0.0 collective-permute-done.10.arrived
  82.7 0.7 far.1
  83.5 1.5 %collective-permute-start.13 = (bf16[128,1024]{1,0:T(8,128)(2,1)S(1)}, bf16[128,1024]{1,0:T(8,128)(2,1)S(1)}, u32[]{:S(2)}, u32[]{:S(2)}) collective-permute-start(bf16[128,1024]{1,0:T(8,128)(2,1)S(1)} %get-tuple-element.34), channel_id=1, source_target_pairs={{0,128},{64,192},{128,0},{192,64},{1,129},{65,193},{129,1},{193,65... | collective-permute-start | bytes 786440 | tf_op jit(solution)/shard_map/ppermute | solution.py:276
  85.0 3.4 %collective-permute-done.11.second = bf16[128,1024]{1,0:T(8,128)(2,1)S(1)} collective-permute-done((bf16[128,1024]{1,0:T(8,128)(2,1)S(1)}, bf16[128,1024]{1,0:T(8,128)(2,1)S(1)}, u32[]{:S(2)}, u32[]{:S(2)}) %collective-permute-start.11) | collective-permute-done | bytes 262176 | tf_op jit(solution)/shard_map/ppermute | solution.py:276
  88.4 6.0 %collective-permute-done.12.third = bf16[128,1024]{1,0:T(8,128)(2,1)S(1)} collective-permute-done((bf16[128,1024]{1,0:T(8,128)(2,1)S(1)}, bf16[128,1024]{1,0:T(8,128)(2,1)S(1)}, u32[]{:S(2)}, u32[]{:S(2)}) %collective-permute-start.12) | collective-permute-done | bytes 262176 | tf_op jit(solution)/shard_map/ppermute | solution.py:276
  94.4 0.1 add.6
  94.5 1.9 %collective-permute-done.13 = bf16[128,1024]{1,0:T(8,128)(2,1)S(1)} collective-permute-done((bf16[128,1024]{1,0:T(8,128)(2,1)S(1)}, bf16[128,1024]{1,0:T(8,128)(2,1)S(1)}, u32[]{:S(2)}, u32[]{:S(2)}) %collective-permute-start.13) | collective-permute-done | bytes 262176 | tf_op jit(solution)/shard_map/ppermute | solution.py:276
  96.4 0.1 add_convert_fusion
  96.4 0.1 reshape.7
  96.5 17.7 %all_to_all.10 = bf16[32,4,1024]{2,1,0:T(4,128)(2,1)S(1)} all-to-all(bf16[32,4,1024]{2,1,0:T(4,128)(2,1)S(1)} %reshape.7), channel_id=1, replica_groups=mesh['y'=4,'zl'=2,'c'=2,'x'=4,'zh'=4] {'zl','x','zh'}, dimensions={0} | all-to-all | bytes 524288 | tf_op jit(solution)/shard_map/all_to_all | solution.py:289
  114.2 0.7 convert_reduce_fusion
  (2 shorter events, 0.0 us)
Async XLA Ops:
  3.1 15.0 %collective-permute-start.1 = (bf16[64,256]{1,0:T(8,128)(2,1)}, bf16[64,256]{1,0:T(8,128)(2,1)S(1)}, u32[]{:S(2)}, u32[]{:S(2)}) collective-permute-start(bf16[64,256]{1,0:T(8,128)(2,1)} %get-tuple-element.21), channel_id=1, source_target_pairs={{0,1},{1,0},{2,3},{3,2},{32,33},{33,32},{34,35},{35,34},{64,67},{6... | collective-permute-start | bytes 98312 | tf_op jit(solution)/shard_map/ppermute | solution.py:168
  6.5 11.7 %collective-permute-start = (bf16[64,256]{1,0:T(8,128)(2,1)}, bf16[64,256]{1,0:T(8,128)(2,1)S(1)}, u32[]{:S(2)}, u32[]{:S(2)}) collective-permute-start(bf16[64,256]{1,0:T(8,128)(2,1)} %get-tuple-element.21), channel_id=1, source_target_pairs={{0,0},{1,1},{2,2},{3,3},{32,32},{33,33},{34,34},{35,35},{64,66},{6... | collective-permute-start | bytes 98312 | tf_op jit(solution)/shard_map/ppermute | solution.py:168
  7.9 60.4 %all-to-all-start = ((bf16[64,64,256]{2,1,0:T(8,128)(2,1)}), bf16[64,64,256]{2,1,0:T(8,128)(2,1)S(1)}, u32[]{:S(2)}, u32[]{:S(2)}) async-start(bf16[64,64,256]{2,1,0:T(8,128)(2,1)} %get-tuple-element.20), calls=%async_computation | async-start | bytes 4194304 | tf_op jit(solution)/shard_map/all_to_all | solution.py:229
  18.1 11.6 %collective-permute-start.4 = (bf16[2,64,256]{2,1,0:T(8,128)(2,1)S(1)}, bf16[2,64,256]{2,1,0:T(8,128)(2,1)S(1)}, u32[]{:S(2)}, u32[]{:S(2)}) collective-permute-start(bf16[2,64,256]{2,1,0:T(8,128)(2,1)S(1)} %pair.1), channel_id=1, source_target_pairs={{0,12},{4,8},{8,4},{12,0},{1,13},{5,9},{9,5},{13,1},{2,14},{6,10},... | collective-permute-start | bytes 196616 | tf_op jit(solution)/shard_map/ppermute | solution.py:27
  19.8 10.0 %collective-permute-start.3 = (bf16[2,64,256]{2,1,0:T(8,128)(2,1)S(1)}, bf16[2,64,256]{2,1,0:T(8,128)(2,1)S(1)}, u32[]{:S(2)}, u32[]{:S(2)}) collective-permute-start(bf16[2,64,256]{2,1,0:T(8,128)(2,1)S(1)} %pair.1), channel_id=1, source_target_pairs={{0,8},{4,12},{8,0},{12,4},{1,9},{5,13},{9,1},{13,5},{2,10},{6,14},... | collective-permute-start | bytes 196616 | tf_op jit(solution)/shard_map/ppermute | solution.py:27
  20.7 9.0 %collective-permute-start.2 = (bf16[2,64,256]{2,1,0:T(8,128)(2,1)S(1)}, bf16[2,64,256]{2,1,0:T(8,128)(2,1)S(1)}, u32[]{:S(2)}, u32[]{:S(2)}) collective-permute-start(bf16[2,64,256]{2,1,0:T(8,128)(2,1)S(1)} %pair.1), channel_id=1, source_target_pairs={{0,4},{4,0},{8,12},{12,8},{1,5},{5,1},{9,13},{13,9},{2,6},{6,2},{1... | collective-permute-start | bytes 196616 | tf_op jit(solution)/shard_map/ppermute | solution.py:27
  29.8 18.9 %collective-permute-start.7 = (bf16[4,2,64,256]{3,2,1,0:T(8,128)(2,1)S(1)}, bf16[4,2,64,256]{3,2,1,0:T(8,128)(2,1)S(1)}, u32[]{:S(2)}, u32[]{:S(2)}) collective-permute-start(bf16[4,2,64,256]{3,2,1,0:T(8,128)(2,1)S(1)} %pad_maximum_fusion.pieces0), channel_id=1, source_target_pairs={{0,192},{64,128},{128,64},{192,0},{1,193},{65,129},{129,65},{193,1... | collective-permute-start | bytes 786440 | tf_op jit(solution)/shard_map/ppermute | solution.py:27
  37.0 11.7 %collective-permute-start.6 = (bf16[4,2,64,256]{3,2,1,0:T(8,128)(2,1)S(1)}, bf16[4,2,64,256]{3,2,1,0:T(8,128)(2,1)S(1)}, u32[]{:S(2)}, u32[]{:S(2)}) collective-permute-start(bf16[4,2,64,256]{3,2,1,0:T(8,128)(2,1)S(1)} %pad_maximum_fusion.pieces0), channel_id=1, source_target_pairs={{0,128},{64,192},{128,0},{192,64},{1,129},{65,193},{129,1},{193,65... | collective-permute-start | bytes 786440 | tf_op jit(solution)/shard_map/ppermute | solution.py:27
  37.6 11.8 %collective-permute-start.5 = (bf16[4,2,64,256]{3,2,1,0:T(8,128)(2,1)S(1)}, bf16[4,2,64,256]{3,2,1,0:T(8,128)(2,1)S(1)}, u32[]{:S(2)}, u32[]{:S(2)}) collective-permute-start(bf16[4,2,64,256]{3,2,1,0:T(8,128)(2,1)S(1)} %pad_maximum_fusion.pieces0), channel_id=1, source_target_pairs={{0,64},{64,0},{128,192},{192,128},{1,65},{65,1},{129,193},{193,129... | collective-permute-start | bytes 786440 | tf_op jit(solution)/shard_map/ppermute | solution.py:27
  50.1 2.7 %collective-permute-start.8 = (bf16[1024,512]{1,0:T(8,128)(2,1)S(1)}, bf16[1024,512]{1,0:T(8,128)(2,1)S(1)}, u32[]{:S(2)}, u32[]{:S(2)}) collective-permute-start(bf16[1024,512]{1,0:T(8,128)(2,1)S(1)} %place.1.mine), channel_id=1, source_target_pairs={{0,16},{16,0},{1,17},{17,1},{2,18},{18,2},{3,19},{19,3},{4,20},{20... | collective-permute-start | bytes 3145736 | tf_op jit(solution)/shard_map/ppermute | solution.py:206
  72.6 2.0 %collective-permute-start.9 = (bf16[256,1024]{1,0:T(8,128)(2,1)S(1)}, bf16[256,1024]{1,0:T(8,128)(2,1)S(1)}, u32[]{:S(2)}, u32[]{:S(2)}) collective-permute-start(bf16[256,1024]{1,0:T(8,128)(2,1)S(1)} %get-tuple-element.26), channel_id=1, source_target_pairs={{0,16},{16,0},{1,17},{17,1},{2,18},{18,2},{3,19},{19,3},{4,20},{20... | collective-permute-start | bytes 1572872 | tf_op jit(solution)/shard_map/ppermute | solution.py:242
  75.3 7.4 %collective-permute-start.10 = (f32[256,1024]{1,0:T(8,128)S(1)}, f32[256,1024]{1,0:T(8,128)S(1)}, u32[]{:S(2)}, u32[]{:S(2)}) collective-permute-start(f32[256,1024]{1,0:T(8,128)S(1)} %get-tuple-element.30), channel_id=1, source_target_pairs={{0,16},{16,0},{1,17},{17,1},{2,18},{18,2},{3,19},{19,3},{4,20},{20... | collective-permute-start | bytes 3145736 | tf_op jit(solution)/shard_map/ppermute | solution.py:274
  75.6 12.8 %collective-permute-start.11 = (bf16[128,1024]{1,0:T(8,128)(2,1)S(1)}, bf16[128,1024]{1,0:T(8,128)(2,1)S(1)}, u32[]{:S(2)}, u32[]{:S(2)}) collective-permute-start(bf16[128,1024]{1,0:T(8,128)(2,1)S(1)} %get-tuple-element.32), channel_id=1, source_target_pairs={{0,64},{64,0},{128,192},{192,128},{1,65},{65,1},{129,193},{193,129... | collective-permute-start | bytes 786440 | tf_op jit(solution)/shard_map/ppermute | solution.py:276
  81.2 13.1 %collective-permute-start.12 = (bf16[128,1024]{1,0:T(8,128)(2,1)S(1)}, bf16[128,1024]{1,0:T(8,128)(2,1)S(1)}, u32[]{:S(2)}, u32[]{:S(2)}) collective-permute-start(bf16[128,1024]{1,0:T(8,128)(2,1)S(1)} %get-tuple-element.33), channel_id=1, source_target_pairs={{0,192},{64,128},{128,64},{192,0},{1,193},{65,129},{129,65},{193,1... | collective-permute-start | bytes 786440 | tf_op jit(solution)/shard_map/ppermute | solution.py:276
  83.5 12.9 %collective-permute-start.13 = (bf16[128,1024]{1,0:T(8,128)(2,1)S(1)}, bf16[128,1024]{1,0:T(8,128)(2,1)S(1)}, u32[]{:S(2)}, u32[]{:S(2)}) collective-permute-start(bf16[128,1024]{1,0:T(8,128)(2,1)S(1)} %get-tuple-element.34), channel_id=1, source_target_pairs={{0,128},{64,192},{128,0},{192,64},{1,129},{65,193},{129,1},{193,65... | collective-permute-start | bytes 786440 | tf_op jit(solution)/shard_map/ppermute | solution.py:276

commit v7 on v6

--- a/solution.py
+++ b/solution.py
@@ -116,7 +116,7 @@
     return lax.dot_general(contracted[...], several, NT, preferred_element_type=jnp.float32)
 
 
-def first_kernel(where, parts, density_in, near, far, screened, density, own_rows, rows, contracted, sems):
+def first_kernel(where, parts, density_in, near, later, screened, density, own_rows, rows, contracted, sems):
     fetch = []
     for half in range(2):
         columns = pl.ds(half * 512, 512)
@@ -141,14 +141,15 @@
         contract_rows(rows, density, contracted, half)
     for half in range(2):
         columns = slice(half * 512, (half + 1) * 512)
-        got = exchange_rows(contracted, screened, half)
-        near[:, columns] = got[:256].astype(near.dtype)
-        far[:, columns] = got[256:]
-
-
-def second_kernel(rows, density, contracted):
+        near[:, columns] = exchange_rows(contracted.at[:256], screened, half).astype(near.dtype)
+    later[...] = contracted[256:, :]
+
+
+def second_kernel(rows, density, later, screened, contracted, far):
     for half in range(2):
         contract_rows(rows, density, contracted, half)
+    for half in range(2):
+        far[:, half * 512 : (half + 1) * 512] = exchange_rows(later, screened, half)
 
 
 def add_kernel(first, second, third, out):
@@ -229,9 +230,9 @@
     parts = lax.all_to_all(screened, PLANE, split_axis=0, concat_axis=0, tiled=True)
     whole = gather(where, two)
     f32 = jnp.float32
-    near, far, screened, whole, rows = pl.pallas_call(
+    near, later, screened, whole, rows = pl.pallas_call(
         first_kernel,
-        out_shape=(shape(256, NA), shape(256, NA, dtype=f32), shape(4, 4, BW, NA), shape(NA, NA), shape(512, NA)),
+        out_shape=(shape(256, NA), shape(256, NA), shape(4, 4, BW, NA), shape(NA, NA), shape(512, NA)),
         in_specs=[SMEM, VMEM, HBM],
         out_specs=(VMEM,) * 5,
         scratch_shapes=[pltpu.VMEM((512, NA), jnp.bfloat16)] * 2 + [pltpu.SemaphoreType.DMA((8,))],
@@ -240,15 +241,15 @@
         name="first",
     )(where, parts.reshape(4, 2, 4, 2, BW, 256), whole)
     arrived = lax.ppermute(near, "c", SWAP)
-    contracted = pl.pallas_call(
+    contracted, far = pl.pallas_call(
         second_kernel,
-        out_shape=shape(512, NA),
-        in_specs=[VMEM] * 2,
-        out_specs=VMEM,
-        compiler_params=PARAMS,
-        cost_estimate=pl.CostEstimate(flops=2**30, bytes_accessed=5 * 2**20, transcendentals=0),
+        out_shape=(shape(512, NA), shape(256, NA, dtype=f32)),
+        in_specs=[VMEM] * 4,
+        out_specs=(VMEM,) * 2,
+        compiler_params=PARAMS,
+        cost_estimate=pl.CostEstimate(flops=3 * 2**29, bytes_accessed=8 * 2**20, transcendentals=0),
         name="own",
-    )(rows, whole)
+    )(rows, whole, later, screened)
     half_rows = [pl.BlockSpec((256, NA), lambda i, half=half: (half, 0)) for half in range(2)]
     everything = pl.BlockSpec((4, 4, BW, NA), lambda i: (0, 0, 0, 0))
     near = pl.pallas_call(

time: 115 us -> 114 us (level)
  transfers between devices with their start and end apart: 15 -> 15, of which waited for: 9 -> 9; matrix products, arithmetic and copies ran while one was open for 0% -> 0% of each run, Pallas kernels for 4% -> 5%
where the time goes in v7:
time: 114 us
  waiting for transfers between devices  46.1 us (40%)
  starting transfers between devices  36.6 us (32%)
  blocking collectives  17.4 us (15%)
  Pallas kernels  12.9 us (11%)
    ppermute x6, waiting for transfers between devices, from_four(): lax.ppermute(one, axis, [(i, i ^ j) for i in range(4)])  18.8 us
    all_to_all x1, blocking collectives, body(): lax.all_to_all(term, ('zl', 'x', 'zh'), split_axis=0, concat_axis=0, tile...  17.4 us
    all_to_all x1, waiting for transfers between devices, body(): lax.all_to_all(screened, PLANE, split_axis=0, concat_axis=0, tiled=True)  13.5 us
    ppermute x6, starting transfers between devices, from_four(): lax.ppermute(one, axis, [(i, i ^ j) for i in range(4)])  12.3 us
    ppermute x3, waiting for transfers between devices, body(): lax.ppermute(quarter, 'y', [(i, i ^ step) for i in range(4)])  11 us
    all_to_all x1, starting transfers between devices, body(): lax.all_to_all(screened, PLANE, split_axis=0, concat_axis=0, tiled=True)  10.2 us
    ppermute x3, starting transfers between devices, body(): lax.ppermute(quarter, 'y', [(i, i ^ step) for i in range(4)])  8.65 us
    ppermute x2, starting transfers between devices, gather_z(): lax.ppermute(block, ('y', 'zl', 'zh'), [(y * 8 + z, y * 8 + (z ^ y * 2 +...  4.76 us
  transfers between devices with their start and end apart: 15, of which 9 were waited for; matrix products, arithmetic and copies ran while one was open for 0% of the time, Pallas kernels for 5%

profile of v7, /device:TPU:2, one launch (start us, length us, event | category | flops | bytes accessed | tf_op | source)
XLA Modules:
  0.0 114.1 jit_solution(4492778224635358458)
XLA Ops:
  0.0 3.1 %prepare.1 = (bf16[64,256]{1,0:T(8,128)(2,1)}, bf16[64,64,256]{2,1,0:T(8,128)(2,1)}) custom-call(s32[1,4]{1,0:T(1,128)} %bitcast.18, bf16[64,256]{1,0:T(8,128)(2,1)} %bitcast.17, s32[1,1,4]{2,1,0:T(1,128)} %mask.1, bf16[64,64,256]{2,1,0:T(8,128)(2,1)} %integrals.1), custom_call_target="tpu_custom_call" | custom-call | bytes 4194304 | tf_op jit(solution)/shard_map/prepare/pallas_call | solution.py:212
  3.1 3.4 %collective-permute-start.1 = (bf16[64,256]{1,0:T(8,128)(2,1)}, bf16[64,256]{1,0:T(8,128)(2,1)S(1)}, u32[]{:S(2)}, u32[]{:S(2)}) collective-permute-start(bf16[64,256]{1,0:T(8,128)(2,1)} %get-tuple-element.23), channel_id=1, source_target_pairs={{0,1},{1,0},{2,3},{3,2},{32,33},{33,32},{34,35},{35,34},{64,67},{6... | collective-permute-start | bytes 98312 | tf_op jit(solution)/shard_map/ppermute | solution.py:169
  6.5 1.4 %collective-permute-start = (bf16[64,256]{1,0:T(8,128)(2,1)}, bf16[64,256]{1,0:T(8,128)(2,1)S(1)}, u32[]{:S(2)}, u32[]{:S(2)}) collective-permute-start(bf16[64,256]{1,0:T(8,128)(2,1)} %get-tuple-element.23), channel_id=1, source_target_pairs={{0,0},{1,1},{2,2},{3,3},{32,32},{33,33},{34,34},{35,35},{64,66},{6... | collective-permute-start | bytes 98312 | tf_op jit(solution)/shard_map/ppermute | solution.py:169
  7.9 10.2 %all-to-all-start = ((bf16[64,64,256]{2,1,0:T(8,128)(2,1)}), bf16[64,64,256]{2,1,0:T(8,128)(2,1)S(1)}, u32[]{:S(2)}, u32[]{:S(2)}) async-start(bf16[64,64,256]{2,1,0:T(8,128)(2,1)} %get-tuple-element.22), calls=%async_computation | async-start | bytes 4194304 | tf_op jit(solution)/shard_map/all_to_all | solution.py:230
  18.1 0.0 collective-permute-done.1.second
  18.1 0.0 collective-permute-done.first
  18.1 1.6 %collective-permute-start.4 = (bf16[2,64,256]{2,1,0:T(8,128)(2,1)S(1)}, bf16[2,64,256]{2,1,0:T(8,128)(2,1)S(1)}, u32[]{:S(2)}, u32[]{:S(2)}) collective-permute-start(bf16[2,64,256]{2,1,0:T(8,128)(2,1)S(1)} %pair.1), channel_id=1, source_target_pairs={{0,12},{4,8},{8,4},{12,0},{1,13},{5,9},{9,5},{13,1},{2,14},{6,10},... | collective-permute-start | bytes 196616 | tf_op jit(solution)/shard_map/ppermute | solution.py:27
  19.8 1.0 collective-permute-start.3
  20.7 1.6 %collective-permute-start.2 = (bf16[2,64,256]{2,1,0:T(8,128)(2,1)S(1)}, bf16[2,64,256]{2,1,0:T(8,128)(2,1)S(1)}, u32[]{:S(2)}, u32[]{:S(2)}) collective-permute-start(bf16[2,64,256]{2,1,0:T(8,128)(2,1)S(1)} %pair.1), channel_id=1, source_target_pairs={{0,4},{4,0},{8,12},{12,8},{1,5},{5,1},{9,13},{13,9},{2,6},{6,2},{1... | collective-permute-start | bytes 196616 | tf_op jit(solution)/shard_map/ppermute | solution.py:27
  22.3 7.4 %collective-permute-done.4 = bf16[2,64,256]{2,1,0:T(8,128)(2,1)S(1)} collective-permute-done((bf16[2,64,256]{2,1,0:T(8,128)(2,1)S(1)}, bf16[2,64,256]{2,1,0:T(8,128)(2,1)S(1)}, u32[]{:S(2)}, u32[]{:S(2)}) %collective-permute-start.4) | collective-permute-done | bytes 65568 | tf_op jit(solution)/shard_map/ppermute | solution.py:27
  29.7 0.0 collective-permute-done.3
  29.7 0.0 collective-permute-done.2
  29.8 7.2 %collective-permute-start.7 = (bf16[4,2,64,256]{3,2,1,0:T(8,128)(2,1)S(1)}, bf16[4,2,64,256]{3,2,1,0:T(8,128)(2,1)S(1)}, u32[]{:S(2)}, u32[]{:S(2)}) collective-permute-start(bf16[4,2,64,256]{3,2,1,0:T(8,128)(2,1)S(1)} %pad_maximum_fusion.pieces0), channel_id=1, source_target_pairs={{0,192},{64,128},{128,64},{192,0},{1,193},{65,129},{129,65},{193,1... | collective-permute-start | bytes 786440 | tf_op jit(solution)/shard_map/ppermute | solution.py:27
  37.0 0.6 collective-permute-start.6
  37.6 0.3 collective-permute-start.5
  37.9 0.1 stack.38.where
  38.0 10.6 %collective-permute-done.7.pieces3 = bf16[4,2,64,256]{3,2,1,0:T(8,128)(2,1)S(1)} collective-permute-done((bf16[4,2,64,256]{3,2,1,0:T(8,128)(2,1)S(1)}, bf16[4,2,64,256]{3,2,1,0:T(8,128)(2,1)S(1)}, u32[]{:S(2)}, u32[]{:S(2)}) %collective-permute-start.7) | collective-permute-done | bytes 262176 | tf_op jit(solution)/shard_map/ppermute | solution.py:27
  48.6 0.0 collective-permute-done.6.pieces2
  48.6 0.7 collective-permute-done.5.pieces1
  49.4 0.7 place.1.mine
  50.1 0.1 collective-permute-start.8
  50.2 2.6 %collective-permute-done.8.theirs = bf16[1024,512]{1,0:T(8,128)(2,1)S(1)} collective-permute-done((bf16[1024,512]{1,0:T(8,128)(2,1)S(1)}, bf16[1024,512]{1,0:T(8,128)(2,1)S(1)}, u32[]{:S(2)}, u32[]{:S(2)}) %collective-permute-start.8) | collective-permute-done | bytes 1048608 | tf_op jit(solution)/shard_map/ppermute | solution.py:207
  52.8 1.9 %join.1.density_in = bf16[8192,1024]{1,0:T(8,128)(2,1)} custom-call(s32[5]{0:T(128)S(1)} %stack.38.where, bf16[1024,512]{1,0:T(8,128)(2,1)S(1)} %place.1.mine, bf16[1024,512]{1,0:T(8,128)(2,1)S(1)} %collective-permute-done.8.theirs), custom_call_target="tpu_custom_call" | custom-call | bytes 4194304 | tf_op jit(solution)/shard_map/join/pallas_call | solution.py:198
  54.8 13.5 %all-to-all-done = bf16[64,64,256]{2,1,0:T(8,128)(2,1)S(1)} async-done(((bf16[64,64,256]{2,1,0:T(8,128)(2,1)}), bf16[64,64,256]{2,1,0:T(8,128)(2,1)S(1)}, u32[]{:S(2)}, u32[]{:S(2)}) %all-to-all-start) | async-done | bytes 2097184 | tf_op jit(solution)/shard_map/all_to_all | solution.py:230
  68.3 3.8 %first.1 = (bf16[256,1024]{1,0:T(8,128)(2,1)S(1)}, bf16[256,1024]{1,0:T(8,128)(2,1)S(1)}, bf16[4,4,64,1024]{3,2,1,0:T(8,128)(2,1)S(1)}, bf16[1024,1024]{1,0:T(8,128)(2,1)S(1)}, bf16[512,1024]{1,0:T(8,128)(2,1)S(1)}) custom-call(s32[5]{0:T(128)S(1)} %stack.38.where, bf16[4,2,4,2,64,256]{5,4,3,2,1,0:T(8,128)(2,1)S(1)} %bitcast.12, ...), custom_call_target="tpu_custom_call" | custom-call | flops 2147483648 | bytes 8388608 | tf_op jit(solution)/shard_map/first/pallas_call | solution.py:233
  72.1 0.1 collective-permute-start.9
  72.2 1.8 %own.1 = (bf16[512,1024]{1,0:T(8,128)(2,1)S(1)}, f32[256,1024]{1,0:T(8,128)S(1)}) custom-call(bf16[512,1024]{1,0:T(8,128)(2,1)S(1)} %get-tuple-element.24.rows, bf16[1024,1024]{1,0:T(8,128)(2,1)S(1)} %get-tuple-element.25.density, bf16[256,1024]{1,0:T(8,128)(2,1)S(1)} %get-tuple-element.26.later, bf16[4,4,64,1024]{3,2,1,0:T(8,128)(2,1)S(1)} %get-tuple-element.27.screened), custom_call_target="tpu_custom_call" | custom-call | flops 1610612736 | bytes 8388608 | tf_op jit(solution)/shard_map/own/pallas_call | solution.py:244
  74.0 0.1 collective-permute-done.9.arrived
  74.1 0.7 near.1
  74.8 0.5 collective-permute-start.10
  75.3 5.7 %collective-permute-start.11 = (bf16[128,1024]{1,0:T(8,128)(2,1)S(1)}, bf16[128,1024]{1,0:T(8,128)(2,1)S(1)}, u32[]{:S(2)}, u32[]{:S(2)}) collective-permute-start(bf16[128,1024]{1,0:T(8,128)(2,1)S(1)} %get-tuple-element.36), channel_id=1, source_target_pairs={{0,64},{64,0},{128,192},{192,128},{1,65},{65,1},{129,193},{193,129... | collective-permute-start | bytes 786440 | tf_op jit(solution)/shard_map/ppermute | solution.py:277
  81.0 1.4 %collective-permute-start.12 = (bf16[128,1024]{1,0:T(8,128)(2,1)S(1)}, bf16[128,1024]{1,0:T(8,128)(2,1)S(1)}, u32[]{:S(2)}, u32[]{:S(2)}) collective-permute-start(bf16[128,1024]{1,0:T(8,128)(2,1)S(1)} %get-tuple-element.37), channel_id=1, source_target_pairs={{0,192},{64,128},{128,64},{192,0},{1,193},{65,129},{129,65},{193,1... | collective-permute-start | bytes 786440 | tf_op jit(solution)/shard_map/ppermute | solution.py:277
  82.4 0.0 collective-permute-done.10.arrived
  82.4 0.7 far.1
  83.2 1.6 %collective-permute-start.13 = (bf16[128,1024]{1,0:T(8,128)(2,1)S(1)}, bf16[128,1024]{1,0:T(8,128)(2,1)S(1)}, u32[]{:S(2)}, u32[]{:S(2)}) collective-permute-start(bf16[128,1024]{1,0:T(8,128)(2,1)S(1)} %get-tuple-element.38), channel_id=1, source_target_pairs={{0,128},{64,192},{128,0},{192,64},{1,129},{65,193},{129,1},{193,65... | collective-permute-start | bytes 786440 | tf_op jit(solution)/shard_map/ppermute | solution.py:277
  84.7 3.0 %collective-permute-done.11.second = bf16[128,1024]{1,0:T(8,128)(2,1)S(1)} collective-permute-done((bf16[128,1024]{1,0:T(8,128)(2,1)S(1)}, bf16[128,1024]{1,0:T(8,128)(2,1)S(1)}, u32[]{:S(2)}, u32[]{:S(2)}) %collective-permute-start.11) | collective-permute-done | bytes 262176 | tf_op jit(solution)/shard_map/ppermute | solution.py:277
  87.7 6.3 %collective-permute-done.12.third = bf16[128,1024]{1,0:T(8,128)(2,1)S(1)} collective-permute-done((bf16[128,1024]{1,0:T(8,128)(2,1)S(1)}, bf16[128,1024]{1,0:T(8,128)(2,1)S(1)}, u32[]{:S(2)}, u32[]{:S(2)}) %collective-permute-start.12) | collective-permute-done | bytes 262176 | tf_op jit(solution)/shard_map/ppermute | solution.py:277
  94.0 0.1 add.6
  94.0 1.8 %collective-permute-done.13 = bf16[128,1024]{1,0:T(8,128)(2,1)S(1)} collective-permute-done((bf16[128,1024]{1,0:T(8,128)(2,1)S(1)}, bf16[128,1024]{1,0:T(8,128)(2,1)S(1)}, u32[]{:S(2)}, u32[]{:S(2)}) %collective-permute-start.13) | collective-permute-done | bytes 262176 | tf_op jit(solution)/shard_map/ppermute | solution.py:277
  95.8 0.1 add_convert_fusion
  95.9 0.1 reshape.7
  96.0 17.4 %all_to_all.10 = bf16[32,4,1024]{2,1,0:T(4,128)(2,1)S(1)} all-to-all(bf16[32,4,1024]{2,1,0:T(4,128)(2,1)S(1)} %reshape.7), channel_id=1, replica_groups=mesh['y'=4,'zl'=2,'c'=2,'x'=4,'zh'=4] {'zl','x','zh'}, dimensions={0} | all-to-all | bytes 524288 | tf_op jit(solution)/shard_map/all_to_all | solution.py:290
  113.4 0.7 convert_reduce_fusion
  (2 shorter events, 0.0 us)
Async XLA Ops:
  3.1 15.0 %collective-permute-start.1 = (bf16[64,256]{1,0:T(8,128)(2,1)}, bf16[64,256]{1,0:T(8,128)(2,1)S(1)}, u32[]{:S(2)}, u32[]{:S(2)}) collective-permute-start(bf16[64,256]{1,0:T(8,128)(2,1)} %get-tuple-element.23), channel_id=1, source_target_pairs={{0,1},{1,0},{2,3},{3,2},{32,33},{33,32},{34,35},{35,34},{64,67},{6... | collective-permute-start | bytes 98312 | tf_op jit(solution)/shard_map/ppermute | solution.py:169
  6.5 11.7 %collective-permute-start = (bf16[64,256]{1,0:T(8,128)(2,1)}, bf16[64,256]{1,0:T(8,128)(2,1)S(1)}, u32[]{:S(2)}, u32[]{:S(2)}) collective-permute-start(bf16[64,256]{1,0:T(8,128)(2,1)} %get-tuple-element.23), channel_id=1, source_target_pairs={{0,0},{1,1},{2,2},{3,3},{32,32},{33,33},{34,34},{35,35},{64,66},{6... | collective-permute-start | bytes 98312 | tf_op jit(solution)/shard_map/ppermute | solution.py:169
  7.9 60.4 %all-to-all-start = ((bf16[64,64,256]{2,1,0:T(8,128)(2,1)}), bf16[64,64,256]{2,1,0:T(8,128)(2,1)S(1)}, u32[]{:S(2)}, u32[]{:S(2)}) async-start(bf16[64,64,256]{2,1,0:T(8,128)(2,1)} %get-tuple-element.22), calls=%async_computation | async-start | bytes 4194304 | tf_op jit(solution)/shard_map/all_to_all | solution.py:230
  18.1 11.6 %collective-permute-start.4 = (bf16[2,64,256]{2,1,0:T(8,128)(2,1)S(1)}, bf16[2,64,256]{2,1,0:T(8,128)(2,1)S(1)}, u32[]{:S(2)}, u32[]{:S(2)}) collective-permute-start(bf16[2,64,256]{2,1,0:T(8,128)(2,1)S(1)} %pair.1), channel_id=1, source_target_pairs={{0,12},{4,8},{8,4},{12,0},{1,13},{5,9},{9,5},{13,1},{2,14},{6,10},... | collective-permute-start | bytes 196616 | tf_op jit(solution)/shard_map/ppermute | solution.py:27
  19.8 10.0 %collective-permute-start.3 = (bf16[2,64,256]{2,1,0:T(8,128)(2,1)S(1)}, bf16[2,64,256]{2,1,0:T(8,128)(2,1)S(1)}, u32[]{:S(2)}, u32[]{:S(2)}) collective-permute-start(bf16[2,64,256]{2,1,0:T(8,128)(2,1)S(1)} %pair.1), channel_id=1, source_target_pairs={{0,8},{4,12},{8,0},{12,4},{1,9},{5,13},{9,1},{13,5},{2,10},{6,14},... | collective-permute-start | bytes 196616 | tf_op jit(solution)/shard_map/ppermute | solution.py:27
  20.7 9.0 %collective-permute-start.2 = (bf16[2,64,256]{2,1,0:T(8,128)(2,1)S(1)}, bf16[2,64,256]{2,1,0:T(8,128)(2,1)S(1)}, u32[]{:S(2)}, u32[]{:S(2)}) collective-permute-start(bf16[2,64,256]{2,1,0:T(8,128)(2,1)S(1)} %pair.1), channel_id=1, source_target_pairs={{0,4},{4,0},{8,12},{12,8},{1,5},{5,1},{9,13},{13,9},{2,6},{6,2},{1... | collective-permute-start | bytes 196616 | tf_op jit(solution)/shard_map/ppermute | solution.py:27
  29.8 18.9 %collective-permute-start.7 = (bf16[4,2,64,256]{3,2,1,0:T(8,128)(2,1)S(1)}, bf16[4,2,64,256]{3,2,1,0:T(8,128)(2,1)S(1)}, u32[]{:S(2)}, u32[]{:S(2)}) collective-permute-start(bf16[4,2,64,256]{3,2,1,0:T(8,128)(2,1)S(1)} %pad_maximum_fusion.pieces0), channel_id=1, source_target_pairs={{0,192},{64,128},{128,64},{192,0},{1,193},{65,129},{129,65},{193,1... | collective-permute-start | bytes 786440 | tf_op jit(solution)/shard_map/ppermute | solution.py:27
  37.0 11.7 %collective-permute-start.6 = (bf16[4,2,64,256]{3,2,1,0:T(8,128)(2,1)S(1)}, bf16[4,2,64,256]{3,2,1,0:T(8,128)(2,1)S(1)}, u32[]{:S(2)}, u32[]{:S(2)}) collective-permute-start(bf16[4,2,64,256]{3,2,1,0:T(8,128)(2,1)S(1)} %pad_maximum_fusion.pieces0), channel_id=1, source_target_pairs={{0,128},{64,192},{128,0},{192,64},{1,129},{65,193},{129,1},{193,65... | collective-permute-start | bytes 786440 | tf_op jit(solution)/shard_map/ppermute | solution.py:27
  37.6 11.8 %collective-permute-start.5 = (bf16[4,2,64,256]{3,2,1,0:T(8,128)(2,1)S(1)}, bf16[4,2,64,256]{3,2,1,0:T(8,128)(2,1)S(1)}, u32[]{:S(2)}, u32[]{:S(2)}) collective-permute-start(bf16[4,2,64,256]{3,2,1,0:T(8,128)(2,1)S(1)} %pad_maximum_fusion.pieces0), channel_id=1, source_target_pairs={{0,64},{64,0},{128,192},{192,128},{1,65},{65,1},{129,193},{193,129... | collective-permute-start | bytes 786440 | tf_op jit(solution)/shard_map/ppermute | solution.py:27
  50.1 2.7 %collective-permute-start.8 = (bf16[1024,512]{1,0:T(8,128)(2,1)S(1)}, bf16[1024,512]{1,0:T(8,128)(2,1)S(1)}, u32[]{:S(2)}, u32[]{:S(2)}) collective-permute-start(bf16[1024,512]{1,0:T(8,128)(2,1)S(1)} %place.1.mine), channel_id=1, source_target_pairs={{0,16},{16,0},{1,17},{17,1},{2,18},{18,2},{3,19},{19,3},{4,20},{20... | collective-permute-start | bytes 3145736 | tf_op jit(solution)/shard_map/ppermute | solution.py:207
  72.1 2.0 %collective-permute-start.9 = (bf16[256,1024]{1,0:T(8,128)(2,1)S(1)}, bf16[256,1024]{1,0:T(8,128)(2,1)S(1)}, u32[]{:S(2)}, u32[]{:S(2)}) collective-permute-start(bf16[256,1024]{1,0:T(8,128)(2,1)S(1)} %get-tuple-element.30), channel_id=1, source_target_pairs={{0,16},{16,0},{1,17},{17,1},{2,18},{18,2},{3,19},{19,3},{4,20},{20... | collective-permute-start | bytes 1572872 | tf_op jit(solution)/shard_map/ppermute | solution.py:243
  74.8 7.6 %collective-permute-start.10 = (f32[256,1024]{1,0:T(8,128)S(1)}, f32[256,1024]{1,0:T(8,128)S(1)}, u32[]{:S(2)}, u32[]{:S(2)}) collective-permute-start(f32[256,1024]{1,0:T(8,128)S(1)} %get-tuple-element.34), channel_id=1, source_target_pairs={{0,16},{16,0},{1,17},{17,1},{2,18},{18,2},{3,19},{19,3},{4,20},{20... | collective-permute-start | bytes 3145736 | tf_op jit(solution)/shard_map/ppermute | solution.py:275
  75.3 12.4 %collective-permute-start.11 = (bf16[128,1024]{1,0:T(8,128)(2,1)S(1)}, bf16[128,1024]{1,0:T(8,128)(2,1)S(1)}, u32[]{:S(2)}, u32[]{:S(2)}) collective-permute-start(bf16[128,1024]{1,0:T(8,128)(2,1)S(1)} %get-tuple-element.36), channel_id=1, source_target_pairs={{0,64},{64,0},{128,192},{192,128},{1,65},{65,1},{129,193},{193,129... | collective-permute-start | bytes 786440 | tf_op jit(solution)/shard_map/ppermute | solution.py:277
  81.0 13.0 %collective-permute-start.12 = (bf16[128,1024]{1,0:T(8,128)(2,1)S(1)}, bf16[128,1024]{1,0:T(8,128)(2,1)S(1)}, u32[]{:S(2)}, u32[]{:S(2)}) collective-permute-start(bf16[128,1024]{1,0:T(8,128)(2,1)S(1)} %get-tuple-element.37), channel_id=1, source_target_pairs={{0,192},{64,128},{128,64},{192,0},{1,193},{65,129},{129,65},{193,1... | collective-permute-start | bytes 786440 | tf_op jit(solution)/shard_map/ppermute | solution.py:277
  83.2 12.7 %collective-permute-start.13 = (bf16[128,1024]{1,0:T(8,128)(2,1)S(1)}, bf16[128,1024]{1,0:T(8,128)(2,1)S(1)}, u32[]{:S(2)}, u32[]{:S(2)}) collective-permute-start(bf16[128,1024]{1,0:T(8,128)(2,1)S(1)} %get-tuple-element.38), channel_id=1, source_target_pairs={{0,128},{64,192},{128,0},{192,64},{1,129},{65,193},{129,1},{193,65... | collective-permute-start | bytes 786440 | tf_op jit(solution)/shard_map/ppermute | solution.py:277

commit v8 on v7

--- a/solution.py
+++ b/solution.py
@@ -75,24 +75,26 @@
         pltpu.make_async_copy(block, block_in, sems.at[1]),
         pltpu.make_async_copy(mask, scalars, sems.at[2]),
     ]
-    for copy in small:
-        copy.start()
+    small[2].start()
     inward, outward = [], []
     for index in range(8):
         part = pl.ds(index * 8, 8)
         inward.append(pltpu.make_async_copy(integrals.at[part], held.at[part], sems.at[3 + index]))
         outward.append(pltpu.make_async_copy(held.at[part], out.at[part], out_sems.at[index]))
         inward[-1].start()
-    for copy in small:
-        copy.wait()
-    row = scale_row([block_scalars[0, index] for index in range(4)])
-    block_out[...] = (block_in[...].astype(jnp.float32) * row).astype(jnp.bfloat16)
+    for copy in small[:2]:
+        copy.start()
+    small[2].wait()
     row = scale_row([scalars[0, 0, index] for index in range(4)]).astype(jnp.bfloat16)
     for index in range(8):
         part = pl.ds(index * 8, 8)
         inward[index].wait()
         held[part] = held[part] * row[None]
         outward[index].start()
+    for copy in small[:2]:
+        copy.wait()
+    row = scale_row([block_scalars[0, index] for index in range(4)])
+    block_out[...] = (block_in[...].astype(jnp.float32) * row).astype(jnp.bfloat16)
     for copy in outward:
         copy.wait()
 

time: 114 us -> 114 us (level)
  no operation moved by 1% of the time
where the time goes in v8:
time: 114 us
  waiting for transfers between devices  46.1 us (40%)
  starting transfers between devices  36.6 us (32%)
  blocking collectives  17.4 us (15%)
  Pallas kernels  12.9 us (11%)
    ppermute x6, waiting for transfers between devices, from_four(): lax.ppermute(one, axis, [(i, i ^ j) for i in range(4)])  18.8 us
    all_to_all x1, blocking collectives, body(): lax.all_to_all(term, ('zl', 'x', 'zh'), split_axis=0, concat_axis=0, tile...  17.4 us
    all_to_all x1, waiting for transfers between devices, body(): lax.all_to_all(screened, PLANE, split_axis=0, concat_axis=0, tiled=True)  13.5 us
    ppermute x6, starting transfers between devices, from_four(): lax.ppermute(one, axis, [(i, i ^ j) for i in range(4)])  12.3 us
    ppermute x3, waiting for transfers between devices, body(): lax.ppermute(quarter, 'y', [(i, i ^ step) for i in range(4)])  11 us
    all_to_all x1, starting transfers between devices, body(): lax.all_to_all(screened, PLANE, split_axis=0, concat_axis=0, tiled=True)  10.2 us
    ppermute x3, starting transfers between devices, body(): lax.ppermute(quarter, 'y', [(i, i ^ step) for i in range(4)])  8.65 us
    ppermute x2, starting transfers between devices, gather_z(): lax.ppermute(block, ('y', 'zl', 'zh'), [(y * 8 + z, y * 8 + (z ^ y * 2 +...  4.76 us
  transfers between devices with their start and end apart: 15, of which 9 were waited for; matrix products, arithmetic and copies ran while one was open for 0% of the time, Pallas kernels for 5%

profile of v8, /device:TPU:2, one launch (start us, length us, event | category | flops | bytes accessed | tf_op | source)
XLA Modules:
  0.0 114.1 jit_solution(7908666590846117675)
XLA Ops:
  0.0 3.1 %prepare.1 = (bf16[64,256]{1,0:T(8,128)(2,1)}, bf16[64,64,256]{2,1,0:T(8,128)(2,1)}) custom-call(s32[1,4]{1,0:T(1,128)} %bitcast.18, bf16[64,256]{1,0:T(8,128)(2,1)} %bitcast.17, s32[1,1,4]{2,1,0:T(1,128)} %mask.1, bf16[64,64,256]{2,1,0:T(8,128)(2,1)} %integrals.1), custom_call_target="tpu_custom_call" | custom-call | bytes 4194304 | tf_op jit(solution)/shard_map/prepare/pallas_call | solution.py:214
  3.1 3.4 %collective-permute-start.1 = (bf16[64,256]{1,0:T(8,128)(2,1)}, bf16[64,256]{1,0:T(8,128)(2,1)S(1)}, u32[]{:S(2)}, u32[]{:S(2)}) collective-permute-start(bf16[64,256]{1,0:T(8,128)(2,1)} %get-tuple-element.23), channel_id=1, source_target_pairs={{0,1},{1,0},{2,3},{3,2},{32,33},{33,32},{34,35},{35,34},{64,67},{6... | collective-permute-start | bytes 98312 | tf_op jit(solution)/shard_map/ppermute | solution.py:171
  6.5 1.4 %collective-permute-start = (bf16[64,256]{1,0:T(8,128)(2,1)}, bf16[64,256]{1,0:T(8,128)(2,1)S(1)}, u32[]{:S(2)}, u32[]{:S(2)}) collective-permute-start(bf16[64,256]{1,0:T(8,128)(2,1)} %get-tuple-element.23), channel_id=1, source_target_pairs={{0,0},{1,1},{2,2},{3,3},{32,32},{33,33},{34,34},{35,35},{64,66},{6... | collective-permute-start | bytes 98312 | tf_op jit(solution)/shard_map/ppermute | solution.py:171
  7.9 10.2 %all-to-all-start = ((bf16[64,64,256]{2,1,0:T(8,128)(2,1)}), bf16[64,64,256]{2,1,0:T(8,128)(2,1)S(1)}, u32[]{:S(2)}, u32[]{:S(2)}) async-start(bf16[64,64,256]{2,1,0:T(8,128)(2,1)} %get-tuple-element.22), calls=%async_computation | async-start | bytes 4194304 | tf_op jit(solution)/shard_map/all_to_all | solution.py:232
  18.1 0.0 collective-permute-done.1.second
  18.1 0.0 collective-permute-done.first
  18.1 1.6 %collective-permute-start.4 = (bf16[2,64,256]{2,1,0:T(8,128)(2,1)S(1)}, bf16[2,64,256]{2,1,0:T(8,128)(2,1)S(1)}, u32[]{:S(2)}, u32[]{:S(2)}) collective-permute-start(bf16[2,64,256]{2,1,0:T(8,128)(2,1)S(1)} %pair.1), channel_id=1, source_target_pairs={{0,12},{4,8},{8,4},{12,0},{1,13},{5,9},{9,5},{13,1},{2,14},{6,10},... | collective-permute-start | bytes 196616 | tf_op jit(solution)/shard_map/ppermute | solution.py:27
  19.8 1.0 collective-permute-start.3
  20.7 1.6 %collective-permute-start.2 = (bf16[2,64,256]{2,1,0:T(8,128)(2,1)S(1)}, bf16[2,64,256]{2,1,0:T(8,128)(2,1)S(1)}, u32[]{:S(2)}, u32[]{:S(2)}) collective-permute-start(bf16[2,64,256]{2,1,0:T(8,128)(2,1)S(1)} %pair.1), channel_id=1, source_target_pairs={{0,4},{4,0},{8,12},{12,8},{1,5},{5,1},{9,13},{13,9},{2,6},{6,2},{1... | collective-permute-start | bytes 196616 | tf_op jit(solution)/shard_map/ppermute | solution.py:27
  22.3 7.4 %collective-permute-done.4 = bf16[2,64,256]{2,1,0:T(8,128)(2,1)S(1)} collective-permute-done((bf16[2,64,256]{2,1,0:T(8,128)(2,1)S(1)}, bf16[2,64,256]{2,1,0:T(8,128)(2,1)S(1)}, u32[]{:S(2)}, u32[]{:S(2)}) %collective-permute-start.4) | collective-permute-done | bytes 65568 | tf_op jit(solution)/shard_map/ppermute | solution.py:27
  29.7 0.0 collective-permute-done.3
  29.7 0.0 collective-permute-done.2
  29.8 7.2 %collective-permute-start.7 = (bf16[4,2,64,256]{3,2,1,0:T(8,128)(2,1)S(1)}, bf16[4,2,64,256]{3,2,1,0:T(8,128)(2,1)S(1)}, u32[]{:S(2)}, u32[]{:S(2)}) collective-permute-start(bf16[4,2,64,256]{3,2,1,0:T(8,128)(2,1)S(1)} %pad_maximum_fusion.pieces0), channel_id=1, source_target_pairs={{0,192},{64,128},{128,64},{192,0},{1,193},{65,129},{129,65},{193,1... | collective-permute-start | bytes 786440 | tf_op jit(solution)/shard_map/ppermute | solution.py:27
  37.0 0.6 collective-permute-start.6
  37.6 0.3 collective-permute-start.5
  37.9 0.1 stack.38.where
  38.0 10.6 %collective-permute-done.7.pieces3 = bf16[4,2,64,256]{3,2,1,0:T(8,128)(2,1)S(1)} collective-permute-done((bf16[4,2,64,256]{3,2,1,0:T(8,128)(2,1)S(1)}, bf16[4,2,64,256]{3,2,1,0:T(8,128)(2,1)S(1)}, u32[]{:S(2)}, u32[]{:S(2)}) %collective-permute-start.7) | collective-permute-done | bytes 262176 | tf_op jit(solution)/shard_map/ppermute | solution.py:27
  48.6 0.0 collective-permute-done.6.pieces2
  48.6 0.7 collective-permute-done.5.pieces1
  49.3 0.7 place.1.mine
  50.1 0.1 collective-permute-start.8
  50.2 2.6 %collective-permute-done.8.theirs = bf16[1024,512]{1,0:T(8,128)(2,1)S(1)} collective-permute-done((bf16[1024,512]{1,0:T(8,128)(2,1)S(1)}, bf16[1024,512]{1,0:T(8,128)(2,1)S(1)}, u32[]{:S(2)}, u32[]{:S(2)}) %collective-permute-start.8) | collective-permute-done | bytes 1048608 | tf_op jit(solution)/shard_map/ppermute | solution.py:209
  52.8 1.9 %join.1.density_in = bf16[8192,1024]{1,0:T(8,128)(2,1)} custom-call(s32[5]{0:T(128)S(1)} %stack.38.where, bf16[1024,512]{1,0:T(8,128)(2,1)S(1)} %place.1.mine, bf16[1024,512]{1,0:T(8,128)(2,1)S(1)} %collective-permute-done.8.theirs), custom_call_target="tpu_custom_call" | custom-call | bytes 4194304 | tf_op jit(solution)/shard_map/join/pallas_call | solution.py:200
  54.8 13.5 %all-to-all-done = bf16[64,64,256]{2,1,0:T(8,128)(2,1)S(1)} async-done(((bf16[64,64,256]{2,1,0:T(8,128)(2,1)}), bf16[64,64,256]{2,1,0:T(8,128)(2,1)S(1)}, u32[]{:S(2)}, u32[]{:S(2)}) %all-to-all-start) | async-done | bytes 2097184 | tf_op jit(solution)/shard_map/all_to_all | solution.py:232
  68.3 3.8 %first.1 = (bf16[256,1024]{1,0:T(8,128)(2,1)S(1)}, bf16[256,1024]{1,0:T(8,128)(2,1)S(1)}, bf16[4,4,64,1024]{3,2,1,0:T(8,128)(2,1)S(1)}, bf16[1024,1024]{1,0:T(8,128)(2,1)S(1)}, bf16[512,1024]{1,0:T(8,128)(2,1)S(1)}) custom-call(s32[5]{0:T(128)S(1)} %stack.38.where, bf16[4,2,4,2,64,256]{5,4,3,2,1,0:T(8,128)(2,1)S(1)} %bitcast.12, ...), custom_call_target="tpu_custom_call" | custom-call | flops 2147483648 | bytes 8388608 | tf_op jit(solution)/shard_map/first/pallas_call | solution.py:235
  72.1 0.1 collective-permute-start.9
  72.2 1.8 %own.1 = (bf16[512,1024]{1,0:T(8,128)(2,1)S(1)}, f32[256,1024]{1,0:T(8,128)S(1)}) custom-call(bf16[512,1024]{1,0:T(8,128)(2,1)S(1)} %get-tuple-element.24.rows, bf16[1024,1024]{1,0:T(8,128)(2,1)S(1)} %get-tuple-element.25.density, bf16[256,1024]{1,0:T(8,128)(2,1)S(1)} %get-tuple-element.26.later, bf16[4,4,64,1024]{3,2,1,0:T(8,128)(2,1)S(1)} %get-tuple-element.27.screened), custom_call_target="tpu_custom_call" | custom-call | flops 1610612736 | bytes 8388608 | tf_op jit(solution)/shard_map/own/pallas_call | solution.py:246
  74.0 0.1 collective-permute-done.9.arrived
  74.1 0.7 near.1
  74.8 0.5 collective-permute-start.10
  75.3 5.7 %collective-permute-start.11 = (bf16[128,1024]{1,0:T(8,128)(2,1)S(1)}, bf16[128,1024]{1,0:T(8,128)(2,1)S(1)}, u32[]{:S(2)}, u32[]{:S(2)}) collective-permute-start(bf16[128,1024]{1,0:T(8,128)(2,1)S(1)} %get-tuple-element.36), channel_id=1, source_target_pairs={{0,64},{64,0},{128,192},{192,128},{1,65},{65,1},{129,193},{193,129... | collective-permute-start | bytes 786440 | tf_op jit(solution)/shard_map/ppermute | solution.py:279
  81.0 1.4 %collective-permute-start.12 = (bf16[128,1024]{1,0:T(8,128)(2,1)S(1)}, bf16[128,1024]{1,0:T(8,128)(2,1)S(1)}, u32[]{:S(2)}, u32[]{:S(2)}) collective-permute-start(bf16[128,1024]{1,0:T(8,128)(2,1)S(1)} %get-tuple-element.37), channel_id=1, source_target_pairs={{0,192},{64,128},{128,64},{192,0},{1,193},{65,129},{129,65},{193,1... | collective-permute-start | bytes 786440 | tf_op jit(solution)/shard_map/ppermute | solution.py:279
  82.4 0.0 collective-permute-done.10.arrived
  82.4 0.7 far.1
  83.1 1.6 %collective-permute-start.13 = (bf16[128,1024]{1,0:T(8,128)(2,1)S(1)}, bf16[128,1024]{1,0:T(8,128)(2,1)S(1)}, u32[]{:S(2)}, u32[]{:S(2)}) collective-permute-start(bf16[128,1024]{1,0:T(8,128)(2,1)S(1)} %get-tuple-element.38), channel_id=1, source_target_pairs={{0,128},{64,192},{128,0},{192,64},{1,129},{65,193},{129,1},{193,65... | collective-permute-start | bytes 786440 | tf_op jit(solution)/shard_map/ppermute | solution.py:279
  84.7 3.0 %collective-permute-done.11.second = bf16[128,1024]{1,0:T(8,128)(2,1)S(1)} collective-permute-done((bf16[128,1024]{1,0:T(8,128)(2,1)S(1)}, bf16[128,1024]{1,0:T(8,128)(2,1)S(1)}, u32[]{:S(2)}, u32[]{:S(2)}) %collective-permute-start.11) | collective-permute-done | bytes 262176 | tf_op jit(solution)/shard_map/ppermute | solution.py:279
  87.7 6.3 %collective-permute-done.12.third = bf16[128,1024]{1,0:T(8,128)(2,1)S(1)} collective-permute-done((bf16[128,1024]{1,0:T(8,128)(2,1)S(1)}, bf16[128,1024]{1,0:T(8,128)(2,1)S(1)}, u32[]{:S(2)}, u32[]{:S(2)}) %collective-permute-start.12) | collective-permute-done | bytes 262176 | tf_op jit(solution)/shard_map/ppermute | solution.py:279
  93.9 0.1 add.6
  94.0 1.8 %collective-permute-done.13 = bf16[128,1024]{1,0:T(8,128)(2,1)S(1)} collective-permute-done((bf16[128,1024]{1,0:T(8,128)(2,1)S(1)}, bf16[128,1024]{1,0:T(8,128)(2,1)S(1)}, u32[]{:S(2)}, u32[]{:S(2)}) %collective-permute-start.13) | collective-permute-done | bytes 262176 | tf_op jit(solution)/shard_map/ppermute | solution.py:279
  95.8 0.1 add_convert_fusion
  95.9 0.1 reshape.7
  96.0 17.4 %all_to_all.10 = bf16[32,4,1024]{2,1,0:T(4,128)(2,1)S(1)} all-to-all(bf16[32,4,1024]{2,1,0:T(4,128)(2,1)S(1)} %reshape.7), channel_id=1, replica_groups=mesh['y'=4,'zl'=2,'c'=2,'x'=4,'zh'=4] {'zl','x','zh'}, dimensions={0} | all-to-all | bytes 524288 | tf_op jit(solution)/shard_map/all_to_all | solution.py:292
  113.4 0.7 convert_reduce_fusion
  (2 shorter events, 0.0 us)
Async XLA Ops:
  3.1 15.0 %collective-permute-start.1 = (bf16[64,256]{1,0:T(8,128)(2,1)}, bf16[64,256]{1,0:T(8,128)(2,1)S(1)}, u32[]{:S(2)}, u32[]{:S(2)}) collective-permute-start(bf16[64,256]{1,0:T(8,128)(2,1)} %get-tuple-element.23), channel_id=1, source_target_pairs={{0,1},{1,0},{2,3},{3,2},{32,33},{33,32},{34,35},{35,34},{64,67},{6... | collective-permute-start | bytes 98312 | tf_op jit(solution)/shard_map/ppermute | solution.py:171
  6.5 11.7 %collective-permute-start = (bf16[64,256]{1,0:T(8,128)(2,1)}, bf16[64,256]{1,0:T(8,128)(2,1)S(1)}, u32[]{:S(2)}, u32[]{:S(2)}) collective-permute-start(bf16[64,256]{1,0:T(8,128)(2,1)} %get-tuple-element.23), channel_id=1, source_target_pairs={{0,0},{1,1},{2,2},{3,3},{32,32},{33,33},{34,34},{35,35},{64,66},{6... | collective-permute-start | bytes 98312 | tf_op jit(solution)/shard_map/ppermute | solution.py:171
  7.9 60.4 %all-to-all-start = ((bf16[64,64,256]{2,1,0:T(8,128)(2,1)}), bf16[64,64,256]{2,1,0:T(8,128)(2,1)S(1)}, u32[]{:S(2)}, u32[]{:S(2)}) async-start(bf16[64,64,256]{2,1,0:T(8,128)(2,1)} %get-tuple-element.22), calls=%async_computation | async-start | bytes 4194304 | tf_op jit(solution)/shard_map/all_to_all | solution.py:232
  18.1 11.6 %collective-permute-start.4 = (bf16[2,64,256]{2,1,0:T(8,128)(2,1)S(1)}, bf16[2,64,256]{2,1,0:T(8,128)(2,1)S(1)}, u32[]{:S(2)}, u32[]{:S(2)}) collective-permute-start(bf16[2,64,256]{2,1,0:T(8,128)(2,1)S(1)} %pair.1), channel_id=1, source_target_pairs={{0,12},{4,8},{8,4},{12,0},{1,13},{5,9},{9,5},{13,1},{2,14},{6,10},... | collective-permute-start | bytes 196616 | tf_op jit(solution)/shard_map/ppermute | solution.py:27
  19.8 10.0 %collective-permute-start.3 = (bf16[2,64,256]{2,1,0:T(8,128)(2,1)S(1)}, bf16[2,64,256]{2,1,0:T(8,128)(2,1)S(1)}, u32[]{:S(2)}, u32[]{:S(2)}) collective-permute-start(bf16[2,64,256]{2,1,0:T(8,128)(2,1)S(1)} %pair.1), channel_id=1, source_target_pairs={{0,8},{4,12},{8,0},{12,4},{1,9},{5,13},{9,1},{13,5},{2,10},{6,14},... | collective-permute-start | bytes 196616 | tf_op jit(solution)/shard_map/ppermute | solution.py:27
  20.7 9.0 %collective-permute-start.2 = (bf16[2,64,256]{2,1,0:T(8,128)(2,1)S(1)}, bf16[2,64,256]{2,1,0:T(8,128)(2,1)S(1)}, u32[]{:S(2)}, u32[]{:S(2)}) collective-permute-start(bf16[2,64,256]{2,1,0:T(8,128)(2,1)S(1)} %pair.1), channel_id=1, source_target_pairs={{0,4},{4,0},{8,12},{12,8},{1,5},{5,1},{9,13},{13,9},{2,6},{6,2},{1... | collective-permute-start | bytes 196616 | tf_op jit(solution)/shard_map/ppermute | solution.py:27
  29.8 18.9 %collective-permute-start.7 = (bf16[4,2,64,256]{3,2,1,0:T(8,128)(2,1)S(1)}, bf16[4,2,64,256]{3,2,1,0:T(8,128)(2,1)S(1)}, u32[]{:S(2)}, u32[]{:S(2)}) collective-permute-start(bf16[4,2,64,256]{3,2,1,0:T(8,128)(2,1)S(1)} %pad_maximum_fusion.pieces0), channel_id=1, source_target_pairs={{0,192},{64,128},{128,64},{192,0},{1,193},{65,129},{129,65},{193,1... | collective-permute-start | bytes 786440 | tf_op jit(solution)/shard_map/ppermute | solution.py:27
  37.0 11.7 %collective-permute-start.6 = (bf16[4,2,64,256]{3,2,1,0:T(8,128)(2,1)S(1)}, bf16[4,2,64,256]{3,2,1,0:T(8,128)(2,1)S(1)}, u32[]{:S(2)}, u32[]{:S(2)}) collective-permute-start(bf16[4,2,64,256]{3,2,1,0:T(8,128)(2,1)S(1)} %pad_maximum_fusion.pieces0), channel_id=1, source_target_pairs={{0,128},{64,192},{128,0},{192,64},{1,129},{65,193},{129,1},{193,65... | collective-permute-start | bytes 786440 | tf_op jit(solution)/shard_map/ppermute | solution.py:27
  37.6 11.8 %collective-permute-start.5 = (bf16[4,2,64,256]{3,2,1,0:T(8,128)(2,1)S(1)}, bf16[4,2,64,256]{3,2,1,0:T(8,128)(2,1)S(1)}, u32[]{:S(2)}, u32[]{:S(2)}) collective-permute-start(bf16[4,2,64,256]{3,2,1,0:T(8,128)(2,1)S(1)} %pad_maximum_fusion.pieces0), channel_id=1, source_target_pairs={{0,64},{64,0},{128,192},{192,128},{1,65},{65,1},{129,193},{193,129... | collective-permute-start | bytes 786440 | tf_op jit(solution)/shard_map/ppermute | solution.py:27
  50.1 2.7 %collective-permute-start.8 = (bf16[1024,512]{1,0:T(8,128)(2,1)S(1)}, bf16[1024,512]{1,0:T(8,128)(2,1)S(1)}, u32[]{:S(2)}, u32[]{:S(2)}) collective-permute-start(bf16[1024,512]{1,0:T(8,128)(2,1)S(1)} %place.1.mine), channel_id=1, source_target_pairs={{0,16},{16,0},{1,17},{17,1},{2,18},{18,2},{3,19},{19,3},{4,20},{20... | collective-permute-start | bytes 3145736 | tf_op jit(solution)/shard_map/ppermute | solution.py:209
  72.1 2.0 %collective-permute-start.9 = (bf16[256,1024]{1,0:T(8,128)(2,1)S(1)}, bf16[256,1024]{1,0:T(8,128)(2,1)S(1)}, u32[]{:S(2)}, u32[]{:S(2)}) collective-permute-start(bf16[256,1024]{1,0:T(8,128)(2,1)S(1)} %get-tuple-element.30), channel_id=1, source_target_pairs={{0,16},{16,0},{1,17},{17,1},{2,18},{18,2},{3,19},{19,3},{4,20},{20... | collective-permute-start | bytes 1572872 | tf_op jit(solution)/shard_map/ppermute | solution.py:245
  74.8 7.6 %collective-permute-start.10 = (f32[256,1024]{1,0:T(8,128)S(1)}, f32[256,1024]{1,0:T(8,128)S(1)}, u32[]{:S(2)}, u32[]{:S(2)}) collective-permute-start(f32[256,1024]{1,0:T(8,128)S(1)} %get-tuple-element.34), channel_id=1, source_target_pairs={{0,16},{16,0},{1,17},{17,1},{2,18},{18,2},{3,19},{19,3},{4,20},{20... | collective-permute-start | bytes 3145736 | tf_op jit(solution)/shard_map/ppermute | solution.py:277
  75.3 12.4 %collective-permute-start.11 = (bf16[128,1024]{1,0:T(8,128)(2,1)S(1)}, bf16[128,1024]{1,0:T(8,128)(2,1)S(1)}, u32[]{:S(2)}, u32[]{:S(2)}) collective-permute-start(bf16[128,1024]{1,0:T(8,128)(2,1)S(1)} %get-tuple-element.36), channel_id=1, source_target_pairs={{0,64},{64,0},{128,192},{192,128},{1,65},{65,1},{129,193},{193,129... | collective-permute-start | bytes 786440 | tf_op jit(solution)/shard_map/ppermute | solution.py:279
  81.0 13.0 %collective-permute-start.12 = (bf16[128,1024]{1,0:T(8,128)(2,1)S(1)}, bf16[128,1024]{1,0:T(8,128)(2,1)S(1)}, u32[]{:S(2)}, u32[]{:S(2)}) collective-permute-start(bf16[128,1024]{1,0:T(8,128)(2,1)S(1)} %get-tuple-element.37), channel_id=1, source_target_pairs={{0,192},{64,128},{128,64},{192,0},{1,193},{65,129},{129,65},{193,1... | collective-permute-start | bytes 786440 | tf_op jit(solution)/shard_map/ppermute | solution.py:279
  83.1 12.7 %collective-permute-start.13 = (bf16[128,1024]{1,0:T(8,128)(2,1)S(1)}, bf16[128,1024]{1,0:T(8,128)(2,1)S(1)}, u32[]{:S(2)}, u32[]{:S(2)}) collective-permute-start(bf16[128,1024]{1,0:T(8,128)(2,1)S(1)} %get-tuple-element.38), channel_id=1, source_target_pairs={{0,128},{64,192},{128,0},{192,64},{1,129},{65,193},{129,1},{193,65... | collective-permute-start | bytes 786440 | tf_op jit(solution)/shard_map/ppermute | solution.py:279

commit v9 on v8

--- a/solution.py
+++ b/solution.py
@@ -10,7 +10,7 @@
 PLANE = ("x", "c", "zh", "zl")
 NT = (((1,), (1,)), ((), ()))
 SWAP = [(0, 1), (1, 0)]
-STEPS = (1, 3, 2, 0)
+STEPS = (2, 3, 1, 0)
 VMEM = pl.BlockSpec(memory_space=pltpu.VMEM)
 HBM = pl.BlockSpec(memory_space=pltpu.HBM)
 SMEM = pl.BlockSpec(memory_space=pltpu.SMEM)

time: 114 us -> 115 us (level); the launches traced: 114 us -> 114 us
  no operation moved by 1% of the time
where the time goes in v9:
time: 115 us; the launch traced here: 114 us
  waiting for transfers between devices  45.7 us (40%)
  starting transfers between devices  36.4 us (32%)
  blocking collectives  17.6 us (15%)
  Pallas kernels  12.9 us (11%)
    ppermute x6, waiting for transfers between devices, from_four(): lax.ppermute(one, axis, [(i, i ^ j) for i in range(4)])  18.8 us
    all_to_all x1, blocking collectives, body(): lax.all_to_all(term, ('zl', 'x', 'zh'), split_axis=0, concat_axis=0, tile...  17.6 us
    all_to_all x1, waiting for transfers between devices, body(): lax.all_to_all(screened, PLANE, split_axis=0, concat_axis=0, tiled=True)  13.5 us
    ppermute x6, starting transfers between devices, from_four(): lax.ppermute(one, axis, [(i, i ^ j) for i in range(4)])  12.3 us
    ppermute x3, waiting for transfers between devices, body(): lax.ppermute(quarter, 'y', [(i, i ^ step) for i in range(4)])  10.6 us
    all_to_all x1, starting transfers between devices, body(): lax.all_to_all(screened, PLANE, split_axis=0, concat_axis=0, tiled=True)  10.2 us
    ppermute x3, starting transfers between devices, body(): lax.ppermute(quarter, 'y', [(i, i ^ step) for i in range(4)])  8.43 us
    ppermute x2, starting transfers between devices, gather_z(): lax.ppermute(block, ('y', 'zl', 'zh'), [(y * 8 + z, y * 8 + (z ^ y * 2 +...  4.76 us
  transfers between devices with their start and end apart: 15, of which 9 were waited for; matrix products, arithmetic and copies ran while one was open for 0% of the time, Pallas kernels for 5%

profile of v9, /device:TPU:2, one launch (start us, length us, event | category | flops | bytes accessed | tf_op | source)
XLA Modules:
  0.0 113.7 jit_solution(16890876140730754046)
XLA Ops:
  0.0 3.1 %prepare.1 = (bf16[64,256]{1,0:T(8,128)(2,1)}, bf16[64,64,256]{2,1,0:T(8,128)(2,1)}) custom-call(s32[1,4]{1,0:T(1,128)} %bitcast.18, bf16[64,256]{1,0:T(8,128)(2,1)} %bitcast.17, s32[1,1,4]{2,1,0:T(1,128)} %mask.1, bf16[64,64,256]{2,1,0:T(8,128)(2,1)} %integrals.1), custom_call_target="tpu_custom_call" | custom-call | bytes 4194304 | tf_op jit(solution)/shard_map/prepare/pallas_call | solution.py:214
  3.1 3.4 %collective-permute-start.1 = (bf16[64,256]{1,0:T(8,128)(2,1)}, bf16[64,256]{1,0:T(8,128)(2,1)S(1)}, u32[]{:S(2)}, u32[]{:S(2)}) collective-permute-start(bf16[64,256]{1,0:T(8,128)(2,1)} %get-tuple-element.23), channel_id=1, source_target_pairs={{0,1},{1,0},{2,3},{3,2},{32,33},{33,32},{34,35},{35,34},{64,67},{6... | collective-permute-start | bytes 98312 | tf_op jit(solution)/shard_map/ppermute | solution.py:171
  6.5 1.4 %collective-permute-start = (bf16[64,256]{1,0:T(8,128)(2,1)}, bf16[64,256]{1,0:T(8,128)(2,1)S(1)}, u32[]{:S(2)}, u32[]{:S(2)}) collective-permute-start(bf16[64,256]{1,0:T(8,128)(2,1)} %get-tuple-element.23), channel_id=1, source_target_pairs={{0,0},{1,1},{2,2},{3,3},{32,32},{33,33},{34,34},{35,35},{64,66},{6... | collective-permute-start | bytes 98312 | tf_op jit(solution)/shard_map/ppermute | solution.py:171
  7.9 10.2 %all-to-all-start = ((bf16[64,64,256]{2,1,0:T(8,128)(2,1)}), bf16[64,64,256]{2,1,0:T(8,128)(2,1)S(1)}, u32[]{:S(2)}, u32[]{:S(2)}) async-start(bf16[64,64,256]{2,1,0:T(8,128)(2,1)} %get-tuple-element.22), calls=%async_computation | async-start | bytes 4194304 | tf_op jit(solution)/shard_map/all_to_all | solution.py:232
  18.1 0.0 collective-permute-done.1.second
  18.1 0.0 collective-permute-done.first
  18.1 1.6 %collective-permute-start.4 = (bf16[2,64,256]{2,1,0:T(8,128)(2,1)S(1)}, bf16[2,64,256]{2,1,0:T(8,128)(2,1)S(1)}, u32[]{:S(2)}, u32[]{:S(2)}) collective-permute-start(bf16[2,64,256]{2,1,0:T(8,128)(2,1)S(1)} %pair.1), channel_id=1, source_target_pairs={{0,12},{4,8},{8,4},{12,0},{1,13},{5,9},{9,5},{13,1},{2,14},{6,10},... | collective-permute-start | bytes 196616 | tf_op jit(solution)/shard_map/ppermute | solution.py:27
  19.8 1.0 collective-permute-start.3
  20.7 1.6 %collective-permute-start.2 = (bf16[2,64,256]{2,1,0:T(8,128)(2,1)S(1)}, bf16[2,64,256]{2,1,0:T(8,128)(2,1)S(1)}, u32[]{:S(2)}, u32[]{:S(2)}) collective-permute-start(bf16[2,64,256]{2,1,0:T(8,128)(2,1)S(1)} %pair.1), channel_id=1, source_target_pairs={{0,4},{4,0},{8,12},{12,8},{1,5},{5,1},{9,13},{13,9},{2,6},{6,2},{1... | collective-permute-start | bytes 196616 | tf_op jit(solution)/shard_map/ppermute | solution.py:27
  22.3 7.4 %collective-permute-done.4 = bf16[2,64,256]{2,1,0:T(8,128)(2,1)S(1)} collective-permute-done((bf16[2,64,256]{2,1,0:T(8,128)(2,1)S(1)}, bf16[2,64,256]{2,1,0:T(8,128)(2,1)S(1)}, u32[]{:S(2)}, u32[]{:S(2)}) %collective-permute-start.4) | collective-permute-done | bytes 65568 | tf_op jit(solution)/shard_map/ppermute | solution.py:27
  29.7 0.0 collective-permute-done.3
  29.7 0.0 collective-permute-done.2
  29.8 7.2 %collective-permute-start.7 = (bf16[4,2,64,256]{3,2,1,0:T(8,128)(2,1)S(1)}, bf16[4,2,64,256]{3,2,1,0:T(8,128)(2,1)S(1)}, u32[]{:S(2)}, u32[]{:S(2)}) collective-permute-start(bf16[4,2,64,256]{3,2,1,0:T(8,128)(2,1)S(1)} %pad_maximum_fusion.pieces0), channel_id=1, source_target_pairs={{0,192},{64,128},{128,64},{192,0},{1,193},{65,129},{129,65},{193,1... | collective-permute-start | bytes 786440 | tf_op jit(solution)/shard_map/ppermute | solution.py:27
  37.0 0.6 collective-permute-start.6
  37.6 0.3 collective-permute-start.5
  37.9 0.1 stack.38.where
  38.0 10.6 %collective-permute-done.7.pieces3 = bf16[4,2,64,256]{3,2,1,0:T(8,128)(2,1)S(1)} collective-permute-done((bf16[4,2,64,256]{3,2,1,0:T(8,128)(2,1)S(1)}, bf16[4,2,64,256]{3,2,1,0:T(8,128)(2,1)S(1)}, u32[]{:S(2)}, u32[]{:S(2)}) %collective-permute-start.7) | collective-permute-done | bytes 262176 | tf_op jit(solution)/shard_map/ppermute | solution.py:27
  48.6 0.0 collective-permute-done.6.pieces2
  48.6 0.7 collective-permute-done.5.pieces1
  49.3 0.7 place.1.mine
  50.1 0.1 collective-permute-start.8
  50.2 2.6 %collective-permute-done.8.theirs = bf16[1024,512]{1,0:T(8,128)(2,1)S(1)} collective-permute-done((bf16[1024,512]{1,0:T(8,128)(2,1)S(1)}, bf16[1024,512]{1,0:T(8,128)(2,1)S(1)}, u32[]{:S(2)}, u32[]{:S(2)}) %collective-permute-start.8) | collective-permute-done | bytes 1048608 | tf_op jit(solution)/shard_map/ppermute | solution.py:209
  52.8 1.9 %join.1.density_in = bf16[8192,1024]{1,0:T(8,128)(2,1)} custom-call(s32[5]{0:T(128)S(1)} %stack.38.where, bf16[1024,512]{1,0:T(8,128)(2,1)S(1)} %place.1.mine, bf16[1024,512]{1,0:T(8,128)(2,1)S(1)} %collective-permute-done.8.theirs), custom_call_target="tpu_custom_call" | custom-call | bytes 4194304 | tf_op jit(solution)/shard_map/join/pallas_call | solution.py:200
  54.8 13.5 %all-to-all-done = bf16[64,64,256]{2,1,0:T(8,128)(2,1)S(1)} async-done(((bf16[64,64,256]{2,1,0:T(8,128)(2,1)}), bf16[64,64,256]{2,1,0:T(8,128)(2,1)S(1)}, u32[]{:S(2)}, u32[]{:S(2)}) %all-to-all-start) | async-done | bytes 2097184 | tf_op jit(solution)/shard_map/all_to_all | solution.py:232
  68.3 3.8 %first.1 = (bf16[256,1024]{1,0:T(8,128)(2,1)S(1)}, bf16[256,1024]{1,0:T(8,128)(2,1)S(1)}, bf16[4,4,64,1024]{3,2,1,0:T(8,128)(2,1)S(1)}, bf16[1024,1024]{1,0:T(8,128)(2,1)S(1)}, bf16[512,1024]{1,0:T(8,128)(2,1)S(1)}) custom-call(s32[5]{0:T(128)S(1)} %stack.38.where, bf16[4,2,4,2,64,256]{5,4,3,2,1,0:T(8,128)(2,1)S(1)} %bitcast.12, ...), custom_call_target="tpu_custom_call" | custom-call | flops 2147483648 | bytes 8388608 | tf_op jit(solution)/shard_map/first/pallas_call | solution.py:235
  72.1 0.1 collective-permute-start.9
  72.2 1.8 %own.1 = (bf16[512,1024]{1,0:T(8,128)(2,1)S(1)}, f32[256,1024]{1,0:T(8,128)S(1)}) custom-call(bf16[512,1024]{1,0:T(8,128)(2,1)S(1)} %get-tuple-element.24.rows, bf16[1024,1024]{1,0:T(8,128)(2,1)S(1)} %get-tuple-element.25.density, bf16[256,1024]{1,0:T(8,128)(2,1)S(1)} %get-tuple-element.26.later, bf16[4,4,64,1024]{3,2,1,0:T(8,128)(2,1)S(1)} %get-tuple-element.27.screened), custom_call_target="tpu_custom_call" | custom-call | flops 1610612736 | bytes 8388608 | tf_op jit(solution)/shard_map/own/pallas_call | solution.py:246
  74.0 0.1 collective-permute-done.9.arrived
  74.1 0.7 near.1
  74.8 0.5 collective-permute-start.10
  75.3 4.7 %collective-permute-start.11 = (bf16[128,1024]{1,0:T(8,128)(2,1)S(1)}, bf16[128,1024]{1,0:T(8,128)(2,1)S(1)}, u32[]{:S(2)}, u32[]{:S(2)}) collective-permute-start(bf16[128,1024]{1,0:T(8,128)(2,1)S(1)} %get-tuple-element.36), channel_id=1, source_target_pairs={{0,128},{64,192},{128,0},{192,64},{1,129},{65,193},{129,1},{193,65... | collective-permute-start | bytes 786440 | tf_op jit(solution)/shard_map/ppermute | solution.py:279
  80.0 3.6 %collective-permute-start.12 = (bf16[128,1024]{1,0:T(8,128)(2,1)S(1)}, bf16[128,1024]{1,0:T(8,128)(2,1)S(1)}, u32[]{:S(2)}, u32[]{:S(2)}) collective-permute-start(bf16[128,1024]{1,0:T(8,128)(2,1)S(1)} %get-tuple-element.37), channel_id=1, source_target_pairs={{0,192},{64,128},{128,64},{192,0},{1,193},{65,129},{129,65},{193,1... | collective-permute-start | bytes 786440 | tf_op jit(solution)/shard_map/ppermute | solution.py:279
  83.6 0.0 collective-permute-done.10.arrived
  83.6 0.7 far.1
  84.4 0.1 collective-permute-start.13
  84.5 2.3 %collective-permute-done.11.second = bf16[128,1024]{1,0:T(8,128)(2,1)S(1)} collective-permute-done((bf16[128,1024]{1,0:T(8,128)(2,1)S(1)}, bf16[128,1024]{1,0:T(8,128)(2,1)S(1)}, u32[]{:S(2)}, u32[]{:S(2)}) %collective-permute-start.11) | collective-permute-done | bytes 262176 | tf_op jit(solution)/shard_map/ppermute | solution.py:279
  86.7 7.4 %collective-permute-done.12.third = bf16[128,1024]{1,0:T(8,128)(2,1)S(1)} collective-permute-done((bf16[128,1024]{1,0:T(8,128)(2,1)S(1)}, bf16[128,1024]{1,0:T(8,128)(2,1)S(1)}, u32[]{:S(2)}, u32[]{:S(2)}) %collective-permute-start.12) | collective-permute-done | bytes 262176 | tf_op jit(solution)/shard_map/ppermute | solution.py:279
  94.1 0.1 add.6
  94.2 1.0 collective-permute-done.13
  95.2 0.1 add_convert_fusion
  95.3 0.1 reshape.7
  95.4 17.6 %all_to_all.10 = bf16[32,4,1024]{2,1,0:T(4,128)(2,1)S(1)} all-to-all(bf16[32,4,1024]{2,1,0:T(4,128)(2,1)S(1)} %reshape.7), channel_id=1, replica_groups=mesh['y'=4,'zl'=2,'c'=2,'x'=4,'zh'=4] {'zl','x','zh'}, dimensions={0} | all-to-all | bytes 524288 | tf_op jit(solution)/shard_map/all_to_all | solution.py:292
  113.0 0.7 convert_reduce_fusion
  (2 shorter events, 0.0 us)
Async XLA Ops:
  3.1 15.0 %collective-permute-start.1 = (bf16[64,256]{1,0:T(8,128)(2,1)}, bf16[64,256]{1,0:T(8,128)(2,1)S(1)}, u32[]{:S(2)}, u32[]{:S(2)}) collective-permute-start(bf16[64,256]{1,0:T(8,128)(2,1)} %get-tuple-element.23), channel_id=1, source_target_pairs={{0,1},{1,0},{2,3},{3,2},{32,33},{33,32},{34,35},{35,34},{64,67},{6... | collective-permute-start | bytes 98312 | tf_op jit(solution)/shard_map/ppermute | solution.py:171
  6.5 11.7 %collective-permute-start = (bf16[64,256]{1,0:T(8,128)(2,1)}, bf16[64,256]{1,0:T(8,128)(2,1)S(1)}, u32[]{:S(2)}, u32[]{:S(2)}) collective-permute-start(bf16[64,256]{1,0:T(8,128)(2,1)} %get-tuple-element.23), channel_id=1, source_target_pairs={{0,0},{1,1},{2,2},{3,3},{32,32},{33,33},{34,34},{35,35},{64,66},{6... | collective-permute-start | bytes 98312 | tf_op jit(solution)/shard_map/ppermute | solution.py:171
  7.9 60.4 %all-to-all-start = ((bf16[64,64,256]{2,1,0:T(8,128)(2,1)}), bf16[64,64,256]{2,1,0:T(8,128)(2,1)S(1)}, u32[]{:S(2)}, u32[]{:S(2)}) async-start(bf16[64,64,256]{2,1,0:T(8,128)(2,1)} %get-tuple-element.22), calls=%async_computation | async-start | bytes 4194304 | tf_op jit(solution)/shard_map/all_to_all | solution.py:232
  18.1 11.6 %collective-permute-start.4 = (bf16[2,64,256]{2,1,0:T(8,128)(2,1)S(1)}, bf16[2,64,256]{2,1,0:T(8,128)(2,1)S(1)}, u32[]{:S(2)}, u32[]{:S(2)}) collective-permute-start(bf16[2,64,256]{2,1,0:T(8,128)(2,1)S(1)} %pair.1), channel_id=1, source_target_pairs={{0,12},{4,8},{8,4},{12,0},{1,13},{5,9},{9,5},{13,1},{2,14},{6,10},... | collective-permute-start | bytes 196616 | tf_op jit(solution)/shard_map/ppermute | solution.py:27
  19.8 10.0 %collective-permute-start.3 = (bf16[2,64,256]{2,1,0:T(8,128)(2,1)S(1)}, bf16[2,64,256]{2,1,0:T(8,128)(2,1)S(1)}, u32[]{:S(2)}, u32[]{:S(2)}) collective-permute-start(bf16[2,64,256]{2,1,0:T(8,128)(2,1)S(1)} %pair.1), channel_id=1, source_target_pairs={{0,8},{4,12},{8,0},{12,4},{1,9},{5,13},{9,1},{13,5},{2,10},{6,14},... | collective-permute-start | bytes 196616 | tf_op jit(solution)/shard_map/ppermute | solution.py:27
  20.7 9.0 %collective-permute-start.2 = (bf16[2,64,256]{2,1,0:T(8,128)(2,1)S(1)}, bf16[2,64,256]{2,1,0:T(8,128)(2,1)S(1)}, u32[]{:S(2)}, u32[]{:S(2)}) collective-permute-start(bf16[2,64,256]{2,1,0:T(8,128)(2,1)S(1)} %pair.1), channel_id=1, source_target_pairs={{0,4},{4,0},{8,12},{12,8},{1,5},{5,1},{9,13},{13,9},{2,6},{6,2},{1... | collective-permute-start | bytes 196616 | tf_op jit(solution)/shard_map/ppermute | solution.py:27
  29.8 18.9 %collective-permute-start.7 = (bf16[4,2,64,256]{3,2,1,0:T(8,128)(2,1)S(1)}, bf16[4,2,64,256]{3,2,1,0:T(8,128)(2,1)S(1)}, u32[]{:S(2)}, u32[]{:S(2)}) collective-permute-start(bf16[4,2,64,256]{3,2,1,0:T(8,128)(2,1)S(1)} %pad_maximum_fusion.pieces0), channel_id=1, source_target_pairs={{0,192},{64,128},{128,64},{192,0},{1,193},{65,129},{129,65},{193,1... | collective-permute-start | bytes 786440 | tf_op jit(solution)/shard_map/ppermute | solution.py:27
  37.0 11.7 %collective-permute-start.6 = (bf16[4,2,64,256]{3,2,1,0:T(8,128)(2,1)S(1)}, bf16[4,2,64,256]{3,2,1,0:T(8,128)(2,1)S(1)}, u32[]{:S(2)}, u32[]{:S(2)}) collective-permute-start(bf16[4,2,64,256]{3,2,1,0:T(8,128)(2,1)S(1)} %pad_maximum_fusion.pieces0), channel_id=1, source_target_pairs={{0,128},{64,192},{128,0},{192,64},{1,129},{65,193},{129,1},{193,65... | collective-permute-start | bytes 786440 | tf_op jit(solution)/shard_map/ppermute | solution.py:27
  37.6 11.8 %collective-permute-start.5 = (bf16[4,2,64,256]{3,2,1,0:T(8,128)(2,1)S(1)}, bf16[4,2,64,256]{3,2,1,0:T(8,128)(2,1)S(1)}, u32[]{:S(2)}, u32[]{:S(2)}) collective-permute-start(bf16[4,2,64,256]{3,2,1,0:T(8,128)(2,1)S(1)} %pad_maximum_fusion.pieces0), channel_id=1, source_target_pairs={{0,64},{64,0},{128,192},{192,128},{1,65},{65,1},{129,193},{193,129... | collective-permute-start | bytes 786440 | tf_op jit(solution)/shard_map/ppermute | solution.py:27
  50.1 2.7 %collective-permute-start.8 = (bf16[1024,512]{1,0:T(8,128)(2,1)S(1)}, bf16[1024,512]{1,0:T(8,128)(2,1)S(1)}, u32[]{:S(2)}, u32[]{:S(2)}) collective-permute-start(bf16[1024,512]{1,0:T(8,128)(2,1)S(1)} %place.1.mine), channel_id=1, source_target_pairs={{0,16},{16,0},{1,17},{17,1},{2,18},{18,2},{3,19},{19,3},{4,20},{20... | collective-permute-start | bytes 3145736 | tf_op jit(solution)/shard_map/ppermute | solution.py:209
  72.1 2.0 %collective-permute-start.9 = (bf16[256,1024]{1,0:T(8,128)(2,1)S(1)}, bf16[256,1024]{1,0:T(8,128)(2,1)S(1)}, u32[]{:S(2)}, u32[]{:S(2)}) collective-permute-start(bf16[256,1024]{1,0:T(8,128)(2,1)S(1)} %get-tuple-element.30), channel_id=1, source_target_pairs={{0,16},{16,0},{1,17},{17,1},{2,18},{18,2},{3,19},{19,3},{4,20},{20... | collective-permute-start | bytes 1572872 | tf_op jit(solution)/shard_map/ppermute | solution.py:245
  74.8 8.8 %collective-permute-start.10 = (f32[256,1024]{1,0:T(8,128)S(1)}, f32[256,1024]{1,0:T(8,128)S(1)}, u32[]{:S(2)}, u32[]{:S(2)}) collective-permute-start(f32[256,1024]{1,0:T(8,128)S(1)} %get-tuple-element.34), channel_id=1, source_target_pairs={{0,16},{16,0},{1,17},{17,1},{2,18},{18,2},{3,19},{19,3},{4,20},{20... | collective-permute-start | bytes 3145736 | tf_op jit(solution)/shard_map/ppermute | solution.py:277
  75.3 11.4 %collective-permute-start.11 = (bf16[128,1024]{1,0:T(8,128)(2,1)S(1)}, bf16[128,1024]{1,0:T(8,128)(2,1)S(1)}, u32[]{:S(2)}, u32[]{:S(2)}) collective-permute-start(bf16[128,1024]{1,0:T(8,128)(2,1)S(1)} %get-tuple-element.36), channel_id=1, source_target_pairs={{0,128},{64,192},{128,0},{192,64},{1,129},{65,193},{129,1},{193,65... | collective-permute-start | bytes 786440 | tf_op jit(solution)/shard_map/ppermute | solution.py:279
  80.0 14.1 %collective-permute-start.12 = (bf16[128,1024]{1,0:T(8,128)(2,1)S(1)}, bf16[128,1024]{1,0:T(8,128)(2,1)S(1)}, u32[]{:S(2)}, u32[]{:S(2)}) collective-permute-start(bf16[128,1024]{1,0:T(8,128)(2,1)S(1)} %get-tuple-element.37), channel_id=1, source_target_pairs={{0,192},{64,128},{128,64},{192,0},{1,193},{65,129},{129,65},{193,1... | collective-permute-start | bytes 786440 | tf_op jit(solution)/shard_map/ppermute | solution.py:279
  84.4 10.8 %collective-permute-start.13 = (bf16[128,1024]{1,0:T(8,128)(2,1)S(1)}, bf16[128,1024]{1,0:T(8,128)(2,1)S(1)}, u32[]{:S(2)}, u32[]{:S(2)}) collective-permute-start(bf16[128,1024]{1,0:T(8,128)(2,1)S(1)} %get-tuple-element.38), channel_id=1, source_target_pairs={{0,64},{64,0},{128,192},{192,128},{1,65},{65,1},{129,193},{193,129... | collective-permute-start | bytes 786440 | tf_op jit(solution)/shard_map/ppermute | solution.py:279
